TPU v7x, 128 devices: a whole 4x4x4 slice. The times are simulated.
128 devices in a mesh: rounds: 16 (over z_lo, x, core), stab: 8 (over y, z_hi).
Axes of the slice: x: 4, y: 4, z: 4 (z_hi: 2, z_lo: 2; z = z_hi * 2 + z_lo), core: 2. Of those that a mesh axis runs over, the one named last changes fastest.
Arguments:
- syndrome: int32 [128, 1024], P('rounds', 'stab'), may hold values from 0 to 1
- basis_ids: int32 [1024], P('stab'), may hold values from 0 to 1
- coordinates: int32 [2, 1024], P(None, 'stab'), may hold values from 0 to 41
- syndrome_table: bfloat16 [2, 256], replicated, may hold values from -3 to 3
- basis_table: bfloat16 [2, 256], replicated, may hold values from -3 to 3
- coord_table: bfloat16 [2, 42, 256], replicated, may hold values from -3 to 3
- round_table: bfloat16 [128, 256], P('rounds'), may hold values from -3 to 3
- gain_space: float32 [256], replicated, may hold values from 0.1 to 1.9
- w_qkv_space: bfloat16 [256, 768], replicated, may hold values from -20 to 20
- w_out_space: bfloat16 [256, 256], replicated, may hold values from -0.375 to 0.375
- gain_time: float32 [256], replicated, may hold values from 0.1 to 1.9
- w_qkv_time: bfloat16 [256, 768], replicated, may hold values from -20 to 20
- w_out_time: bfloat16 [256, 256], replicated, may hold values from -0.375 to 0.375
- grad_hidden: bfloat16 [128, 1024, 256], P('rounds', 'stab'), may hold values from -6 to 6
Outputs:
- hidden: bfloat16 [128, 1024, 256], P('rounds', 'stab')
- grad_embedded: bfloat16 [128, 1024, 256], P('rounds', 'stab')
- grad_w_qkv_space: float32 [256, 768], replicated
- grad_w_out_space: float32 [256, 256], replicated
- grad_w_qkv_time: float32 [256, 768], replicated
- grad_w_out_time: float32 [256, 256], replicated
All inputs are finite; a program needn't handle non-finite values.
Results may differ from a plain program's by a relative error of at most 0.029.
The roundings to bfloat16 on the way count: a program that leaves them out, or rounds other values in their place, can miss the bound.
Values may be sent and summed in bfloat16 or wider, within the bound.
No kernel may reach another device: no remote copies, remote signals or barrier semaphores. Data moves between devices by JAX's collectives and lax.ppermute only.
A program may use at most 128 MiB of HBM per device.

v0:
```python
import math

import jax
import jax.numpy as jnp
from jax import lax
from jax.experimental import pallas as pl
from jax.experimental.pallas import tpu as pltpu
from jax.sharding import PartitionSpec as P

HEADS = 4
EPSILON = 1e-06
BOTH = ("stab", "rounds")
LEVELS = 128
VMEM_BYTES = 56 * 2**20
F32 = jnp.float32
BF16 = jnp.bfloat16


def dot(left, right, left_dim, right_dim):
    return lax.dot_general(
        left, right, (((left_dim,), (right_dim,)), ((), ())), preferred_element_type=F32
    )


def kernel_params(cost):
    return dict(
        compiler_params=pltpu.CompilerParams(vmem_limit_bytes=VMEM_BYTES),
        cost_estimate=pl.CostEstimate(flops=cost, bytes_accessed=cost // 400, transcendentals=0),
    )


def whole(shape):
    return pl.BlockSpec(shape, lambda *_: (0,) * len(shape))


def norm_columns(values, gain):
    inverse = lax.rsqrt(jnp.mean(values * values, axis=0, keepdims=True) + EPSILON)
    return (values * inverse * gain).astype(BF16), inverse


def norm_columns_backward(values, gain, inverse, grad_normed):
    gained = grad_normed * gain
    inner = jnp.mean(gained * values, axis=0, keepdims=True)
    return inverse * gained - values * (inverse * inverse * inverse) * inner


def space_forward_kernel(
    index_ref, table_ref, gain_ref, w_qkv_ref, w_out_ref,
    middle_ref, x_ref, normed_ref, inverse_ref, packed_ref, attended_ref, exps_ref, total_ref,
    row_ref, onehot_ref,
):
    head = pl.program_id(0)
    features, tokens = x_ref.shape
    depth = features // HEADS
    scale = depth**-0.5

    @pl.when(head == 0)
    def _():
        width = index_ref.shape[2]
        for block in range(index_ref.shape[0]):
            levels = lax.broadcasted_iota(jnp.int32, (LEVELS, width), 0)
            hit = levels == LEVELS - 1
            for kind in range(index_ref.shape[1]):
                hit = hit | (levels == index_ref[block, kind : kind + 1, :])
            onehot_ref[:, block * width : (block + 1) * width] = hit.astype(F32).astype(BF16)
        onehot = onehot_ref[...]
        table = table_ref[...]
        row_ref[...] = dot(onehot, table, 0, 0).astype(BF16)
        x = dot(table, onehot, 0, 0).astype(BF16)
        x_ref[...] = x
        normed, inverse = norm_columns(x.astype(F32), gain_ref[...])
        normed_ref[...] = normed
        inverse_ref[...] = inverse
        packed_ref[...] = dot(w_qkv_ref[...], normed, 0, 0).astype(BF16)

    at = pl.multiple_of(head * depth, depth)
    query = packed_ref[pl.ds(at, depth), :]
    keys = packed_ref[pl.ds(features + at, depth), :]
    values = packed_ref[pl.ds(2 * features + at, depth), :]
    block = 256
    for start in range(0, tokens, block):
        cols = slice(start, start + block)
        scores = dot(keys, query[:, cols], 0, 0) * scale
        shifted = jnp.exp(scores - jnp.max(scores, axis=0, keepdims=True))
        total = jnp.sum(shifted, axis=0, keepdims=True)
        exps = shifted.astype(BF16)
        exps_ref[0, :, cols] = exps
        inverse_total = 1.0 / total
        total_ref[0, :, cols] = inverse_total
        attended = dot(values, exps, 1, 0) * inverse_total
        attended_ref[pl.ds(at, depth), cols] = attended.astype(BF16)

    @pl.when(head == HEADS - 1)
    def _():
        branch = dot(attended_ref[...], w_out_ref[...], 0, 0)
        middle = (row_ref[...].astype(F32) + branch).astype(BF16)
        middle_ref[...] = middle.reshape(middle_ref.shape)


def space_forward(index, table, gain, w_qkv, w_out, chunks):
    tokens = index.shape[0] * index.shape[2]
    features = table.shape[1]
    shapes = [
        ((chunks, tokens // chunks, features), BF16),
        ((features, tokens), BF16),
        ((features, tokens), BF16),
        ((1, tokens), F32),
        ((3 * features, tokens), BF16),
        ((features, tokens), BF16),
        ((HEADS, tokens, tokens), BF16),
        ((HEADS, 1, tokens), F32),
    ]
    per_head = lambda shape: pl.BlockSpec((1,) + shape[1:], lambda head: (head, 0, 0))
    return pl.pallas_call(
        space_forward_kernel,
        grid=(HEADS,),
        out_shape=[jax.ShapeDtypeStruct(*item) for item in shapes],
        in_specs=[whole(a.shape) for a in (index, table, gain, w_qkv, w_out)],
        out_specs=[whole(shape) for shape, _ in shapes[:6]]
        + [per_head(shape) for shape, _ in shapes[6:]],
        scratch_shapes=[
            pltpu.VMEM((tokens, features), BF16),
            pltpu.VMEM((LEVELS, tokens), BF16),
        ],
        **kernel_params(4_000_000_000),
        name="space_forward",
    )(index, table, gain, w_qkv, w_out)


def time_kernel(
    middle_ref, grad_ref, gain_ref, w_qkv_ref, w_out_ref,
    grad_middle_ref, hidden_ref, normed_ref, grad_packed_ref, attended_ref, grad_row_ref,
    x_ref, inverse_ref, packed_ref, grad_attended_ref, rows_ref, grads_ref,
):
    stab_parts, round_parts, stabs, features = middle_ref.shape
    rounds = stab_parts * round_parts
    tokens = rounds * stabs
    depth = features // HEADS
    scale = depth**-0.5

    middle = jnp.swapaxes(middle_ref[...].astype(F32), 0, 1).reshape(tokens, features)
    grad = grad_ref[...].astype(F32).reshape(tokens, features)
    lanes = rows_ref.shape[2]
    halves = [slice(part * lanes, (part + 1) * lanes) for part in range(features // lanes)]
    for part, half in enumerate(halves):
        rows_ref[part] = middle[:, half]
        grads_ref[part] = grad[:, half]
    for stab in range(stabs):
        cols = slice(stab * rounds, (stab + 1) * rounds)
        at = pl.ds(stab, rounds, stride=stabs)
        for part, half in enumerate(halves):
            x_ref[half, cols] = rows_ref[part, at, :].T
            grad_row_ref[cols, half] = grads_ref[part, at, :].astype(BF16)
    x = x_ref[...]
    normed, inverse = norm_columns(x, gain_ref[...])
    normed_ref[...] = normed
    inverse_ref[...] = inverse
    packed_ref[...] = dot(w_qkv_ref[...], normed, 0, 0).astype(BF16)
    grad_attended_ref[...] = dot(w_out_ref[...], grad_row_ref[...], 1, 1).astype(BF16)

    def one_stab(stab, carry):
        cols = pl.ds(pl.multiple_of(stab * rounds, rounds), rounds)
        for head in range(HEADS):
            at = head * depth
            query = packed_ref[at : at + depth, cols]
            keys = packed_ref[features + at : features + at + depth, cols]
            values = packed_ref[2 * features + at : 2 * features + at + depth, cols]
            grad = grad_attended_ref[at : at + depth, cols]
            scores = dot(keys, query, 0, 0) * scale
            shifted = jnp.exp(scores - jnp.max(scores, axis=0, keepdims=True))
            probabilities = shifted * (1.0 / jnp.sum(shifted, axis=0, keepdims=True))
            weights = probabilities.astype(BF16)
            attended_ref[at : at + depth, cols] = dot(values, weights, 1, 0).astype(BF16)
            grad_weights = dot(values, grad, 0, 0)
            inner = jnp.sum(probabilities * grad_weights, axis=0, keepdims=True)
            grad_scores = (probabilities * (grad_weights - inner) * scale).astype(BF16)
            grad_packed_ref[at : at + depth, cols] = dot(keys, grad_scores, 1, 0).astype(BF16)
            grad_packed_ref[features + at : features + at + depth, cols] = dot(
                query, grad_scores, 1, 1
            ).astype(BF16)
            grad_packed_ref[2 * features + at : 2 * features + at + depth, cols] = dot(
                grad, weights, 1, 1
            ).astype(BF16)
        return carry

    lax.fori_loop(0, stabs, one_stab, 0)

    grad_normed = dot(w_qkv_ref[...], grad_packed_ref[...], 1, 0)
    grad_stream = norm_columns_backward(x_ref[...], gain_ref[...], inverse_ref[...], grad_normed)
    for stab in range(stabs):
        cols = slice(stab * rounds, (stab + 1) * rounds)
        at = pl.ds(stab, rounds, stride=stabs)
        for part, half in enumerate(halves):
            grads_ref[part, at, :] = grads_ref[part, at, :] + grad_stream[half, cols].T
    for part, half in enumerate(halves):
        grad_middle = grads_ref[part].reshape(round_parts, stab_parts, stabs, lanes)
        grad_middle_ref[:, :, :, half] = jnp.swapaxes(grad_middle, 0, 1).astype(BF16)
    branch = dot(attended_ref[...], w_out_ref[...], 0, 0)
    for stab in range(stabs):
        cols = slice(stab * rounds, (stab + 1) * rounds)
        at = pl.ds(stab, rounds, stride=stabs)
        for part, half in enumerate(halves):
            rows_ref[part, at, :] = rows_ref[part, at, :] + branch[cols, half]
    for part, half in enumerate(halves):
        hidden = rows_ref[part].reshape(hidden_ref.shape[:3] + (lanes,))
        hidden_ref[:, :, :, half] = hidden.astype(BF16)


def time_block(middle, grad, gain, w_qkv, w_out):
    stab_parts, round_parts, stabs, features = middle.shape
    tokens = stab_parts * round_parts * stabs
    shapes = [
        (middle.shape, BF16),
        (grad.shape, BF16),
        ((features, tokens), BF16),
        ((3 * features, tokens), BF16),
        ((features, tokens), BF16),
        ((tokens, features), BF16),
    ]
    return pl.pallas_call(
        time_kernel,
        out_shape=[jax.ShapeDtypeStruct(*item) for item in shapes],
        scratch_shapes=[
            pltpu.VMEM((features, tokens), F32),
            pltpu.VMEM((1, tokens), F32),
            pltpu.VMEM((3 * features, tokens), BF16),
            pltpu.VMEM((features, tokens), BF16),
            pltpu.VMEM((features // 128, tokens, 128), F32),
            pltpu.VMEM((features // 128, tokens, 128), F32),
        ],
        **kernel_params(3_000_000_000),
        name="time_block",
    )(middle, grad, gain, w_qkv, w_out)


def space_backward_kernel(
    grad_ref, x_ref, normed_ref, inverse_ref, packed_ref, attended_ref, exps_ref, total_ref,
    gain_ref, w_qkv_ref, w_out_ref,
    grad_stream_ref, grad_w_qkv_ref, grad_w_out_ref,
    grad_attended_ref, grad_packed_ref,
):
    head = pl.program_id(0)
    features, tokens = x_ref.shape
    depth = features // HEADS
    scale = depth**-0.5

    @pl.when(head == 0)
    def _():
        grad = grad_ref[...].reshape(tokens, features)
        grad_attended_ref[...] = dot(w_out_ref[...], grad, 1, 1).astype(BF16)
        grad_w_out_ref[...] = dot(attended_ref[...], grad, 1, 0).astype(grad_w_out_ref.dtype)

    at = pl.multiple_of(head * depth, depth)
    query = packed_ref[pl.ds(at, depth), :]
    keys = packed_ref[pl.ds(features + at, depth), :]
    values = packed_ref[pl.ds(2 * features + at, depth), :]
    grad = grad_attended_ref[pl.ds(at, depth), :].astype(F32) * total_ref[0]
    inner = jnp.sum(
        grad * attended_ref[pl.ds(at, depth), :].astype(F32), axis=0, keepdims=True
    )
    grad = grad.astype(BF16)
    block = 256
    grad_keys = jnp.zeros((depth, tokens), F32)
    grad_values = jnp.zeros((depth, tokens), F32)
    for start in range(0, tokens, block):
        cols = slice(start, start + block)
        exps = exps_ref[0, :, cols]
        grad_weights = dot(values, grad[:, cols], 0, 0)
        grad_scores = (exps.astype(F32) * (grad_weights - inner[:, cols])).astype(BF16)
        grad_query = dot(keys, grad_scores, 1, 0) * scale
        grad_packed_ref[pl.ds(at, depth), cols] = grad_query.astype(BF16)
        grad_keys = grad_keys + dot(query[:, cols], grad_scores, 1, 1)
        grad_values = grad_values + dot(grad[:, cols], exps, 1, 1)
    grad_packed_ref[pl.ds(features + at, depth), :] = (grad_keys * scale).astype(BF16)
    grad_packed_ref[pl.ds(2 * features + at, depth), :] = grad_values.astype(BF16)

    @pl.when(head == HEADS - 1)
    def _():
        grad_packed = grad_packed_ref[...]
        grad_w_qkv_ref[...] = dot(normed_ref[...], grad_packed, 1, 1).astype(grad_w_qkv_ref.dtype)
        grad_normed = dot(w_qkv_ref[...], grad_packed, 1, 0)
        grad_stream = norm_columns_backward(
            x_ref[...].astype(F32), gain_ref[...], inverse_ref[...], grad_normed
        )
        grad_new = grad_ref[...].reshape(tokens, features).astype(F32)
        grad_stream_ref[...] = (grad_new + grad_stream.T).astype(BF16)


def space_backward(grad, saved, gain, w_qkv, w_out):
    x, normed, inverse, packed, attended, exps, totals = saved
    features, tokens = x.shape
    arguments = (grad, x, normed, inverse, packed, attended, exps, totals, gain, w_qkv, w_out)
    per_head = lambda shape: pl.BlockSpec((1,) + shape[1:], lambda head: (head, 0, 0))
    in_specs = [whole(a.shape) for a in arguments]
    in_specs[5 + 1] = per_head(exps.shape)
    in_specs[5 + 2] = per_head(totals.shape)
    shapes = [
        ((tokens, features), BF16),
        ((features, 3 * features), BF16),
        ((features, features), BF16),
    ]
    return pl.pallas_call(
        space_backward_kernel,
        grid=(HEADS,),
        out_shape=[jax.ShapeDtypeStruct(*item) for item in shapes],
        in_specs=in_specs,
        out_specs=[whole(shape) for shape, _ in shapes],
        scratch_shapes=[
            pltpu.VMEM((features, tokens), BF16),
            pltpu.VMEM((3 * features, tokens), BF16),
        ],
        **kernel_params(8_000_000_000),
        name="space_backward",
    )(*arguments)


def weight_grad_kernel(normed_ref, grad_packed_ref, attended_ref, grad_ref, qkv_ref, out_ref):
    qkv_ref[...] = dot(normed_ref[...], grad_packed_ref[...], 1, 1).astype(qkv_ref.dtype)
    out_ref[...] = dot(attended_ref[...], grad_ref[...], 1, 0).astype(out_ref.dtype)


def weight_grads(normed, grad_packed, attended, grad):
    features = normed.shape[0]
    return pl.pallas_call(
        weight_grad_kernel,
        out_shape=[
            jax.ShapeDtypeStruct((features, 3 * features), BF16),
            jax.ShapeDtypeStruct((features, features), BF16),
        ],
        **kernel_params(600_000_000),
        name="weight_grads",
    )(normed, grad_packed, attended, grad)


def exchange(values, axes):
    return lax.all_to_all(values, axes, split_axis=0, concat_axis=0, tiled=True)


def reduce_to_all(flat, parts, scaling):
    pieces = exchange(flat.reshape(parts, flat.shape[0] // parts, flat.shape[1]), BOTH)
    mine = jnp.sum(pieces.astype(F32), axis=0) * scaling
    spread = jnp.broadcast_to(mine.astype(BF16)[None], pieces.shape)
    return exchange(spread, BOTH).reshape(flat.shape).astype(F32)


def on_device(
    syndrome,
    basis_ids,
    coordinates,
    syndrome_table,
    basis_table,
    coord_table,
    round_table,
    gain_space,
    w_qkv_space,
    w_out_space,
    gain_time,
    w_qkv_time,
    w_out_time,
    grad_hidden,
):
    stab_parts = lax.axis_size("stab")
    round_parts = lax.axis_size("rounds")
    parts = stab_parts * round_parts
    rounds_here, stabs_here, features = grad_hidden.shape
    stabs_time = stabs_here // round_parts
    coords = coord_table.shape[1]

    own = jnp.stack([basis_ids + 2 * coords, coordinates[0], coordinates[1] + coords])
    own = jnp.broadcast_to(own[None], (rounds_here,) + own.shape)
    index = exchange(
        jnp.concatenate([syndrome[:, None, :] + 2 * coords + 2, own], axis=1), "stab"
    )
    my_round = lax.dynamic_slice_in_dim(round_table, lax.axis_index("stab"), 1, axis=0)
    used = 2 * coords + 4
    table = jnp.concatenate(
        [
            coord_table.reshape(2 * coords, features),
            basis_table,
            syndrome_table,
            jnp.zeros((LEVELS - 1 - used, features), BF16),
            my_round,
        ]
    )
    grad_chunks = grad_hidden.reshape(rounds_here, round_parts, stabs_time, features)
    grad_time = exchange(jnp.swapaxes(grad_chunks, 0, 1), "rounds")

    gain_s = gain_space.reshape(features, 1)
    gain_t = gain_time.reshape(features, 1)
    middle, *saved = space_forward(index, table, gain_s, w_qkv_space, w_out_space, parts)
    middle_time = exchange(middle, BOTH)
    middle_time = middle_time.reshape(stab_parts, round_parts, stabs_time, features)
    grad_middle, hidden, normed, grad_packed, attended, grad_rows = time_block(
        middle_time, grad_time, gain_t, w_qkv_time, w_out_time
    )
    grad_space = exchange(grad_middle.reshape(parts, stabs_time, features), BOTH)
    hidden_home = exchange(hidden, "rounds")
    hidden_home = jnp.swapaxes(hidden_home, 0, 1).reshape(grad_hidden.shape)
    time_qkv, time_out = weight_grads(normed, grad_packed, attended, grad_rows)
    scaling = 1.0 / math.sqrt(parts * rounds_here * stabs_here)
    time_grads = reduce_to_all(
        jnp.concatenate([time_qkv.reshape(-1, features), time_out]), parts, scaling
    )
    grad_stream, space_qkv, space_out = space_backward(
        grad_space, saved, gain_s, w_qkv_space, w_out_space
    )
    grad_embedded = exchange(grad_stream.reshape(rounds_here, stabs_here, features), "stab")
    space_grads = reduce_to_all(
        jnp.concatenate([space_qkv.reshape(-1, features), space_out]), parts, scaling
    )

    def unpack(grads):
        return grads[: 3 * features].reshape(features, 3 * features), grads[3 * features :]

    return (hidden_home, grad_embedded) + unpack(space_grads) + unpack(time_grads)


def solution(mesh):
    in_specs = (
        P("rounds", "stab"),
        P("stab"),
        P(None, "stab"),
        P(),
        P(),
        P(),
        P("rounds", None),
        P(),
        P(),
        P(),
        P(),
        P(),
        P(),
        P("rounds", "stab", None),
    )
    out_specs = (P("rounds", "stab", None), P("rounds", "stab", None), P(), P(), P(), P())
    return jax.shard_map(
        on_device, mesh=mesh, in_specs=in_specs, out_specs=out_specs, check_vma=False
    )
```

profile of v0, /device:TPU:1, one launch (start us, length us, event | category | flops | bytes accessed | tf_op | source)
XLA Modules:
  0.0 218.2 jit_solution(16860514168547589519)
XLA Ops:
  3.5 8.3 %all-to-all-start = ((s32[8,4,128]{2,1,0:T(4,128)}), s32[8,4,128]{2,1,0:T(4,128)S(1)}, u32[]{:S(2)}, u32[]{:S(2)}) async-start(s32[8,4,128]{2,1,0:T(4,128)} %pad_add_fusion), calls=%async_computation | async-start | bytes 32768 | tf_op jit(solution)/shard_map/all_to_all | solution.py:336
  11.8 0.9 copy_bitcast_fusion.1
  12.7 5.7 %all-to-all-done.index_ref = s32[8,4,128]{2,1,0:T(4,128)S(1)} async-done(((s32[8,4,128]{2,1,0:T(4,128)}), s32[8,4,128]{2,1,0:T(4,128)S(1)}, u32[]{:S(2)}, u32[]{:S(2)}) %all-to-all-start) | async-done | bytes 16416 | tf_op jit(solution)/shard_map/all_to_all | solution.py:336
  18.4 6.9 %all-to-all-start.2 = ((bf16[16,8,8,256]{3,2,1,0:T(8,128)(2,1)}), bf16[16,8,8,256]{3,2,1,0:T(8,128)(2,1)S(1)}, u32[]{:S(2)}, u32[]{:S(2)}) async-start(bf16[16,8,8,256]{3,2,1,0:T(8,128)(2,1)} %copy_bitcast_fusion.1), calls=%async_computation.2 | async-start | bytes 1048576 | tf_op jit(solution)/shard_map/all_to_all | solution.py:336
  26.8 3.8 %concatenate.13.table_ref = bf16[128,256]{1,0:T(8,128)(2,1)} concatenate(bf16[84,256]{1,0:T(8,128)(2,1)S(1)} %reshape.74, bf16[2,256]{1,0:T(2,128)(2,1)S(1)} %copy-done.8, bf16[2,256]{1,0:T(2,128)(2,1)S(1)} %copy-done.9, bf16[39,256]{1,0:T(8,128)(2,1)S(1)} %broadcast_in_dim.9, bf16[1,256]{1,0:T(2,128)(2,1)S(1)} %constant_dynamic-slice_fusion), dimensions={0} | concatenate | bytes 131072 | tf_op jit(solution)/shard_map/concatenate | solution.py:376
  30.6 18.4 %space_forward.1 = (bf16[128,8,256]{2,1,0:T(8,128)(2,1)}, bf16[256,1024]{1,0:T(8,128)(2,1)}, bf16[256,1024]{1,0:T(8,128)(2,1)}, f32[1,1024]{1,0:T(1,128)}, bf16[...) custom-call(s32[8,4,128]{2,1,0:T(4,128)} %copy-done.6, ...), custom_call_target="tpu_custom_call" | custom-call | flops 4000000000 | bytes 10000000 | tf_op jit(solution)/shard_map/space_forward/pallas_call | solution.py:114
  49.0 6.0 %all-to-all-start.1 = ((bf16[128,8,256]{2,1,0:T(8,128)(2,1)}), bf16[128,8,256]{2,1,0:T(8,128)(2,1)S(1)}, u32[]{:S(2)}, u32[]{:S(2)}) async-start(bf16[128,8,256]{2,1,0:T(8,128)(2,1)} %get-tuple-element.25), calls=%async_computation.1 | async-start | bytes 1048576 | tf_op jit(solution)/shard_map/all_to_all | solution.py:336
  55.8 12.9 %all-to-all-done.1 = bf16[128,8,256]{2,1,0:T(8,128)(2,1)S(1)} async-done(((bf16[128,8,256]{2,1,0:T(8,128)(2,1)}), bf16[128,8,256]{2,1,0:T(8,128)(2,1)S(1)}, u32[]{:S(2)}, u32[]{:S(2)}) %all-to-all-start.1) | async-done | bytes 524320 | tf_op jit(solution)/shard_map/all_to_all | solution.py:336
  69.5 15.3 %time_block.1 = (bf16[8,16,8,256]{3,2,1,0:T(8,128)(2,1)}, bf16[16,8,8,256]{3,2,1,0:T(8,128)(2,1)}, bf16[256,1024]{1,0:T(8,128)(2,1)}, bf16[768,1024]{1,0:T(8,128...) custom-call(bf16[8,16,8,256]{3,2,1,0:T(8,128)(2,1)} %bitcast.28, bf16[16,8,8,256]{3,2,1,0:T(8,128)(2,1)} %copy-done.1, ...), custom_call_target="tpu_custom_call" | custom-call | flops 3000000000 | bytes 7500000 | tf_op jit(solution)/shard_map/time_block/pallas_call | solution.py:220
  84.8 14.2 %all_to_all.50 = bf16[16,8,8,256]{3,2,1,0:T(8,128)(2,1)S(1)} all-to-all(bf16[16,8,8,256]{3,2,1,0:T(8,128)(2,1)} %get-tuple-element.26), channel_id=1, replica_groups=mesh['rounds'=16,'stab'=8] {'rounds'}, dimensions={0} | all-to-all | bytes 1048576 | tf_op jit(solution)/shard_map/all_to_all | solution.py:336
  99.0 4.5 %all-to-all-start.4 = ((bf16[128,8,256]{2,1,0:T(8,128)(2,1)}), bf16[128,8,256]{2,1,0:T(8,128)(2,1)S(1)}, u32[]{:S(2)}, u32[]{:S(2)}) async-start(bf16[128,8,256]{2,1,0:T(8,128)(2,1)} %bitcast.27), calls=%async_computation.4 | async-start | bytes 1048576 | tf_op jit(solution)/shard_map/all_to_all | solution.py:336
  103.4 3.4 %weight_grads.1 = (bf16[256,768]{1,0:T(8,128)(2,1)}, bf16[256,256]{1,0:T(8,128)(2,1)}) custom-call(bf16[256,1024]{1,0:T(8,128)(2,1)} %get-tuple-element.38.normed_ref, bf16[768,1024]{1,0:T(8,128)(2,1)} %get-tuple-element.39.grad_packed_ref, bf16[256,1024]{1,0:T(8,128)(2,1)} %get-tuple-element.40.attended_ref, bf16[1024,256]{1,0:T(8,128)(2,1)} %get-tuple-element.41.grad_ref), custom_call_target="tpu_custom_call" | custom-call | flops 600000000 | bytes 1500000 | tf_op jit(solution)/shard_map/weight_grads/pallas_call | solution.py:324
  106.8 1.2 reshape.85
  108.0 1.8 maximum_bitcast_fusion.1
  109.7 7.6 %all-to-all-done.4.grad_ref = bf16[128,8,256]{2,1,0:T(8,128)(2,1)S(1)} async-done(((bf16[128,8,256]{2,1,0:T(8,128)(2,1)}), bf16[128,8,256]{2,1,0:T(8,128)(2,1)S(1)}, u32[]{:S(2)}, u32[]{:S(2)}) %all-to-all-start.4) | async-done | bytes 524320 | tf_op jit(solution)/shard_map/all_to_all | solution.py:336
  117.3 4.5 %all-to-all-start.8 = ((bf16[128,8,256]{2,1,0:T(8,128)(2,1)}), bf16[128,8,256]{2,1,0:T(8,128)(2,1)S(1)}, u32[]{:S(2)}, u32[]{:S(2)}) async-start(bf16[128,8,256]{2,1,0:T(8,128)(2,1)} %maximum_bitcast_fusion.1), calls=%async_computation.8 | async-start | bytes 1048576 | tf_op jit(solution)/shard_map/all_to_all | solution.py:336
  121.8 17.1 %space_backward.1 = (bf16[1024,256]{1,0:T(8,128)(2,1)}, bf16[256,768]{1,0:T(8,128)(2,1)}, bf16[256,256]{1,0:T(8,128)(2,1)}) custom-call(bf16[128,8,256]{2,1,0:T(8,128)(2,1)} %copy-done.2, bf16[256,1024]{1,0:T(8,128)(2,1)} %get-tuple-element.28.x_ref, bf16[256,1024]{1,0:T(8,128)(2,1)} %get-tuple-element.29.normed_ref, ...), custom_call_target="tpu_custom_call" | custom-call | flops 8000000000 | bytes 20000000 | tf_op jit(solution)/shard_map/space_backward/pallas_call | solution.py:302
  139.0 7.2 %all-to-all-start.5 = ((bf16[8,128,256]{2,1,0:T(8,128)(2,1)}), bf16[8,128,256]{2,1,0:T(8,128)(2,1)S(1)}, u32[]{:S(2)}, u32[]{:S(2)}) async-start(bf16[8,128,256]{2,1,0:T(8,128)(2,1)} %bitcast.26), calls=%async_computation.5 | async-start | bytes 1048576 | tf_op jit(solution)/shard_map/all_to_all | solution.py:336
  146.2 1.2 reshape.82
  147.4 0.8 maximum_bitcast_fusion
  148.2 8.7 %all-to-all-done.5 = bf16[8,128,256]{2,1,0:T(8,128)(2,1)S(1)} async-done(((bf16[8,128,256]{2,1,0:T(8,128)(2,1)}), bf16[8,128,256]{2,1,0:T(8,128)(2,1)S(1)}, u32[]{:S(2)}, u32[]{:S(2)}) %all-to-all-start.5) | async-done | bytes 524320 | tf_op jit(solution)/shard_map/all_to_all | solution.py:336
  156.9 6.6 %all-to-all-start.6 = ((bf16[128,8,256]{2,1,0:T(8,128)(2,1)}), bf16[128,8,256]{2,1,0:T(8,128)(2,1)S(1)}, u32[]{:S(2)}, u32[]{:S(2)}) async-start(bf16[128,8,256]{2,1,0:T(8,128)(2,1)} %maximum_bitcast_fusion), calls=%async_computation.6 | async-start | bytes 1048576 | tf_op jit(solution)/shard_map/all_to_all | solution.py:336
  163.7 13.6 %all-to-all-done.6 = bf16[128,8,256]{2,1,0:T(8,128)(2,1)S(1)} async-done(((bf16[128,8,256]{2,1,0:T(8,128)(2,1)}), bf16[128,8,256]{2,1,0:T(8,128)(2,1)S(1)}, u32[]{:S(2)}, u32[]{:S(2)}) %all-to-all-start.6) | async-done | bytes 524320 | tf_op jit(solution)/shard_map/all_to_all | solution.py:336
  177.3 0.8 broadcast_in_dim.11
  178.1 4.5 %all-to-all-start.9 = ((bf16[128,8,256]{2,1,0:T(8,128)(2,1)}), bf16[128,8,256]{2,1,0:T(8,128)(2,1)S(1)}, u32[]{:S(2)}, u32[]{:S(2)}) async-start(bf16[128,8,256]{2,1,0:T(8,128)(2,1)} %broadcast_in_dim.11), calls=%async_computation.9 | async-start | bytes 1048576 | tf_op jit(solution)/shard_map/all_to_all | solution.py:336
  182.8 13.6 %all-to-all-done.9 = bf16[128,8,256]{2,1,0:T(8,128)(2,1)S(1)} async-done(((bf16[128,8,256]{2,1,0:T(8,128)(2,1)}), bf16[128,8,256]{2,1,0:T(8,128)(2,1)S(1)}, u32[]{:S(2)}, u32[]{:S(2)}) %all-to-all-start.9) | async-done | bytes 524320 | tf_op jit(solution)/shard_map/all_to_all | solution.py:336
  196.3 0.8 broadcast_in_dim.10
  197.2 4.5 %all-to-all-start.7 = ((bf16[128,8,256]{2,1,0:T(8,128)(2,1)}), bf16[128,8,256]{2,1,0:T(8,128)(2,1)S(1)}, u32[]{:S(2)}, u32[]{:S(2)}) async-start(bf16[128,8,256]{2,1,0:T(8,128)(2,1)} %broadcast_in_dim.10), calls=%async_computation.7 | async-start | bytes 1048576 | tf_op jit(solution)/shard_map/all_to_all | solution.py:336
  201.7 0.8 copy_bitcast_fusion
  202.6 1.1 reshape.87
  204.5 10.9 %all-to-all-done.7 = bf16[128,8,256]{2,1,0:T(8,128)(2,1)S(1)} async-done(((bf16[128,8,256]{2,1,0:T(8,128)(2,1)}), bf16[128,8,256]{2,1,0:T(8,128)(2,1)S(1)}, u32[]{:S(2)}, u32[]{:S(2)}) %all-to-all-start.7) | async-done | bytes 524320 | tf_op jit(solution)/shard_map/all_to_all | solution.py:336
  215.5 1.1 reshape.84
  (47 shorter events, 8.7 us)
Async XLA Ops:
  0.6 11.2 %copy-start = (bf16[8,128,256]{2,1,0:T(8,128)(2,1)S(1)}, bf16[8,128,256]{2,1,0:T(8,128)(2,1)}, u32[]{:S(2)}) copy-start(bf16[8,128,256]{2,1,0:T(8,128)(2,1)} %param.27) | copy-start | bytes 1572868
  0.6 24.6 %copy-start.5 = (bf16[2,42,256]{2,0,1:T(2,128)(2,1)S(1)}, bf16[2,42,256]{2,0,1:T(2,128)(2,1)}, u32[]{:S(2)}) copy-start(bf16[2,42,256]{2,0,1:T(2,128)(2,1)} %param.19) | copy-start | bytes 129028
  0.7 24.6 %copy-start.7 = (f32[256]{0:T(256)S(1)}, f32[256]{0:T(256)}, u32[]{:S(2)}) copy-start(f32[256]{0:T(256)} %param.21) | copy-start | bytes 3076
  0.7 26.1 %copy-start.8 = (bf16[2,256]{1,0:T(2,128)(2,1)S(1)}, bf16[2,256]{1,0:T(2,128)(2,1)}, u32[]{:S(2)}) copy-start(bf16[2,256]{1,0:T(2,128)(2,1)} %param.18) | copy-start | bytes 3076
  0.7 26.1 %copy-start.9 = (bf16[2,256]{1,0:T(2,128)(2,1)S(1)}, bf16[2,256]{1,0:T(2,128)(2,1)}, u32[]{:S(2)}) copy-start(bf16[2,256]{1,0:T(2,128)(2,1)} %param.17) | copy-start | bytes 3076
  3.5 14.9 %all-to-all-start = ((s32[8,4,128]{2,1,0:T(4,128)}), s32[8,4,128]{2,1,0:T(4,128)S(1)}, u32[]{:S(2)}, u32[]{:S(2)}) async-start(s32[8,4,128]{2,1,0:T(4,128)} %pad_add_fusion), calls=%async_computation | async-start | bytes 32768 | tf_op jit(solution)/shard_map/all_to_all | solution.py:336
  18.4 12.3 %copy-start.6 = (s32[8,4,128]{2,1,0:T(4,128)}, s32[8,4,128]{2,1,0:T(4,128)S(1)}, u32[]{:S(2)}) copy-start(s32[8,4,128]{2,1,0:T(4,128)S(1)} %all-to-all-done.index_ref) | copy-start | bytes 49156
  18.4 30.6 %all-to-all-start.2 = ((bf16[16,8,8,256]{3,2,1,0:T(8,128)(2,1)}), bf16[16,8,8,256]{3,2,1,0:T(8,128)(2,1)S(1)}, u32[]{:S(2)}, u32[]{:S(2)}) async-start(bf16[16,8,8,256]{3,2,1,0:T(8,128)(2,1)} %copy_bitcast_fusion.1), calls=%async_computation.2 | async-start | bytes 1048576 | tf_op jit(solution)/shard_map/all_to_all | solution.py:336
  30.6 24.3 %copy-start.10 = (f32[256]{0:T(256)S(1)}, f32[256]{0:T(256)}, u32[]{:S(2)}) copy-start(f32[256]{0:T(256)} %param.24) | copy-start | bytes 3076
  49.0 19.7 %copy-start.1 = (bf16[16,8,8,256]{3,2,1,0:T(8,128)(2,1)}, bf16[16,8,8,256]{3,2,1,0:T(8,128)(2,1)S(1)}, u32[]{:S(2)}) copy-start(bf16[16,8,8,256]{3,2,1,0:T(8,128)(2,1)S(1)} %all-to-all-done.2.grad_ref) | copy-start | bytes 1572868
  49.0 19.7 %all-to-all-start.1 = ((bf16[128,8,256]{2,1,0:T(8,128)(2,1)}), bf16[128,8,256]{2,1,0:T(8,128)(2,1)S(1)}, u32[]{:S(2)}, u32[]{:S(2)}) async-start(bf16[128,8,256]{2,1,0:T(8,128)(2,1)} %get-tuple-element.25), calls=%async_computation.1 | async-start | bytes 1048576 | tf_op jit(solution)/shard_map/all_to_all | solution.py:336
  68.7 0.8 copy-start.3
  99.0 18.3 %all-to-all-start.4 = ((bf16[128,8,256]{2,1,0:T(8,128)(2,1)}), bf16[128,8,256]{2,1,0:T(8,128)(2,1)S(1)}, u32[]{:S(2)}, u32[]{:S(2)}) async-start(bf16[128,8,256]{2,1,0:T(8,128)(2,1)} %bitcast.27), calls=%async_computation.4 | async-start | bytes 1048576 | tf_op jit(solution)/shard_map/all_to_all | solution.py:336
  117.3 4.5 %copy-start.2 = (bf16[128,8,256]{2,1,0:T(8,128)(2,1)}, bf16[128,8,256]{2,1,0:T(8,128)(2,1)S(1)}, u32[]{:S(2)}) copy-start(bf16[128,8,256]{2,1,0:T(8,128)(2,1)S(1)} %all-to-all-done.4.grad_ref) | copy-start | bytes 1572868
  117.3 21.7 %all-to-all-start.8 = ((bf16[128,8,256]{2,1,0:T(8,128)(2,1)}), bf16[128,8,256]{2,1,0:T(8,128)(2,1)S(1)}, u32[]{:S(2)}, u32[]{:S(2)}) async-start(bf16[128,8,256]{2,1,0:T(8,128)(2,1)} %maximum_bitcast_fusion.1), calls=%async_computation.8 | async-start | bytes 1048576 | tf_op jit(solution)/shard_map/all_to_all | solution.py:336
  139.0 8.4 %copy-start.4 = (bf16[256,256]{1,0:T(8,128)(2,1)S(1)}, bf16[256,256]{1,0:T(8,128)(2,1)}, u32[]{:S(2)}) copy-start(bf16[256,256]{1,0:T(8,128)(2,1)} %get-tuple-element.37) | copy-start | bytes 393220
  139.0 18.0 %all-to-all-start.5 = ((bf16[8,128,256]{2,1,0:T(8,128)(2,1)}), bf16[8,128,256]{2,1,0:T(8,128)(2,1)S(1)}, u32[]{:S(2)}, u32[]{:S(2)}) async-start(bf16[8,128,256]{2,1,0:T(8,128)(2,1)} %bitcast.26), calls=%async_computation.5 | async-start | bytes 1048576 | tf_op jit(solution)/shard_map/all_to_all | solution.py:336
  156.9 20.3 %all-to-all-start.6 = ((bf16[128,8,256]{2,1,0:T(8,128)(2,1)}), bf16[128,8,256]{2,1,0:T(8,128)(2,1)S(1)}, u32[]{:S(2)}, u32[]{:S(2)}) async-start(bf16[128,8,256]{2,1,0:T(8,128)(2,1)} %maximum_bitcast_fusion), calls=%async_computation.6 | async-start | bytes 1048576 | tf_op jit(solution)/shard_map/all_to_all | solution.py:336
  178.1 18.2 %all-to-all-start.9 = ((bf16[128,8,256]{2,1,0:T(8,128)(2,1)}), bf16[128,8,256]{2,1,0:T(8,128)(2,1)S(1)}, u32[]{:S(2)}, u32[]{:S(2)}) async-start(bf16[128,8,256]{2,1,0:T(8,128)(2,1)} %broadcast_in_dim.11), calls=%async_computation.9 | async-start | bytes 1048576 | tf_op jit(solution)/shard_map/all_to_all | solution.py:336
  197.2 18.2 %all-to-all-start.7 = ((bf16[128,8,256]{2,1,0:T(8,128)(2,1)}), bf16[128,8,256]{2,1,0:T(8,128)(2,1)S(1)}, u32[]{:S(2)}, u32[]{:S(2)}) async-start(bf16[128,8,256]{2,1,0:T(8,128)(2,1)} %broadcast_in_dim.10), calls=%async_computation.7 | async-start | bytes 1048576 | tf_op jit(solution)/shard_map/all_to_all | solution.py:336
where the time goes:
time: 219 us; the launch traced here: 218 us
  waiting for transfers between devices  72.9 us (33%)
  Pallas kernels  54.1 us (25%)
  starting transfers between devices  53 us (24%)
  local copies, waits for them, and re-layouts  17.2 us (8%)
  blocking collectives  14.2 us (6%)
  other arithmetic  5.79 us (3%)
    all_to_all x9, waiting for transfers between devices, exchange(): return lax.all_to_all(values, axes, split_axis=0, concat_axis=0, tiled=True)  72.9 us
    all_to_all x9, starting transfers between devices, exchange(): return lax.all_to_all(values, axes, split_axis=0, concat_axis=0, tiled=True)  53 us
    pallas_call x1, Pallas kernels, space_forward(): pl.pallas_call(space_forward_kernel, grid=(HEADS,), out_shape=[jax.ShapeD...  18.4 us
    pallas_call x1, Pallas kernels, space_backward(): pl.pallas_call(space_backward_kernel, grid=(HEADS,), out_shape=[jax.Shape...  17.1 us
    pallas_call x1, Pallas kernels, time_block(): pl.pallas_call(time_kernel, out_shape=[jax.ShapeDtypeStruct(*item) for it...  15.3 us
    all_to_all x1, blocking collectives, exchange(): return lax.all_to_all(values, axes, split_axis=0, concat_axis=0, tiled=True)  14.2 us
  transfers between devices with their start and end apart: 9, of which 7 were waited for; matrix products, arithmetic and copies ran while one was open for 7% of the time, Pallas kernels for 18%

commit v1 on v0

v1 whole, which is shorter than its diff:
```python
import math

import jax
import jax.numpy as jnp
from jax import lax
from jax.experimental import pallas as pl
from jax.experimental.pallas import tpu as pltpu
from jax.sharding import PartitionSpec as P

HEADS = 4
EPSILON = 1e-06
F32 = jnp.float32
BF16 = jnp.bfloat16

LEVELS = 128
ROW_AT, COLUMN_AT, BASIS_AT, SYNDROME_AT, ROUND_AT = 0, 48, 96, 104, 112


def dot(left, right, left_dim, right_dim):
    return lax.dot_general(
        left, right, (((left_dim,), (right_dim,)), ((), ())), preferred_element_type=F32
    )


def call(kernel, shapes, arguments, megabytes, microseconds, scratch=(), **grid):
    return pl.pallas_call(
        kernel,
        out_shape=[jax.ShapeDtypeStruct(*item) for item in shapes],
        scratch_shapes=[pltpu.VMEM(*item) for item in scratch],
        compiler_params=pltpu.CompilerParams(vmem_limit_bytes=megabytes * 2**20),
        cost_estimate=pl.CostEstimate(
            flops=microseconds * 500_000_000,
            bytes_accessed=microseconds * 2_000_000,
            transcendentals=0,
        ),
        name=kernel.__name__,
        **grid,
    )(*arguments)


def whole(shape):
    return pl.BlockSpec(shape, lambda *_: (0,) * len(shape))


def per_head(shape):
    return pl.BlockSpec((1,) + shape[1:], lambda head: (head,) + (0,) * (len(shape) - 1))


def as_column(gain):
    return jnp.broadcast_to(gain, (8, gain.shape[1])).T[:, :1]


def norm_columns(values, gain):
    inverse = lax.rsqrt(jnp.mean(values * values, axis=0, keepdims=True) + EPSILON)
    return (values * inverse * gain).astype(BF16), inverse


def norm_columns_backward(values, gain, inverse, grad_normed):
    gained = grad_normed * gain
    inner = jnp.mean(gained * values, axis=0, keepdims=True)
    return inverse * gained - values * (inverse * inverse * inverse) * inner


def store_blocks(ref, kind, grad_qkv, grad_out):
    features = grad_out.shape[0]
    blocks = [grad_qkv[:, j * features : (j + 1) * features] for j in range(3)] + [grad_out]
    count = ref.shape[0] // len(blocks)
    for j, block in enumerate(blocks):
        ref[j * count : (j + 1) * count, kind] = block.astype(BF16).reshape(
            count, ref.shape[2], features
        )


def index_kernel(syndrome_ref, basis_ref, coordinates_ref, index_ref):
    width = index_ref.shape[2]
    for block in range(index_ref.shape[0]):
        index_ref[block, 0:1, :] = syndrome_ref[block : block + 1, :] + SYNDROME_AT
        index_ref[block, 1:2, :] = basis_ref[...] + BASIS_AT
        index_ref[block, 2:3, :] = coordinates_ref[0:1, :] + ROW_AT
        index_ref[block, 3:4, :] = coordinates_ref[1:2, :] + COLUMN_AT
        index_ref[block, 4:5, :] = jnp.full((1, width), ROUND_AT + block, jnp.int32)


def space_forward(
    index_ref, syndrome_table_ref, basis_table_ref, coord_table_ref, round_table_ref,
    gain_ref, w_qkv_ref, w_out_ref,
    middle_ref, x_ref, normed_ref, inverse_ref, packed_ref, attended_ref, exps_ref, total_ref,
    table_ref, row_ref, onehot_ref,
):
    head = pl.program_id(0)
    features, tokens = x_ref.shape
    depth = features // HEADS

    @pl.when(head == 0)
    def _():
        coords = coord_table_ref.shape[1]
        table_ref[...] = jnp.zeros(table_ref.shape, F32)
        table_ref[ROW_AT : ROW_AT + coords, :] = coord_table_ref[0].astype(F32)
        table_ref[COLUMN_AT : COLUMN_AT + coords, :] = coord_table_ref[1].astype(F32)
        table_ref[BASIS_AT : BASIS_AT + 2, :] = basis_table_ref[...].astype(F32)
        table_ref[SYNDROME_AT : SYNDROME_AT + 2, :] = syndrome_table_ref[...].astype(F32)
        rounds = round_table_ref.shape[0]
        table_ref[ROUND_AT : ROUND_AT + rounds, :] = round_table_ref[...].astype(F32)
        width = index_ref.shape[2]
        levels = lax.broadcasted_iota(jnp.int32, (LEVELS, width), 0)
        for block in range(index_ref.shape[0]):
            hit = levels == index_ref[block, 0:1, :]
            for kind in range(1, index_ref.shape[1]):
                hit = hit | (levels == index_ref[block, kind : kind + 1, :])
            onehot_ref[:, block * width : (block + 1) * width] = hit.astype(F32).astype(BF16)
        onehot = onehot_ref[...]
        table = table_ref[...].astype(BF16)
        row_ref[...] = dot(onehot, table, 0, 0).astype(BF16)
        x = dot(table, onehot, 0, 0).astype(BF16)
        x_ref[...] = x
        normed, inverse = norm_columns(x.astype(F32), as_column(gain_ref[...]))
        normed_ref[...] = normed
        inverse_ref[...] = inverse
        packed = dot(w_qkv_ref[...], normed, 0, 0)
        packed_ref[:features, :] = (packed[:features] * (math.log2(math.e) * depth**-0.5)).astype(
            BF16
        )
        packed_ref[features:, :] = packed[features:].astype(BF16)

    at = pl.multiple_of(head * depth, depth)
    query = packed_ref[pl.ds(at, depth), :]
    keys = packed_ref[pl.ds(features + at, depth), :].T
    values = packed_ref[pl.ds(2 * features + at, depth), :]
    values = jnp.concatenate([values, jnp.ones((16, tokens), BF16)])
    block = SPACE_BLOCK
    starts = list(range(0, tokens, block))
    scores = dot(keys, query[:, :block], 1, 0)
    for start in starts:
        cols = slice(start, start + block)
        if start + block < tokens:
            later = dot(keys, query[:, start + block : start + 2 * block], 1, 0)
        exps = jnp.exp2(scores - jnp.max(scores, axis=0, keepdims=True)).astype(BF16)
        exps_ref[0, :, cols] = exps
        product = dot(values, exps, 1, 0)
        inverse_total = 1.0 / product[depth : depth + 1]
        total_ref[0, :, cols] = inverse_total
        attended_ref[pl.ds(at, depth), cols] = (product[:depth] * inverse_total).astype(BF16)
        scores = later

    @pl.when(head == HEADS - 1)
    def _():
        branch = dot(attended_ref[...], w_out_ref[...], 0, 0)
        middle = (row_ref[...].astype(F32) + branch).astype(BF16)
        middle_ref[...] = middle.reshape(middle_ref.shape)


SPACE_BLOCK = 256


def run_space_forward(index, tables, gain, w_qkv, w_out, chunks):
    tokens = index.shape[0] * index.shape[2]
    features = w_out.shape[0]
    shapes = [
        ((chunks, tokens // chunks, features), BF16),
        ((features, tokens), BF16),
        ((features, tokens), BF16),
        ((1, tokens), F32),
        ((3 * features, tokens), BF16),
        ((features, tokens), BF16),
        ((HEADS, tokens, tokens), BF16),
        ((HEADS, 1, tokens), F32),
    ]
    arguments = (index,) + tables + (gain, w_qkv, w_out)
    return call(
        space_forward,
        shapes,
        arguments,
        32,
        10,
        scratch=[
            ((LEVELS, features), F32),
            ((tokens, features), BF16),
            ((LEVELS, tokens), BF16),
        ],
        grid=(HEADS,),
        in_specs=[whole(a.shape) for a in arguments],
        out_specs=[whole(shape) for shape, _ in shapes[:6]]
        + [per_head(shape) for shape, _ in shapes[6:]],
    )


def time_block(
    middle_ref, grad_ref, gain_ref, w_qkv_ref, w_out_ref,
    grad_middle_ref, normed_ref, grad_packed_ref, attended_ref, grad_row_ref,
    x_ref, inverse_ref, packed_ref, grad_attended_ref, rows_ref, grads_ref,
):
    stab_parts, round_parts, stabs, features = middle_ref.shape
    rounds = stab_parts * round_parts
    tokens = rounds * stabs
    depth = features // HEADS
    scale = depth**-0.5

    middle = jnp.swapaxes(middle_ref[...].astype(F32), 0, 1).reshape(tokens, features)
    grad = grad_ref[...].astype(F32).reshape(tokens, features)
    lanes = rows_ref.shape[2]
    halves = [slice(part * lanes, (part + 1) * lanes) for part in range(features // lanes)]
    for part, half in enumerate(halves):
        rows_ref[part] = middle[:, half]
        grads_ref[part] = grad[:, half]
    for stab in range(stabs):
        cols = slice(stab * rounds, (stab + 1) * rounds)
        at = pl.ds(stab, rounds, stride=stabs)
        for part, half in enumerate(halves):
            x_ref[half, cols] = rows_ref[part, at, :].T
            grad_row_ref[cols, half] = grads_ref[part, at, :].astype(BF16)
    x = x_ref[...]
    gain = as_column(gain_ref[...])
    normed, inverse = norm_columns(x, gain)
    normed_ref[...] = normed
    inverse_ref[...] = inverse
    packed = dot(w_qkv_ref[...], normed, 0, 0)
    to_base_two = math.log2(math.e) * scale
    packed_ref[:features, :] = (packed[:features] * to_base_two).astype(BF16)
    packed_ref[features:, :] = packed[features:].astype(BF16)
    grad_attended_ref[...] = dot(w_out_ref[...], grad_row_ref[...], 1, 1).astype(BF16)

    def one_stab(stab, carry):
        cols = pl.ds(pl.multiple_of(stab * rounds, rounds), rounds)
        for head in range(HEADS):
            at = head * depth
            query = packed_ref[at : at + depth, cols]
            keys = packed_ref[features + at : features + at + depth, cols]
            values = packed_ref[2 * features + at : 2 * features + at + depth, cols]
            grad = grad_attended_ref[at : at + depth, cols]
            scores = dot(keys, query, 0, 0)
            shifted = jnp.exp2(scores - jnp.max(scores, axis=0, keepdims=True))
            probabilities = shifted * (1.0 / jnp.sum(shifted, axis=0, keepdims=True))
            weights = probabilities.astype(BF16)
            attended_ref[at : at + depth, cols] = dot(values, weights, 1, 0).astype(BF16)
            grad_weights = dot(values, grad, 0, 0)
            inner = jnp.sum(probabilities * grad_weights, axis=0, keepdims=True)
            grad_scores = (probabilities * (grad_weights - inner)).astype(BF16)
            grad_packed_ref[at : at + depth, cols] = (dot(keys, grad_scores, 1, 0) * scale).astype(
                BF16
            )
            grad_packed_ref[features + at : features + at + depth, cols] = (
                dot(query, grad_scores, 1, 1) * math.log(2.0)
            ).astype(BF16)
            grad_packed_ref[2 * features + at : 2 * features + at + depth, cols] = dot(
                grad, weights, 1, 1
            ).astype(BF16)
        return carry

    lax.fori_loop(0, stabs, one_stab, 0, unroll=TIME_UNROLL)

    grad_normed = dot(w_qkv_ref[...], grad_packed_ref[...], 1, 0)
    grad_stream = norm_columns_backward(x_ref[...], gain, inverse_ref[...], grad_normed)
    for stab in range(stabs):
        cols = slice(stab * rounds, (stab + 1) * rounds)
        at = pl.ds(stab, rounds, stride=stabs)
        for part, half in enumerate(halves):
            grads_ref[part, at, :] = grads_ref[part, at, :] + grad_stream[half, cols].T
    for part, half in enumerate(halves):
        grad_middle = grads_ref[part].reshape(round_parts, stab_parts, stabs, lanes)
        grad_middle_ref[:, :, :, half] = jnp.swapaxes(grad_middle, 0, 1).astype(BF16)


TIME_UNROLL = 2


def run_time_block(middle, grad, gain, w_qkv, w_out):
    stab_parts, round_parts, stabs, features = middle.shape
    tokens = stab_parts * round_parts * stabs
    shapes = [
        (middle.shape, BF16),
        ((features, tokens), BF16),
        ((3 * features, tokens), BF16),
        ((features, tokens), BF16),
        ((tokens, features), BF16),
    ]
    return call(
        time_block,
        shapes,
        (middle, grad, gain, w_qkv, w_out),
        24,
        10,
        scratch=[
            ((features, tokens), F32),
            ((1, tokens), F32),
            ((3 * features, tokens), BF16),
            ((features, tokens), BF16),
            ((features // 128, tokens, 128), F32),
            ((features // 128, tokens, 128), F32),
        ],
    )


def time_rest(
    middle_ref, normed_ref, grad_packed_ref, attended_ref, grad_row_ref, w_out_ref,
    hidden_ref, pieces_ref,
    rows_ref,
):
    stab_parts, round_parts, stabs, features = middle_ref.shape
    rounds = stab_parts * round_parts
    tokens = rounds * stabs
    lanes = rows_ref.shape[2]
    halves = [slice(part * lanes, (part + 1) * lanes) for part in range(features // lanes)]
    attended = attended_ref[...]
    branch = dot(attended, w_out_ref[...], 0, 0)
    middle = jnp.swapaxes(middle_ref[...].astype(F32), 0, 1).reshape(tokens, features)
    for part, half in enumerate(halves):
        rows_ref[part] = middle[:, half]
    for stab in range(stabs):
        cols = slice(stab * rounds, (stab + 1) * rounds)
        at = pl.ds(stab, rounds, stride=stabs)
        for part, half in enumerate(halves):
            rows_ref[part, at, :] = rows_ref[part, at, :] + branch[cols, half]
    for part, half in enumerate(halves):
        hidden = rows_ref[part].reshape(hidden_ref.shape[:3] + (lanes,))
        hidden_ref[:, :, :, half] = hidden.astype(BF16)
    store_blocks(
        pieces_ref,
        0,
        dot(normed_ref[...], grad_packed_ref[...], 1, 1),
        dot(attended, grad_row_ref[...], 1, 0),
    )


def run_time_rest(middle, grad_shape, normed, grad_packed, attended, grad_rows, w_out):
    features, tokens = normed.shape
    parts = middle.shape[0] * middle.shape[1]
    return call(
        time_rest,
        [(grad_shape, BF16), ((parts, 1, 4 * features // parts, features), BF16)],
        (middle, normed, grad_packed, attended, grad_rows, w_out),
        24,
        5,
        scratch=[((features // 128, tokens, 128), F32)],
    )


def space_backward(
    grad_ref, normed_ref, packed_ref, attended_ref, exps_ref, total_ref, w_out_ref, time_ref,
    grad_packed_ref, pieces_ref,
    grad_attended_ref, grad_scores_ref,
):
    head = pl.program_id(0)
    features, tokens = attended_ref.shape
    depth = features // HEADS

    @pl.when(head == 0)
    def _():
        grad = grad_ref[...].reshape(tokens, features)
        grad_attended_ref[...] = dot(w_out_ref[...], grad, 1, 1).astype(BF16)

    at = pl.multiple_of(head * depth, depth)
    query = packed_ref[pl.ds(at, depth), :]
    keys = packed_ref[pl.ds(features + at, depth), :]
    values = packed_ref[pl.ds(2 * features + at, depth), :].T
    grad = grad_attended_ref[pl.ds(at, depth), :].astype(F32) * total_ref[0]
    inner = jnp.sum(
        grad * attended_ref[pl.ds(at, depth), :].astype(F32), axis=0, keepdims=True
    )
    grad = grad.astype(BF16)
    block = SPACE_BLOCK
    grad_weights = dot(values, grad[:, :block], 1, 0)
    for start in range(0, tokens, block):
        cols = slice(start, start + block)
        if start + block < tokens:
            later = dot(values, grad[:, start + block : start + 2 * block], 1, 0)
        exps = exps_ref[0, :, cols].astype(F32)
        grad_scores = (exps * (grad_weights - inner[:, cols])).astype(BF16)
        grad_scores_ref[:, cols] = grad_scores
        grad_query = dot(keys, grad_scores, 1, 0) * depth**-0.5
        grad_packed_ref[pl.ds(at, depth), cols] = grad_query.astype(BF16)
        grad_weights = later
    grad_packed_ref[pl.ds(2 * features + at, depth), :] = dot(grad, exps_ref[0], 1, 1).astype(BF16)
    grad_packed_ref[pl.ds(features + at, depth), :] = (
        dot(query, grad_scores_ref[...], 1, 1) * math.log(2.0)
    ).astype(BF16)

    @pl.when(head == HEADS - 1)
    def _():
        grad = grad_ref[...].reshape(tokens, features)
        pieces_ref[:, 0:1] = time_ref[...]
        store_blocks(
            pieces_ref,
            1,
            dot(normed_ref[...], grad_packed_ref[...], 1, 1),
            dot(attended_ref[...], grad, 1, 0),
        )


def run_space_backward(grad, normed, packed, attended, exps, totals, w_out, time_pieces):
    features, tokens = attended.shape
    arguments = (grad, normed, packed, attended, exps, totals, w_out, time_pieces)
    in_specs = [whole(a.shape) for a in arguments]
    in_specs[4] = per_head(exps.shape)
    in_specs[5] = per_head(totals.shape)
    parts, _, rows, _ = time_pieces.shape
    shapes = [((3 * features, tokens), BF16), ((parts, 2, rows, features), BF16)]
    return call(
        space_backward,
        shapes,
        arguments,
        32,
        14,
        scratch=[((features, tokens), BF16), ((tokens, tokens), BF16)],
        grid=(HEADS,),
        in_specs=in_specs,
        out_specs=[whole(shape) for shape, _ in shapes],
    )


def space_stream(
    grad_ref, x_ref, inverse_ref, grad_packed_ref, gain_ref, w_qkv_ref, out_ref
):
    features, tokens = x_ref.shape
    grad_normed = dot(w_qkv_ref[...], grad_packed_ref[...], 1, 0)
    grad_stream = norm_columns_backward(
        x_ref[...].astype(F32), as_column(gain_ref[...]), inverse_ref[...], grad_normed
    )
    parts, groups, rows, _ = out_ref.shape
    grad_new = grad_ref[...].reshape(tokens, features).astype(F32)
    result = (grad_new + grad_stream.T).astype(BF16)
    here = tokens // (parts * rows)
    out_ref[:, :here] = result.reshape(parts, here, rows, features)
    out_ref[:, here:] = jnp.zeros((parts, groups - here, rows, features), BF16)


def run_space_stream(grad, x, inverse, grad_packed, gain, w_qkv, parts):
    features, tokens = x.shape
    rows = grad.shape[1]
    return call(
        space_stream,
        [((parts, tokens // (parts * rows) + 2, rows, features), BF16)],
        (grad, x, inverse, grad_packed, gain, w_qkv),
        24,
        4,
    )[0]


def unpack_weights(pieces_ref, space_qkv_ref, space_out_ref, time_qkv_ref, time_out_ref):
    features = space_out_ref.shape[0]
    count = pieces_ref.shape[0] // 4
    for kind, qkv_ref, out_ref in (
        (0, time_qkv_ref, time_out_ref),
        (1, space_qkv_ref, space_out_ref),
    ):
        for j in range(4):
            block = pieces_ref[j * count : (j + 1) * count, kind].reshape(features, features)
            if j < 3:
                qkv_ref[:, j * features : (j + 1) * features] = block.astype(F32)
            else:
                out_ref[...] = block.astype(F32)


def exchange(values, axes):
    return lax.all_to_all(values, axes, split_axis=0, concat_axis=0, tiled=True)


def on_device(
    syndrome,
    basis_ids,
    coordinates,
    syndrome_table,
    basis_table,
    coord_table,
    round_table,
    gain_space,
    w_qkv_space,
    w_out_space,
    gain_time,
    w_qkv_time,
    w_out_time,
    grad_hidden,
):
    stab_parts = lax.axis_size("stab")
    round_parts = lax.axis_size("rounds")
    parts = stab_parts * round_parts
    rounds_here, stabs_here, features = grad_hidden.shape
    stabs_time = stabs_here // round_parts

    own_index = call(
        index_kernel,
        [((stab_parts, 5, stabs_here), jnp.int32)],
        (syndrome, basis_ids.reshape(1, stabs_here), coordinates),
        4,
        1,
    )[0]
    index = exchange(own_index, "stab")
    grad_chunks = grad_hidden.reshape(rounds_here, round_parts, stabs_time, features)
    grad_chunks, index = lax.optimization_barrier((jnp.swapaxes(grad_chunks, 0, 1), index))
    grad_time = exchange(grad_chunks, "rounds")

    gain_s = gain_space.reshape(1, features)
    gain_t = gain_time.reshape(1, features)
    tables = (syndrome_table, basis_table, coord_table, round_table)
    middle, x, normed, inverse, packed, attended, exps, totals = run_space_forward(
        index, tables, gain_s, w_qkv_space, w_out_space, parts
    )
    middle_time = exchange(middle, ("stab", "rounds"))
    middle_time = middle_time.reshape(stab_parts, round_parts, stabs_time, features)
    grad_middle, normed_t, grad_packed_t, attended_t, grad_rows = run_time_block(
        middle_time, grad_time, gain_t, w_qkv_time, w_out_time
    )
    grad_space = exchange(grad_middle.reshape(parts, stabs_time, features), ("stab", "rounds"))
    hidden, time_pieces = run_time_rest(
        middle_time, grad_time.shape, normed_t, grad_packed_t, attended_t, grad_rows, w_out_time
    )
    hidden, grad_space = lax.optimization_barrier((hidden, grad_space))
    hidden_home = exchange(hidden, "rounds")
    hidden_home = jnp.swapaxes(hidden_home, 0, 1).reshape(grad_hidden.shape)
    grad_packed, pieces = run_space_backward(
        grad_space, normed, packed, attended, exps, totals, w_out_space, time_pieces
    )
    sources = exchange(pieces, ("rounds", "stab"))
    outgoing = run_space_stream(
        grad_space, x, inverse, grad_packed, gain_s, w_qkv_space, stab_parts
    )
    scaling = 1.0 / math.sqrt(parts * rounds_here * stabs_here)
    summed = (jnp.sum(sources.astype(F32), axis=0) * scaling).astype(BF16)
    here = outgoing.shape[1] - summed.shape[0]
    spread = jnp.broadcast_to(summed[None], (stab_parts,) + summed.shape)
    incoming = exchange(lax.dynamic_update_slice(outgoing, spread, (0, here, 0, 0)), "stab")
    grad_embedded = incoming[:, :here].reshape(grad_hidden.shape)
    gathered = incoming[:, here:]
    gathered = exchange(
        jnp.broadcast_to(gathered[None], (round_parts,) + gathered.shape), "rounds"
    )
    weights = call(
        unpack_weights,
        [((features, 3 * features), F32), ((features, features), F32)] * 2,
        (gathered.reshape((parts,) + summed.shape),),
        24,
        3,
    )
    return (hidden_home, grad_embedded) + tuple(weights)


def solution(mesh):
    in_specs = (
        P("rounds", "stab"),
        P("stab"),
        P(None, "stab"),
        P(),
        P(),
        P(),
        P("rounds", None),
        P(),
        P(),
        P(),
        P(),
        P(),
        P(),
        P("rounds", "stab", None),
    )
    out_specs = (P("rounds", "stab", None), P("rounds", "stab", None), P(), P(), P(), P())
    return jax.shard_map(
        on_device, mesh=mesh, in_specs=in_specs, out_specs=out_specs, check_vma=False
    )
```

time: 219 us -> 194 us (0.89)
  blocking collectives: 14.2 us -> 35.2 us
  waiting for transfers between devices: 72.9 us -> 52.6 us
  starting transfers between devices: 53 us -> 35.1 us
  Pallas kernels: 54.1 us -> 37.7 us
  local copies, waits for them, and re-layouts: 17.2 us -> 30.1 us
  other arithmetic: 5.79 us -> 1.43 us
    unnamed x24 -> x69, local copies, waits for them, and re-layouts: 1.64 us -> 26.5 us
    all_to_all x1 -> x2, blocking collectives: 14.2 us -> 35.2 us  [exchange(): return lax.all_to_all(values, axes, split_axis=0, concat_axis=0, tiled=True)]
    all_to_all x9 -> x6, waiting for transfers between devices: 72.9 us -> 52.6 us  [exchange(): return lax.all_to_all(values, axes, split_axis=0, concat_axis=0, tiled=True)]
    all_to_all x9 -> x6, starting transfers between devices: 53 us -> 35.1 us  [exchange(): return lax.all_to_all(values, axes, split_axis=0, concat_axis=0, tiled=True)]
    pallas_call x4 -> x7, Pallas kernels: 54.1 us -> 37.7 us  [call(): pl.pallas_call(kernel, out_shape=[jax.ShapeDtypeStruct(*item) for item in...]
    reshape x7 -> x1, local copies, waits for them, and re-layouts: 6.18 us -> 0.83 us  [on_device(): grad_embedded = incoming[:, :here].reshape(grad_hidden.shape)]
    concatenate x1 -> x0, local copies, waits for them, and re-layouts: 3.82 us -> none  [on_device(): jnp.concatenate([coord_table.reshape(2 * coords, features), basis_table,...]
    reshape x2 -> x0, other arithmetic: 2.58 us -> none  [reduce_to_all(): flat.reshape(parts, flat.shape[0] // parts, flat.shape[1])]
  transfers between devices with their start and end apart: 9 -> 6, of which waited for: 7 -> 5; matrix products, arithmetic and copies ran while one was open for 7% -> 1% of each run, Pallas kernels for 18% -> 6%
where the time goes in v1:
time: 194 us; the launch traced here: 193 us
  waiting for transfers between devices  52.6 us (27%)
  Pallas kernels  37.7 us (19%)
  blocking collectives  35.2 us (18%)
  starting transfers between devices  35.1 us (18%)
  local copies, waits for them, and re-layouts  30.1 us (16%)
    all_to_all x6, waiting for transfers between devices, exchange(): return lax.all_to_all(values, axes, split_axis=0, concat_axis=0, tiled=True)  52.6 us
    pallas_call x7, Pallas kernels, call(): pl.pallas_call(kernel, out_shape=[jax.ShapeDtypeStruct(*item) for item in...  37.7 us
    all_to_all x2, blocking collectives, exchange(): return lax.all_to_all(values, axes, split_axis=0, concat_axis=0, tiled=True)  35.2 us
    all_to_all x6, starting transfers between devices, exchange(): return lax.all_to_all(values, axes, split_axis=0, concat_axis=0, tiled=True)  35.1 us
    unnamed x69, local copies, waits for them, and re-layouts  26.5 us
  transfers between devices with their start and end apart: 6, of which 5 were waited for; matrix products, arithmetic and copies ran while one was open for 1% of the time, Pallas kernels for 6%

profile of v1, /device:TPU:1, one launch (start us, length us, event | category | flops | bytes accessed | tf_op | source)
XLA Modules:
  0.0 193.1 jit_solution(7112214329680481292)
XLA Ops:
  3.4 8.5 %all-to-all-start = ((s32[8,5,128]{2,1,0:T(8,128)}), s32[8,5,128]{2,1,0:T(8,128)S(1)}, u32[]{:S(2)}, u32[]{:S(2)}) async-start(s32[8,5,128]{2,1,0:T(8,128)} %index_kernel.1), calls=%async_computation | async-start | bytes 65536 | tf_op jit(solution)/shard_map/all_to_all | solution.py:454
  12.7 5.8 %all-to-all-done.index_ref = s32[8,5,128]{2,1,0:T(8,128)S(1)} async-done(((s32[8,5,128]{2,1,0:T(8,128)}), s32[8,5,128]{2,1,0:T(8,128)S(1)}, u32[]{:S(2)}, u32[]{:S(2)}) %all-to-all-start) | async-done | bytes 20512 | tf_op jit(solution)/shard_map/all_to_all | solution.py:454
  18.5 6.8 %all-to-all-start.2 = ((bf16[16,8,8,256]{3,2,1,0:T(8,128)(2,1)}), bf16[16,8,8,256]{3,2,1,0:T(8,128)(2,1)S(1)}, u32[]{:S(2)}, u32[]{:S(2)}) async-start(bf16[16,8,8,256]{3,2,1,0:T(8,128)(2,1)} %copy_bitcast_fusion.1), calls=%async_computation.2 | async-start | bytes 1048576 | tf_op jit(solution)/shard_map/all_to_all | solution.py:454
  25.4 9.5 %space_forward.1 = (bf16[128,8,256]{2,1,0:T(8,128)(2,1)S(1)}, bf16[256,1024]{1,0:T(8,128)(2,1)S(1)}, bf16[256,1024]{1,0:T(8,128)(2,1)S(1)}, f32[1,1024]{1,0:T(1,...) custom-call(s32[8,5,128]{2,1,0:T(8,128)S(1)} %all-to-all-done.index_, ...), custom_call_target="tpu_custom_call" | custom-call | flops 5000000000 | bytes 20000000 | tf_op jit(solution)/shard_map/space_forward/pallas_call | solution.py:26
  34.9 3.3 %copy-done.17 = bf16[4,1024,1024]{2,1,0:T(8,128)(2,1)} copy-done((bf16[4,1024,1024]{2,1,0:T(8,128)(2,1)}, bf16[4,1024,1024]{2,1,0:T(8,128)(2,1)S(1)}, u32[]{:S(2)}) %copy-start.17) | copy-done | bytes 8388632
  39.0 1.1 copy-done.27
  41.8 19.5 %all_to_all.40 = bf16[128,8,256]{2,1,0:T(8,128)(2,1)S(1)} all-to-all(bf16[128,8,256]{2,1,0:T(8,128)(2,1)S(1)} %get-tuple-element.32), channel_id=1, replica_groups=mesh['rounds'=16,'stab'=8] {'stab','rounds'}, dimensions={0} | all-to-all | bytes 1048576 | tf_op jit(solution)/shard_map/all_to_all | solution.py:454
  61.4 11.9 %time_block.1 = (bf16[8,16,8,256]{3,2,1,0:T(8,128)(2,1)}, bf16[256,1024]{1,0:T(8,128)(2,1)S(1)}, bf16[768,1024]{1,0:T(8,128)(2,1)S(1)}, bf16[256,1024]{1,0:T(8,128)(2,1)S(1)}, bf16[1024,256]{1,0:T(8,128)(2,1)S(1)}) custom-call(bf16[8,16,8,256]{3,2,1,0:T(8,128)(2,1)S(1)} %bitcast.19, bf16[16,8,8,256]{3,2,1,0:T(8,128)(2,1)S(1)} %all-to-all-done.2.grad_ref, ...), custom_call_target="tpu_custom_call" | custom-call | flops 5000000000 | bytes 20000000 | tf_op jit(solution)/shard_map/time_block/pallas_call | solution.py:26
  73.3 1.1 copy-done.15
  76.8 4.5 %all-to-all-start.3 = ((bf16[128,8,256]{2,1,0:T(8,128)(2,1)}), bf16[128,8,256]{2,1,0:T(8,128)(2,1)S(1)}, u32[]{:S(2)}, u32[]{:S(2)}) async-start(bf16[128,8,256]{2,1,0:T(8,128)(2,1)} %bitcast.6), calls=%async_computation.3 | async-start | bytes 1048576 | tf_op jit(solution)/shard_map/all_to_all | solution.py:454
  81.3 1.4 copy-done.16
  83.8 1.0 copy-done.24
  84.8 1.0 copy-done.26
  85.8 1.7 time_rest.1
  87.6 7.5 %all-to-all-done.3.grad_ref = bf16[128,8,256]{2,1,0:T(8,128)(2,1)S(1)} async-done(((bf16[128,8,256]{2,1,0:T(8,128)(2,1)}), bf16[128,8,256]{2,1,0:T(8,128)(2,1)S(1)}, u32[]{:S(2)}, u32[]{:S(2)}) %all-to-all-start.3) | async-done | bytes 524320 | tf_op jit(solution)/shard_map/all_to_all | solution.py:454
  95.0 3.4 %copy-done.18 = bf16[4,1024,1024]{2,1,0:T(8,128)(2,1)S(1)} copy-done((bf16[4,1024,1024]{2,1,0:T(8,128)(2,1)S(1)}, bf16[4,1024,1024]{2,1,0:T(8,128)(2,1)}, u32[]{:S(2)}) %copy-start.18) | copy-done | bytes 8388632
  98.4 1.4 copy-done.28
  99.8 1.0 copy-done.30
  100.9 1.0 copy-done.32
  101.9 11.5 %space_backward.1 = (bf16[768,1024]{1,0:T(8,128)(2,1)S(1)}, bf16[128,2,8,256]{3,2,1,0:T(8,128)(2,1)}) custom-call(bf16[128,8,256]{2,1,0:T(8,128)(2,1)S(1)} %all-to-all-done.3.grad_ref, bf16[256,1024]{1,0:T(8,128)(2,1)S(1)} %copy-done.30, bf16[768,1024]{1,0:T(8,128)(2,1)S(1)} %copy-done.28, bf16[256,1024]{1,0:T(8,128)(2,1)S(1)} %copy-done.32, ...), custom_call_target="tpu_custom_call" | custom-call | flops 7000000000 | bytes 28000000 | tf_op jit(solution)/shard_map/space_backward/pallas_call | solution.py:26
  113.4 1.2 copy-done.13
  114.6 5.7 %all-to-all-start.5 = ((bf16[128,2,8,256]{3,2,1,0:T(8,128)(2,1)}), bf16[128,2,8,256]{3,2,1,0:T(8,128)(2,1)}, u32[]{:S(2)}, u32[]{:S(2)}) async-start(bf16[128,2,8,256]{3,2,1,0:T(8,128)(2,1)} %get-tuple-element.51), calls=%async_computation.5 | async-start | bytes 2097152 | tf_op jit(solution)/shard_map/all_to_all | solution.py:454
  120.3 1.4 copy-done.14
  122.7 15.1 %all-to-all-done.5 = bf16[128,2,8,256]{3,2,1,0:T(8,128)(2,1)} async-done(((bf16[128,2,8,256]{3,2,1,0:T(8,128)(2,1)}), bf16[128,2,8,256]{3,2,1,0:T(8,128)(2,1)}, u32[]{:S(2)}, u32[]{:S(2)}) %all-to-all-start.5) | async-done | bytes 1048608 | tf_op jit(solution)/shard_map/all_to_all | solution.py:454
  137.8 1.4 convert_reduce_fusion
  139.3 15.6 %all_to_all.41 = bf16[8,18,8,256]{3,2,1,0:T(8,128)(2,1)S(1)} all-to-all(bf16[8,18,8,256]{3,2,1,0:T(8,128)(2,1)S(1)} %broadcast_dynamic-update-slice_fusion), channel_id=1, replica_groups=mesh['rounds'=16,'stab'=8] {'stab'}, dimensions={0} | all-to-all | bytes 1179648 | tf_op jit(solution)/shard_map/all_to_all | solution.py:454
  154.9 5.2 %all-to-all-start.4 = ((bf16[16,8,8,256]{3,2,1,0:T(8,128)(2,1)}), bf16[16,8,8,256]{3,2,1,0:T(8,128)(2,1)S(1)}, u32[]{:S(2)}, u32[]{:S(2)}) async-start(bf16[16,8,8,256]{3,2,1,0:T(8,128)(2,1)} %get-tuple-element.40), calls=%async_computation.4 | async-start | bytes 1048576 | tf_op jit(solution)/shard_map/all_to_all | solution.py:454
  160.1 10.0 %all-to-all-done.4 = bf16[16,8,8,256]{3,2,1,0:T(8,128)(2,1)S(1)} async-done(((bf16[16,8,8,256]{3,2,1,0:T(8,128)(2,1)}), bf16[16,8,8,256]{3,2,1,0:T(8,128)(2,1)S(1)}, u32[]{:S(2)}, u32[]{:S(2)}) %all-to-all-start.4) | async-done | bytes 524320 | tf_op jit(solution)/shard_map/all_to_all | solution.py:454
  170.1 1.1 broadcast_in_dim.5
  171.2 4.5 %all-to-all-start.7 = ((bf16[16,8,2,8,256]{4,3,2,1,0:T(8,128)(2,1)}), bf16[16,8,2,8,256]{4,3,2,1,0:T(8,128)(2,1)S(1)}, u32[]{:S(2)}, u32[]{:S(2)}) async-start(bf16[16,8,2,8,256]{4,3,2,1,0:T(8,128)(2,1)} %broadcast_in_dim.5), calls=%async_computation.7 | async-start | bytes 2097152 | tf_op jit(solution)/shard_map/all_to_all | solution.py:454
  177.4 14.3 %all-to-all-done.7 = bf16[16,8,2,8,256]{4,3,2,1,0:T(8,128)(2,1)S(1)} async-done(((bf16[16,8,2,8,256]{4,3,2,1,0:T(8,128)(2,1)}), bf16[16,8,2,8,256]{4,3,2,1,0:T(8,128)(2,1)S(1)}, u32[]{:S(2)}, u32[]{:S(2)}) %all-to-all-start.7) | async-done | bytes 1048608 | tf_op jit(solution)/shard_map/all_to_all | solution.py:454
  191.7 1.4 unpack_weights.1
  (66 shorter events, 12.2 us)
Async XLA Ops:
  0.6 11.2 %copy-start = (bf16[8,128,256]{2,1,0:T(8,128)(2,1)S(1)}, bf16[8,128,256]{2,1,0:T(8,128)(2,1)}, u32[]{:S(2)}) copy-start(bf16[8,128,256]{2,1,0:T(8,128)(2,1)} %param.27) | copy-start | bytes 1572868
  2.7 22.6 %copy-start.33 = (bf16[2,42,256]{2,0,1:T(2,128)(2,1)S(1)}, bf16[2,42,256]{2,0,1:T(2,128)(2,1)}, u32[]{:S(2)}) copy-start(bf16[2,42,256]{2,0,1:T(2,128)(2,1)} %param.19) | copy-start | bytes 129028
  3.4 22.0 %copy-start.2 = (bf16[256,768]{1,0:T(8,128)(2,1)S(1)}, bf16[256,768]{1,0:T(8,128)(2,1)}, u32[]{:S(2)}) copy-start(bf16[256,768]{1,0:T(8,128)(2,1)} %w_qkv_ref.5) | copy-start | bytes 1179652
  3.4 22.0 %copy-start.4 = (bf16[256,256]{1,0:T(8,128)(2,1)S(1)}, bf16[256,256]{1,0:T(8,128)(2,1)}, u32[]{:S(2)}) copy-start(bf16[256,256]{1,0:T(8,128)(2,1)} %w_out_ref.7) | copy-start | bytes 393220
  3.4 22.0 %copy-start.6 = (bf16[8,256]{1,0:T(8,128)(2,1)S(1)}, bf16[8,256]{1,0:T(8,128)(2,1)}, u32[]{:S(2)}) copy-start(bf16[8,256]{1,0:T(8,128)(2,1)} %round_table_ref.1) | copy-start | bytes 12292
  3.4 22.0 %copy-start.8 = (bf16[2,256]{1,0:T(2,128)(2,1)S(1)}, bf16[2,256]{1,0:T(2,128)(2,1)}, u32[]{:S(2)}) copy-start(bf16[2,256]{1,0:T(2,128)(2,1)} %syndrome_table_ref.1) | copy-start | bytes 3076
  3.4 22.0 %copy-start.9 = (bf16[2,256]{1,0:T(2,128)(2,1)S(1)}, bf16[2,256]{1,0:T(2,128)(2,1)}, u32[]{:S(2)}) copy-start(bf16[2,256]{1,0:T(2,128)(2,1)} %basis_table_ref.1) | copy-start | bytes 3076
  3.4 22.0 %copy-start.11 = (f32[256]{0:T(256)S(1)}, f32[256]{0:T(256)}, u32[]{:S(2)}) copy-start(f32[256]{0:T(256)} %param.21) | copy-start | bytes 3076
  3.4 15.1 %all-to-all-start = ((s32[8,5,128]{2,1,0:T(8,128)}), s32[8,5,128]{2,1,0:T(8,128)S(1)}, u32[]{:S(2)}, u32[]{:S(2)}) async-start(s32[8,5,128]{2,1,0:T(8,128)} %index_kernel.1), calls=%async_computation | async-start | bytes 65536 | tf_op jit(solution)/shard_map/all_to_all | solution.py:454
  18.5 23.3 %all-to-all-start.2 = ((bf16[16,8,8,256]{3,2,1,0:T(8,128)(2,1)}), bf16[16,8,8,256]{3,2,1,0:T(8,128)(2,1)S(1)}, u32[]{:S(2)}, u32[]{:S(2)}) async-start(bf16[16,8,8,256]{3,2,1,0:T(8,128)(2,1)} %copy_bitcast_fusion.1), calls=%async_computation.2 | async-start | bytes 1048576 | tf_op jit(solution)/shard_map/all_to_all | solution.py:454
  25.4 35.9 %copy-start.1 = (bf16[256,768]{1,0:T(8,128)(2,1)S(1)}, bf16[256,768]{1,0:T(8,128)(2,1)}, u32[]{:S(2)}) copy-start(bf16[256,768]{1,0:T(8,128)(2,1)} %w_qkv_ref.4) | copy-start | bytes 1179652
  25.4 35.9 %copy-start.3 = (bf16[256,256]{1,0:T(8,128)(2,1)S(1)}, bf16[256,256]{1,0:T(8,128)(2,1)}, u32[]{:S(2)}) copy-start(bf16[256,256]{1,0:T(8,128)(2,1)} %w_out_ref.6) | copy-start | bytes 393220
  25.4 35.9 %copy-start.10 = (f32[256]{0:T(256)S(1)}, f32[256]{0:T(256)}, u32[]{:S(2)}) copy-start(f32[256]{0:T(256)} %param.24) | copy-start | bytes 3076
  34.9 3.3 %copy-start.17 = (bf16[4,1024,1024]{2,1,0:T(8,128)(2,1)}, bf16[4,1024,1024]{2,1,0:T(8,128)(2,1)S(1)}, u32[]{:S(2)}) copy-start(bf16[4,1024,1024]{2,1,0:T(8,128)(2,1)S(1)} %get-tuple-element.47.exps_ref) | copy-start | bytes 25165828
  39.0 1.1 copy-start.27
  40.2 0.8 copy-start.29
  73.3 1.1 copy-start.15
  76.8 18.2 %all-to-all-start.3 = ((bf16[128,8,256]{2,1,0:T(8,128)(2,1)}), bf16[128,8,256]{2,1,0:T(8,128)(2,1)S(1)}, u32[]{:S(2)}, u32[]{:S(2)}) async-start(bf16[128,8,256]{2,1,0:T(8,128)(2,1)} %bitcast.6), calls=%async_computation.3 | async-start | bytes 1048576 | tf_op jit(solution)/shard_map/all_to_all | solution.py:454
  81.3 1.4 copy-start.16
  82.7 1.0 copy-start.22
  83.8 1.0 copy-start.24
  84.8 1.0 copy-start.26
  95.0 3.4 %copy-start.18 = (bf16[4,1024,1024]{2,1,0:T(8,128)(2,1)S(1)}, bf16[4,1024,1024]{2,1,0:T(8,128)(2,1)}, u32[]{:S(2)}) copy-start(bf16[4,1024,1024]{2,1,0:T(8,128)(2,1)} %copy-done.17) | copy-start | bytes 25165828
  98.4 1.4 copy-start.28
  99.8 1.0 copy-start.30
  100.9 1.0 copy-start.32
  113.4 1.2 copy-start.13
  114.6 5.7 %copy-start.20 = (bf16[256,1024]{1,0:T(8,128)(2,1)S(1)}, bf16[256,1024]{1,0:T(8,128)(2,1)}, u32[]{:S(2)}) copy-start(bf16[256,1024]{1,0:T(8,128)(2,1)} %copy-done.19) | copy-start | bytes 1572868
  114.6 23.3 %all-to-all-start.5 = ((bf16[128,2,8,256]{3,2,1,0:T(8,128)(2,1)}), bf16[128,2,8,256]{3,2,1,0:T(8,128)(2,1)}, u32[]{:S(2)}, u32[]{:S(2)}) async-start(bf16[128,2,8,256]{3,2,1,0:T(8,128)(2,1)} %get-tuple-element.51), calls=%async_computation.5 | async-start | bytes 2097152 | tf_op jit(solution)/shard_map/all_to_all | solution.py:454
  120.2 1.4 copy-start.14
  154.9 15.2 %all-to-all-start.4 = ((bf16[16,8,8,256]{3,2,1,0:T(8,128)(2,1)}), bf16[16,8,8,256]{3,2,1,0:T(8,128)(2,1)S(1)}, u32[]{:S(2)}, u32[]{:S(2)}) async-start(bf16[16,8,8,256]{3,2,1,0:T(8,128)(2,1)} %get-tuple-element.40), calls=%async_computation.4 | async-start | bytes 1048576 | tf_op jit(solution)/shard_map/all_to_all | solution.py:454
  171.2 20.5 %all-to-all-start.7 = ((bf16[16,8,2,8,256]{4,3,2,1,0:T(8,128)(2,1)}), bf16[16,8,2,8,256]{4,3,2,1,0:T(8,128)(2,1)S(1)}, u32[]{:S(2)}, u32[]{:S(2)}) async-start(bf16[16,8,2,8,256]{4,3,2,1,0:T(8,128)(2,1)} %broadcast_in_dim.5), calls=%async_computation.7 | async-start | bytes 2097152 | tf_op jit(solution)/shard_map/all_to_all | solution.py:454
  (8 other events, 6.1 us)

commit v2 on v1

--- a/solution.py
+++ b/solution.py
@@ -9,6 +9,7 @@
 
 HEADS = 4
 EPSILON = 1e-06
+VMEM_BYTES = 60 * 2**20
 F32 = jnp.float32
 BF16 = jnp.bfloat16
 
@@ -22,12 +23,12 @@
     )
 
 
-def call(kernel, shapes, arguments, megabytes, microseconds, scratch=(), **grid):
+def call(kernel, shapes, arguments, microseconds, scratch=(), **grid):
     return pl.pallas_call(
         kernel,
         out_shape=[jax.ShapeDtypeStruct(*item) for item in shapes],
         scratch_shapes=[pltpu.VMEM(*item) for item in scratch],
-        compiler_params=pltpu.CompilerParams(vmem_limit_bytes=megabytes * 2**20),
+        compiler_params=pltpu.CompilerParams(vmem_limit_bytes=VMEM_BYTES),
         cost_estimate=pl.CostEstimate(
             flops=microseconds * 500_000_000,
             bytes_accessed=microseconds * 2_000_000,
@@ -170,7 +171,6 @@
         space_forward,
         shapes,
         arguments,
-        32,
         10,
         scratch=[
             ((LEVELS, features), F32),
@@ -184,10 +184,37 @@
     )
 
 
+def time_grad(grad_ref, w_out_ref, grad_row_ref, grad_attended_ref, grads_ref):
+    round_parts, stab_parts, stabs, features = grad_ref.shape
+    rounds = stab_parts * round_parts
+    grad = grad_ref[...].astype(F32).reshape(rounds * stabs, features)
+    lanes = grads_ref.shape[2]
+    for part in range(features // lanes):
+        half = slice(part * lanes, (part + 1) * lanes)
+        grads_ref[part] = grad[:, half]
+        for stab in range(stabs):
+            cols = slice(stab * rounds, (stab + 1) * rounds)
+            at = pl.ds(stab, rounds, stride=stabs)
+            grad_row_ref[cols, half] = grads_ref[part, at, :].astype(BF16)
+    grad_attended_ref[...] = dot(w_out_ref[...], grad_row_ref[...], 1, 1).astype(BF16)
+
+
+def run_time_grad(grad, w_out):
+    round_parts, stab_parts, stabs, features = grad.shape
+    tokens = stab_parts * round_parts * stabs
+    return call(
+        time_grad,
+        [((tokens, features), BF16), ((features, tokens), BF16)],
+        (grad, w_out),
+        3,
+        scratch=[((features // 128, tokens, 128), F32)],
+    )
+
+
 def time_block(
-    middle_ref, grad_ref, gain_ref, w_qkv_ref, w_out_ref,
-    grad_middle_ref, normed_ref, grad_packed_ref, attended_ref, grad_row_ref,
-    x_ref, inverse_ref, packed_ref, grad_attended_ref, rows_ref, grads_ref,
+    middle_ref, grad_ref, grad_attended_ref, gain_ref, w_qkv_ref,
+    grad_middle_ref, normed_ref, grad_packed_ref, attended_ref,
+    x_ref, inverse_ref, packed_ref, rows_ref,
 ):
     stab_parts, round_parts, stabs, features = middle_ref.shape
     rounds = stab_parts * round_parts
@@ -196,18 +223,15 @@
     scale = depth**-0.5
 
     middle = jnp.swapaxes(middle_ref[...].astype(F32), 0, 1).reshape(tokens, features)
-    grad = grad_ref[...].astype(F32).reshape(tokens, features)
     lanes = rows_ref.shape[2]
     halves = [slice(part * lanes, (part + 1) * lanes) for part in range(features // lanes)]
     for part, half in enumerate(halves):
         rows_ref[part] = middle[:, half]
-        grads_ref[part] = grad[:, half]
     for stab in range(stabs):
         cols = slice(stab * rounds, (stab + 1) * rounds)
         at = pl.ds(stab, rounds, stride=stabs)
         for part, half in enumerate(halves):
             x_ref[half, cols] = rows_ref[part, at, :].T
-            grad_row_ref[cols, half] = grads_ref[part, at, :].astype(BF16)
     x = x_ref[...]
     gain = as_column(gain_ref[...])
     normed, inverse = norm_columns(x, gain)
@@ -217,7 +241,6 @@
     to_base_two = math.log2(math.e) * scale
     packed_ref[:features, :] = (packed[:features] * to_base_two).astype(BF16)
     packed_ref[features:, :] = packed[features:].astype(BF16)
-    grad_attended_ref[...] = dot(w_out_ref[...], grad_row_ref[...], 1, 1).astype(BF16)
 
     def one_stab(stab, carry):
         cols = pl.ds(pl.multiple_of(stab * rounds, rounds), rounds)
@@ -254,16 +277,17 @@
         cols = slice(stab * rounds, (stab + 1) * rounds)
         at = pl.ds(stab, rounds, stride=stabs)
         for part, half in enumerate(halves):
-            grads_ref[part, at, :] = grads_ref[part, at, :] + grad_stream[half, cols].T
+            rows_ref[part, at, :] = grad_stream[half, cols].T
     for part, half in enumerate(halves):
-        grad_middle = grads_ref[part].reshape(round_parts, stab_parts, stabs, lanes)
+        grad_middle = rows_ref[part].reshape(round_parts, stab_parts, stabs, lanes)
+        grad_middle = grad_middle + grad_ref[:, :, :, half].astype(F32)
         grad_middle_ref[:, :, :, half] = jnp.swapaxes(grad_middle, 0, 1).astype(BF16)
 
 
 TIME_UNROLL = 2
 
 
-def run_time_block(middle, grad, gain, w_qkv, w_out):
+def run_time_block(middle, grad, grad_attended, gain, w_qkv):
     stab_parts, round_parts, stabs, features = middle.shape
     tokens = stab_parts * round_parts * stabs
     shapes = [
@@ -271,20 +295,16 @@
         ((features, tokens), BF16),
         ((3 * features, tokens), BF16),
         ((features, tokens), BF16),
-        ((tokens, features), BF16),
     ]
     return call(
         time_block,
         shapes,
-        (middle, grad, gain, w_qkv, w_out),
-        24,
+        (middle, grad, grad_attended, gain, w_qkv),
         10,
         scratch=[
             ((features, tokens), F32),
             ((1, tokens), F32),
             ((3 * features, tokens), BF16),
-            ((features, tokens), BF16),
-            ((features // 128, tokens, 128), F32),
             ((features // 128, tokens, 128), F32),
         ],
     )
@@ -311,8 +331,10 @@
         for part, half in enumerate(halves):
             rows_ref[part, at, :] = rows_ref[part, at, :] + branch[cols, half]
     for part, half in enumerate(halves):
-        hidden = rows_ref[part].reshape(hidden_ref.shape[:3] + (lanes,))
-        hidden_ref[:, :, :, half] = hidden.astype(BF16)
+        hidden = rows_ref[part].reshape(round_parts, stab_parts, stabs, lanes)
+        hidden_ref[:, :stab_parts, :, half] = hidden.astype(BF16)
+    groups = hidden_ref.shape[1] - stab_parts
+    hidden_ref[:, stab_parts:] = jnp.zeros((round_parts, groups, stabs, features), BF16)
     store_blocks(
         pieces_ref,
         0,
@@ -321,14 +343,17 @@
     )
 
 
-def run_time_rest(middle, grad_shape, normed, grad_packed, attended, grad_rows, w_out):
+def run_time_rest(middle, normed, grad_packed, attended, grad_rows, w_out):
     features, tokens = normed.shape
-    parts = middle.shape[0] * middle.shape[1]
+    stab_parts, round_parts, stabs, _ = middle.shape
+    parts = stab_parts * round_parts
     return call(
         time_rest,
-        [(grad_shape, BF16), ((parts, 1, 4 * features // parts, features), BF16)],
+        [
+            ((round_parts, 3 * stab_parts, stabs, features), BF16),
+            ((parts, 1, 4 * features // parts, features), BF16),
+        ],
         (middle, normed, grad_packed, attended, grad_rows, w_out),
-        24,
         5,
         scratch=[((features // 128, tokens, 128), F32)],
     )
@@ -398,7 +423,6 @@
         space_backward,
         shapes,
         arguments,
-        32,
         14,
         scratch=[((features, tokens), BF16), ((tokens, tokens), BF16)],
         grid=(HEADS,),
@@ -430,24 +454,31 @@
         space_stream,
         [((parts, tokens // (parts * rows) + 2, rows, features), BF16)],
         (grad, x, inverse, grad_packed, gain, w_qkv),
-        24,
         4,
     )[0]
 
 
-def unpack_weights(pieces_ref, space_qkv_ref, space_out_ref, time_qkv_ref, time_out_ref):
-    features = space_out_ref.shape[0]
-    count = pieces_ref.shape[0] // 4
-    for kind, qkv_ref, out_ref in (
-        (0, time_qkv_ref, time_out_ref),
-        (1, space_qkv_ref, space_out_ref),
-    ):
-        for j in range(4):
-            block = pieces_ref[j * count : (j + 1) * count, kind].reshape(features, features)
+def unpack(
+    incoming_ref, hidden_ref, space_qkv_ref, space_out_ref, time_qkv_ref, time_out_ref
+):
+    round_parts, _, stabs, features = incoming_ref.shape
+    here = hidden_ref.shape[0]
+    for block in range(round_parts):
+        cols = slice(block * stabs, (block + 1) * stabs)
+        hidden_ref[:, cols, :] = incoming_ref[block, :here]
+    count = round_parts // 4
+    for j in range(4):
+        pieces = incoming_ref[j * count : (j + 1) * count, here:].astype(F32)
+        pieces = pieces.reshape(count, here, 2, stabs, features)
+        for kind, qkv_ref, out_ref in (
+            (0, time_qkv_ref, time_out_ref),
+            (1, space_qkv_ref, space_out_ref),
+        ):
+            block = pieces[:, :, kind].reshape(features, features)
             if j < 3:
-                qkv_ref[:, j * features : (j + 1) * features] = block.astype(F32)
+                qkv_ref[:, j * features : (j + 1) * features] = block
             else:
-                out_ref[...] = block.astype(F32)
+                out_ref[...] = block
 
 
 def exchange(values, axes):
@@ -480,7 +511,6 @@
         index_kernel,
         [((stab_parts, 5, stabs_here), jnp.int32)],
         (syndrome, basis_ids.reshape(1, stabs_here), coordinates),
-        4,
         1,
     )[0]
     index = exchange(own_index, "stab")
@@ -494,18 +524,17 @@
     middle, x, normed, inverse, packed, attended, exps, totals = run_space_forward(
         index, tables, gain_s, w_qkv_space, w_out_space, parts
     )
+    middle, grad_time = lax.optimization_barrier((middle, grad_time))
     middle_time = exchange(middle, ("stab", "rounds"))
     middle_time = middle_time.reshape(stab_parts, round_parts, stabs_time, features)
-    grad_middle, normed_t, grad_packed_t, attended_t, grad_rows = run_time_block(
-        middle_time, grad_time, gain_t, w_qkv_time, w_out_time
+    grad_rows, grad_attended_t = run_time_grad(grad_time, w_out_time)
+    grad_middle, normed_t, grad_packed_t, attended_t = run_time_block(
+        middle_time, grad_time, grad_attended_t, gain_t, w_qkv_time
     )
     grad_space = exchange(grad_middle.reshape(parts, stabs_time, features), ("stab", "rounds"))
     hidden, time_pieces = run_time_rest(
-        middle_time, grad_time.shape, normed_t, grad_packed_t, attended_t, grad_rows, w_out_time
-    )
-    hidden, grad_space = lax.optimization_barrier((hidden, grad_space))
-    hidden_home = exchange(hidden, "rounds")
-    hidden_home = jnp.swapaxes(hidden_home, 0, 1).reshape(grad_hidden.shape)
+        middle_time, normed_t, grad_packed_t, attended_t, grad_rows, w_out_time
+    )
     grad_packed, pieces = run_space_backward(
         grad_space, normed, packed, attended, exps, totals, w_out_space, time_pieces
     )
@@ -519,15 +548,14 @@
     spread = jnp.broadcast_to(summed[None], (stab_parts,) + summed.shape)
     incoming = exchange(lax.dynamic_update_slice(outgoing, spread, (0, here, 0, 0)), "stab")
     grad_embedded = incoming[:, :here].reshape(grad_hidden.shape)
-    gathered = incoming[:, here:]
-    gathered = exchange(
-        jnp.broadcast_to(gathered[None], (round_parts,) + gathered.shape), "rounds"
-    )
-    weights = call(
-        unpack_weights,
-        [((features, 3 * features), F32), ((features, features), F32)] * 2,
-        (gathered.reshape((parts,) + summed.shape),),
-        24,
+    gathered = incoming[:, here:].reshape(1, 2 * stab_parts, stabs_time, features)
+    spread = jnp.broadcast_to(gathered, (round_parts,) + gathered.shape[1:])
+    incoming = exchange(lax.dynamic_update_slice(hidden, spread, (0, stab_parts, 0, 0)), "rounds")
+    hidden_home, *weights = call(
+        unpack,
+        [(grad_hidden.shape, BF16)]
+        + [((features, 3 * features), F32), ((features, features), F32)] * 2,
+        (incoming,),
         3,
     )
     return (hidden_home, grad_embedded) + tuple(weights)

time: 194 us -> 177 us (0.912)
  local copies, waits for them, and re-layouts: 30.1 us -> 6.86 us
  blocking collectives: 35.2 us -> 15.8 us
  Pallas kernels: 37.7 us -> 56.2 us
  waiting for transfers between devices: 52.6 us -> 61.2 us
    unnamed x69 -> x15, local copies, waits for them, and re-layouts: 26.5 us -> 3.4 us
    all_to_all x2 -> x1, blocking collectives: 35.2 us -> 15.8 us  [exchange(): return lax.all_to_all(values, axes, split_axis=0, concat_axis=0, tiled=True)]
    pallas_call x7 -> x8, Pallas kernels: 37.7 us -> 56.2 us  [call(): pl.pallas_call(kernel, out_shape=[jax.ShapeDtypeStruct(*item) for item in...]
    all_to_all x6, waiting for transfers between devices: 52.6 us -> 61.2 us  [exchange(): return lax.all_to_all(values, axes, split_axis=0, concat_axis=0, tiled=True)]
  transfers between devices with their start and end apart: 6 -> 6, of which waited for: 5 -> 5; matrix products, arithmetic and copies ran while one was open for 1% -> 1% of each run, Pallas kernels for 6% -> 14%
where the time goes in v2:
time: 177 us
  waiting for transfers between devices  61.2 us (35%)
  Pallas kernels  56.2 us (32%)
  starting transfers between devices  35.5 us (20%)
  blocking collectives  15.8 us (9%)
  local copies, waits for them, and re-layouts  6.86 us (4%)
    all_to_all x6, waiting for transfers between devices, exchange(): return lax.all_to_all(values, axes, split_axis=0, concat_axis=0, tiled=True)  61.2 us
    pallas_call x8, Pallas kernels, call(): pl.pallas_call(kernel, out_shape=[jax.ShapeDtypeStruct(*item) for item in...  56.2 us
    all_to_all x6, starting transfers between devices, exchange(): return lax.all_to_all(values, axes, split_axis=0, concat_axis=0, tiled=True)  35.5 us
    all_to_all x1, blocking collectives, exchange(): return lax.all_to_all(values, axes, split_axis=0, concat_axis=0, tiled=True)  15.8 us
  transfers between devices with their start and end apart: 6, of which 5 were waited for; matrix products, arithmetic and copies ran while one was open for 1% of the time, Pallas kernels for 14%

profile of v2, /device:TPU:1, one launch (start us, length us, event | category | flops | bytes accessed | tf_op | source)
XLA Modules:
  0.0 176.5 jit_solution(15400710173128387646)
XLA Ops:
  0.6 0.0 copy-start
  0.6 0.0 copy-start.5
  0.7 1.4 index_kernel.1
  2.1 8.3 %all-to-all-start = ((s32[8,5,128]{2,1,0:T(8,128)}), s32[8,5,128]{2,1,0:T(8,128)S(1)}, u32[]{:S(2)}, u32[]{:S(2)}) async-start(s32[8,5,128]{2,1,0:T(8,128)} %index_kernel.1), calls=%async_computation | async-start | bytes 65536 | tf_op jit(solution)/shard_map/all_to_all | solution.py:485
  10.4 0.9 copy_bitcast_fusion
  11.3 5.7 %all-to-all-done.index_ref = s32[8,5,128]{2,1,0:T(8,128)S(1)} async-done(((s32[8,5,128]{2,1,0:T(8,128)}), s32[8,5,128]{2,1,0:T(8,128)S(1)}, u32[]{:S(2)}, u32[]{:S(2)}) %all-to-all-start) | async-done | bytes 20512 | tf_op jit(solution)/shard_map/all_to_all | solution.py:485
  17.0 6.8 %all-to-all-start.1 = ((bf16[16,8,8,256]{3,2,1,0:T(8,128)(2,1)}), bf16[16,8,8,256]{3,2,1,0:T(8,128)(2,1)S(1)}, u32[]{:S(2)}, u32[]{:S(2)}) async-start(bf16[16,8,8,256]{3,2,1,0:T(8,128)(2,1)} %copy_bitcast_fusion), calls=%async_computation.1 | async-start | bytes 1048576 | tf_op jit(solution)/shard_map/all_to_all | solution.py:485
  23.8 0.6 copy.22.coord_table_ref
  24.5 13.4 %space_forward.1 = (bf16[128,8,256]{2,1,0:T(8,128)(2,1)}, bf16[256,1024]{1,0:T(8,128)(2,1)}, bf16[256,1024]{1,0:T(8,128)(2,1)}, f32[1,1024]{1,0:T(1,128)}, bf16[...) custom-call(s32[8,5,128]{2,1,0:T(8,128)} %copy-done.6, ...), custom_call_target="tpu_custom_call" | custom-call | flops 5000000000 | bytes 20000000 | tf_op jit(solution)/shard_map/space_forward/pallas_call | solution.py:27
  37.9 0.0 all-to-all-done.1.grad_ref
  37.9 6.0 %all-to-all-start.2 = ((bf16[128,8,256]{2,1,0:T(8,128)(2,1)}), bf16[128,8,256]{2,1,0:T(8,128)(2,1)S(1)}, u32[]{:S(2)}, u32[]{:S(2)}) async-start(bf16[128,8,256]{2,1,0:T(8,128)(2,1)} %get-tuple-element.36), calls=%async_computation.2 | async-start | bytes 1048576 | tf_op jit(solution)/shard_map/all_to_all | solution.py:485
  43.9 2.5 %time_grad.1 = (bf16[1024,256]{1,0:T(8,128)(2,1)}, bf16[256,1024]{1,0:T(8,128)(2,1)}) custom-call(bf16[16,8,8,256]{3,2,1,0:T(8,128)(2,1)} %copy-done.2, bf16[256,256]{1,0:T(8,128)(2,1)} %w_out_ref.6), custom_call_target="tpu_custom_call" | custom-call | flops 1500000000 | bytes 6000000 | tf_op jit(solution)/shard_map/time_grad/pallas_call | solution.py:27
  46.4 11.3 %all-to-all-done.2 = bf16[128,8,256]{2,1,0:T(8,128)(2,1)S(1)} async-done(((bf16[128,8,256]{2,1,0:T(8,128)(2,1)}), bf16[128,8,256]{2,1,0:T(8,128)(2,1)S(1)}, u32[]{:S(2)}, u32[]{:S(2)}) %all-to-all-start.2) | async-done | bytes 524320 | tf_op jit(solution)/shard_map/all_to_all | solution.py:485
  57.6 0.8 copy-done.4
  58.4 13.0 %time_block.1 = (bf16[8,16,8,256]{3,2,1,0:T(8,128)(2,1)}, bf16[256,1024]{1,0:T(8,128)(2,1)}, bf16[768,1024]{1,0:T(8,128)(2,1)}, bf16[256,1024]{1,0:T(8,128)(2,1)}) custom-call(bf16[8,16,8,256]{3,2,1,0:T(8,128)(2,1)} %bitcast.13, bf16[16,8,8,256]{3,2,1,0:T(8,128)(2,1)} %copy-done.2, bf16[256,1024]{1,0:T(8,128)(2,1)} %get-tuple-element.38.grad_attended_ref, ...), custom_call_target="tpu_custom_call" | custom-call | flops 5000000000 | bytes 20000000 | tf_op jit(solution)/shard_map/time_block/pallas_call | solution.py:27
  71.4 4.5 %all-to-all-start.3 = ((bf16[128,8,256]{2,1,0:T(8,128)(2,1)}), bf16[128,8,256]{2,1,0:T(8,128)(2,1)S(1)}, u32[]{:S(2)}, u32[]{:S(2)}) async-start(bf16[128,8,256]{2,1,0:T(8,128)(2,1)} %bitcast.15), calls=%async_computation.3 | async-start | bytes 1048576 | tf_op jit(solution)/shard_map/all_to_all | solution.py:485
  76.0 4.5 %time_rest.1 = (bf16[16,24,8,256]{3,2,1,0:T(8,128)(2,1)}, bf16[128,1,8,256]{3,2,1,0:T(8,128)(2,1)}) custom-call(bf16[8,16,8,256]{3,2,1,0:T(8,128)(2,1)} %bitcast.14, bf16[256,1024]{1,0:T(8,128)(2,1)} %get-tuple-element.39.normed_ref, bf16[768,1024]{1,0:T(8,128)(2,1)} %get-tuple-element.40.grad_packed_ref, bf16[256,1024]{1,0:T(8,128)(2,1)} %get-tuple-element.41.attended_ref, ...), custom_call_target="tpu_custom_call" | custom-call | flops 2500000000 | bytes 10000000 | tf_op jit(solution)/shard_map/time_rest/pallas_call | solution.py:27
  80.4 9.3 %all-to-all-done.3.grad_ref = bf16[128,8,256]{2,1,0:T(8,128)(2,1)S(1)} async-done(((bf16[128,8,256]{2,1,0:T(8,128)(2,1)}), bf16[128,8,256]{2,1,0:T(8,128)(2,1)S(1)}, u32[]{:S(2)}, u32[]{:S(2)}) %all-to-all-start.3) | async-done | bytes 524320 | tf_op jit(solution)/shard_map/all_to_all | solution.py:485
  89.7 0.8 copy-done.3
  90.5 14.9 %space_backward.1 = (bf16[768,1024]{1,0:T(8,128)(2,1)}, bf16[128,2,8,256]{3,2,1,0:T(8,128)(2,1)}) custom-call(bf16[128,8,256]{2,1,0:T(8,128)(2,1)} %copy-done.3, bf16[256,1024]{1,0:T(8,128)(2,1)} %get-tuple-element.47.normed_ref, bf16[768,1024]{1,0:T(8,128)(2,1)} %get-tuple-element.48.packed_ref, bf16[256,1024]{1,0:T(8,128)(2,1)} %get-tuple-element.49.attended_ref, ...), custom_call_target="tpu_custom_call" | custom-call | flops 7000000000 | bytes 28000000 | tf_op jit(solution)/shard_map/space_backward/pallas_call | solution.py:27
  105.3 4.5 %all-to-all-start.4 = ((bf16[128,2,8,256]{3,2,1,0:T(8,128)(2,1)}), bf16[128,2,8,256]{3,2,1,0:T(8,128)(2,1)S(1)}, u32[]{:S(2)}, u32[]{:S(2)}) async-start(bf16[128,2,8,256]{3,2,1,0:T(8,128)(2,1)} %get-tuple-element.54), calls=%async_computation.4 | async-start | bytes 2097152 | tf_op jit(solution)/shard_map/all_to_all | solution.py:485
  109.9 3.6 %space_stream.1 = bf16[8,18,8,256]{3,2,1,0:T(8,128)(2,1)} custom-call(bf16[128,8,256]{2,1,0:T(8,128)(2,1)} %copy-done.3, bf16[256,1024]{1,0:T(8,128)(2,1)} %get-tuple-element.45.x_ref, f32[1,1024]{1,0:T(1,128)} %get-tuple-element.46.inverse_ref, bf16[768,1024]{1,0:T(8,128)(2,1)} %get-tuple-element.53.grad_packed_ref, f32[1,256]{1,0:T(1,128)} %bitcast.19, ...), custom_call_target="tpu_custom_call" | custom-call | flops 2000000000 | bytes 8000000 | tf_op jit(solution)/shard_map/space_stream/pallas_call | solution.py:27
  113.5 14.2 %all-to-all-done.4 = bf16[128,2,8,256]{3,2,1,0:T(8,128)(2,1)S(1)} async-done(((bf16[128,2,8,256]{3,2,1,0:T(8,128)(2,1)}), bf16[128,2,8,256]{3,2,1,0:T(8,128)(2,1)S(1)}, u32[]{:S(2)}, u32[]{:S(2)}) %all-to-all-start.4) | async-done | bytes 1048608 | tf_op jit(solution)/shard_map/all_to_all | solution.py:485
  127.7 0.2 convert_reduce_fusion
  127.9 0.6 broadcast_dynamic-update-slice_fusion.1
  128.5 15.8 %all_to_all.35 = bf16[8,18,8,256]{3,2,1,0:T(8,128)(2,1)S(1)} all-to-all(bf16[8,18,8,256]{3,2,1,0:T(8,128)(2,1)} %broadcast_dynamic-update-slice_fusion.1), channel_id=1, replica_groups=mesh['rounds'=16,'stab'=8] {'stab'}, dimensions={0} | all-to-all | bytes 1179648 | tf_op jit(solution)/shard_map/all_to_all | solution.py:485
  144.4 1.1 broadcast_dynamic-update-slice_fusion
  145.5 5.3 %all-to-all-start.6 = ((bf16[16,24,8,256]{3,2,1,0:T(8,128)(2,1)}), bf16[16,24,8,256]{3,2,1,0:T(8,128)(2,1)S(1)}, u32[]{:S(2)}, u32[]{:S(2)}) async-start(bf16[16,24,8,256]{3,2,1,0:T(8,128)(2,1)} %broadcast_dynamic-update-slice_fusion), calls=%async_computation.6 | async-start | bytes 3145728 | tf_op jit(solution)/shard_map/all_to_all | solution.py:485
  150.8 0.8 slice_bitcast_fusion
  151.6 20.7 %all-to-all-done.6.incoming_ref = bf16[16,24,8,256]{3,2,1,0:T(8,128)(2,1)S(1)} async-done(((bf16[16,24,8,256]{3,2,1,0:T(8,128)(2,1)}), bf16[16,24,8,256]{3,2,1,0:T(8,128)(2,1)S(1)}, u32[]{:S(2)}, u32[]{:S(2)}) %all-to-all-start.6) | async-done | bytes 1572896 | tf_op jit(solution)/shard_map/all_to_all | solution.py:485
  172.4 1.2 copy-done.1
  173.5 3.0 %unpack.1 = (bf16[8,128,256]{2,1,0:T(8,128)(2,1)}, f32[256,768]{1,0:T(8,128)}, f32[256,256]{1,0:T(8,128)}, f32[256,768]{1,0:T(8,128)}, f32[256,256]{1,0:T(8,128)}) custom-call(bf16[16,24,8,256]{3,2,1,0:T(8,128)(2,1)} %copy-done.1), custom_call_target="tpu_custom_call" | custom-call | flops 1500000000 | bytes 6000000 | tf_op jit(solution)/shard_map/unpack/pallas_call | solution.py:27
  (11 shorter events, 0.0 us)
Async XLA Ops:
  0.6 9.8 %copy-start = (bf16[8,128,256]{2,1,0:T(8,128)(2,1)S(1)}, bf16[8,128,256]{2,1,0:T(8,128)(2,1)}, u32[]{:S(2)}) copy-start(bf16[8,128,256]{2,1,0:T(8,128)(2,1)} %param.27) | copy-start | bytes 1572868
  0.6 23.2 %copy-start.5 = (bf16[2,42,256]{2,0,1:T(2,128)(2,1)S(1)}, bf16[2,42,256]{2,0,1:T(2,128)(2,1)}, u32[]{:S(2)}) copy-start(bf16[2,42,256]{2,0,1:T(2,128)(2,1)} %param.19) | copy-start | bytes 129028
  2.1 14.9 %all-to-all-start = ((s32[8,5,128]{2,1,0:T(8,128)}), s32[8,5,128]{2,1,0:T(8,128)S(1)}, u32[]{:S(2)}, u32[]{:S(2)}) async-start(s32[8,5,128]{2,1,0:T(8,128)} %index_kernel.1), calls=%async_computation | async-start | bytes 65536 | tf_op jit(solution)/shard_map/all_to_all | solution.py:485
  17.0 7.5 %copy-start.6 = (s32[8,5,128]{2,1,0:T(8,128)}, s32[8,5,128]{2,1,0:T(8,128)S(1)}, u32[]{:S(2)}) copy-start(s32[8,5,128]{2,1,0:T(8,128)S(1)} %all-to-all-done.index_ref) | copy-start | bytes 61444
  17.0 20.9 %all-to-all-start.1 = ((bf16[16,8,8,256]{3,2,1,0:T(8,128)(2,1)}), bf16[16,8,8,256]{3,2,1,0:T(8,128)(2,1)S(1)}, u32[]{:S(2)}, u32[]{:S(2)}) async-start(bf16[16,8,8,256]{3,2,1,0:T(8,128)(2,1)} %copy_bitcast_fusion), calls=%async_computation.1 | async-start | bytes 1048576 | tf_op jit(solution)/shard_map/all_to_all | solution.py:485
  37.9 6.0 %copy-start.2 = (bf16[16,8,8,256]{3,2,1,0:T(8,128)(2,1)}, bf16[16,8,8,256]{3,2,1,0:T(8,128)(2,1)S(1)}, u32[]{:S(2)}) copy-start(bf16[16,8,8,256]{3,2,1,0:T(8,128)(2,1)S(1)} %all-to-all-done.1.grad_ref) | copy-start | bytes 1572868
  37.9 19.7 %all-to-all-start.2 = ((bf16[128,8,256]{2,1,0:T(8,128)(2,1)}), bf16[128,8,256]{2,1,0:T(8,128)(2,1)S(1)}, u32[]{:S(2)}, u32[]{:S(2)}) async-start(bf16[128,8,256]{2,1,0:T(8,128)(2,1)} %get-tuple-element.36), calls=%async_computation.2 | async-start | bytes 1048576 | tf_op jit(solution)/shard_map/all_to_all | solution.py:485
  57.6 0.8 copy-start.4
  71.4 18.2 %all-to-all-start.3 = ((bf16[128,8,256]{2,1,0:T(8,128)(2,1)}), bf16[128,8,256]{2,1,0:T(8,128)(2,1)S(1)}, u32[]{:S(2)}, u32[]{:S(2)}) async-start(bf16[128,8,256]{2,1,0:T(8,128)(2,1)} %bitcast.15), calls=%async_computation.3 | async-start | bytes 1048576 | tf_op jit(solution)/shard_map/all_to_all | solution.py:485
  89.7 0.8 copy-start.3
  105.3 22.3 %all-to-all-start.4 = ((bf16[128,2,8,256]{3,2,1,0:T(8,128)(2,1)}), bf16[128,2,8,256]{3,2,1,0:T(8,128)(2,1)S(1)}, u32[]{:S(2)}, u32[]{:S(2)}) async-start(bf16[128,2,8,256]{3,2,1,0:T(8,128)(2,1)} %get-tuple-element.54), calls=%async_computation.4 | async-start | bytes 2097152 | tf_op jit(solution)/shard_map/all_to_all | solution.py:485
  145.5 26.9 %all-to-all-start.6 = ((bf16[16,24,8,256]{3,2,1,0:T(8,128)(2,1)}), bf16[16,24,8,256]{3,2,1,0:T(8,128)(2,1)S(1)}, u32[]{:S(2)}, u32[]{:S(2)}) async-start(bf16[16,24,8,256]{3,2,1,0:T(8,128)(2,1)} %broadcast_dynamic-update-slice_fusion), calls=%async_computation.6 | async-start | bytes 3145728 | tf_op jit(solution)/shard_map/all_to_all | solution.py:485
  172.4 1.2 copy-start.1

commit v3 on v2

--- a/solution.py
+++ b/solution.py
@@ -9,7 +9,7 @@
 
 HEADS = 4
 EPSILON = 1e-06
-VMEM_BYTES = 60 * 2**20
+VMEM_BYTES = 20 * 2**20
 F32 = jnp.float32
 BF16 = jnp.bfloat16
 
@@ -26,8 +26,10 @@
 def call(kernel, shapes, arguments, microseconds, scratch=(), **grid):
     return pl.pallas_call(
         kernel,
-        out_shape=[jax.ShapeDtypeStruct(*item) for item in shapes],
-        scratch_shapes=[pltpu.VMEM(*item) for item in scratch],
+        out_shape=[
+            jax.ShapeDtypeStruct(*item) if isinstance(item, tuple) else item for item in shapes
+        ],
+        scratch_shapes=[pltpu.VMEM(*item) if isinstance(item, tuple) else item for item in scratch],
         compiler_params=pltpu.CompilerParams(vmem_limit_bytes=VMEM_BYTES),
         cost_estimate=pl.CostEstimate(
             flops=microseconds * 500_000_000,
@@ -39,12 +41,22 @@
     )(*arguments)
 
 
-def whole(shape):
-    return pl.BlockSpec(shape, lambda *_: (0,) * len(shape))
-
-
-def per_head(shape):
-    return pl.BlockSpec((1,) + shape[1:], lambda head: (head,) + (0,) * (len(shape) - 1))
+def in_vmem(*arrays):
+    return [pltpu.with_memory_space_constraint(array, pltpu.VMEM) for array in arrays]
+
+
+def in_range(inverse_totals):
+    least, most = jnp.min(inverse_totals), jnp.max(inverse_totals)
+    return jnp.logical_and(least > 2.0**-30, most < 2.0**30)
+
+
+def split_rows(row):
+    terms = []
+    for _ in range(3):
+        terms.append(row.astype(BF16))
+        row = row - terms[-1].astype(F32)
+    zeros = jnp.zeros((16 - len(terms), row.shape[1]), BF16)
+    return jnp.concatenate(terms + [zeros])
 
 
 def as_column(gain):
@@ -85,72 +97,86 @@
 def space_forward(
     index_ref, syndrome_table_ref, basis_table_ref, coord_table_ref, round_table_ref,
     gain_ref, w_qkv_ref, w_out_ref,
-    middle_ref, x_ref, normed_ref, inverse_ref, packed_ref, attended_ref, exps_ref, total_ref,
+    middle_ref, inverse_ref, attended_ref, total_ref, x_ref, normed_ref, packed_ref, exps_ref,
     table_ref, row_ref, onehot_ref,
 ):
-    head = pl.program_id(0)
     features, tokens = x_ref.shape
     depth = features // HEADS
-
-    @pl.when(head == 0)
+    coords = coord_table_ref.shape[1]
+    table_ref[...] = jnp.zeros(table_ref.shape, F32)
+    table_ref[ROW_AT : ROW_AT + coords, :] = coord_table_ref[0].astype(F32)
+    table_ref[COLUMN_AT : COLUMN_AT + coords, :] = coord_table_ref[1].astype(F32)
+    table_ref[BASIS_AT : BASIS_AT + 2, :] = basis_table_ref[...].astype(F32)
+    table_ref[SYNDROME_AT : SYNDROME_AT + 2, :] = syndrome_table_ref[...].astype(F32)
+    rounds = round_table_ref.shape[0]
+    table_ref[ROUND_AT : ROUND_AT + rounds, :] = round_table_ref[...].astype(F32)
+    width = index_ref.shape[2]
+    levels = lax.broadcasted_iota(jnp.int32, (LEVELS, width), 0)
+    for block in range(index_ref.shape[0]):
+        hit = levels == index_ref[block, 0:1, :]
+        for kind in range(1, index_ref.shape[1]):
+            hit = hit | (levels == index_ref[block, kind : kind + 1, :])
+        onehot_ref[:, block * width : (block + 1) * width] = hit.astype(F32).astype(BF16)
+    table = table_ref[...].astype(BF16)
+    x = dot(table, onehot_ref[...], 0, 0).astype(BF16)
+    x_ref[...] = x
+    normed, inverse = norm_columns(x.astype(F32), as_column(gain_ref[...]))
+    normed_ref[...] = normed
+    inverse_ref[...] = inverse
+    packed = dot(w_qkv_ref[...], normed, 0, 0)
+    packed_ref[:features, :] = (packed[:features] * (math.log2(math.e) * depth**-0.5)).astype(BF16)
+    packed_ref[features:, :] = packed[features:].astype(BF16)
+    row_ref[...] = dot(onehot_ref[...], table, 0, 0).astype(BF16)
+
+    def operands(head):
+        at = head * depth
+        query = packed_ref[at : at + depth, :]
+        keys = packed_ref[features + at : features + at + depth, :].T
+        values = packed_ref[2 * features + at : 2 * features + at + depth, :]
+        return query, keys, jnp.concatenate([values, jnp.ones((16, tokens), BF16)])
+
+    def attend(head, values, cols):
+        product = dot(values, exps_ref[head, :, cols], 1, 0)
+        inverse_total = 1.0 / product[depth : depth + 1]
+        total_ref[head, :, cols] = inverse_total
+        attended_ref[head * depth : (head + 1) * depth, cols] = (
+            product[:depth] * inverse_total
+        ).astype(BF16)
+
+    blocks = [slice(start, start + SPACE_BLOCK) for start in range(0, tokens, SPACE_BLOCK)]
+    before = None
+    for head in range(HEADS):
+        query, keys, values = operands(head)
+        for cols in blocks:
+            for low in range(0, tokens, KEY_TILE):
+                rows = slice(low, low + KEY_TILE)
+                exps_ref[head, rows, cols] = jnp.exp2(
+                    dot(keys[rows], query[:, cols], 1, 0)
+                ).astype(BF16)
+            if before is not None:
+                attend(*before)
+            before = head, values, cols
+    attend(*before)
+
+    @pl.when(jnp.logical_not(in_range(total_ref[...])))
     def _():
-        coords = coord_table_ref.shape[1]
-        table_ref[...] = jnp.zeros(table_ref.shape, F32)
-        table_ref[ROW_AT : ROW_AT + coords, :] = coord_table_ref[0].astype(F32)
-        table_ref[COLUMN_AT : COLUMN_AT + coords, :] = coord_table_ref[1].astype(F32)
-        table_ref[BASIS_AT : BASIS_AT + 2, :] = basis_table_ref[...].astype(F32)
-        table_ref[SYNDROME_AT : SYNDROME_AT + 2, :] = syndrome_table_ref[...].astype(F32)
-        rounds = round_table_ref.shape[0]
-        table_ref[ROUND_AT : ROUND_AT + rounds, :] = round_table_ref[...].astype(F32)
-        width = index_ref.shape[2]
-        levels = lax.broadcasted_iota(jnp.int32, (LEVELS, width), 0)
-        for block in range(index_ref.shape[0]):
-            hit = levels == index_ref[block, 0:1, :]
-            for kind in range(1, index_ref.shape[1]):
-                hit = hit | (levels == index_ref[block, kind : kind + 1, :])
-            onehot_ref[:, block * width : (block + 1) * width] = hit.astype(F32).astype(BF16)
-        onehot = onehot_ref[...]
-        table = table_ref[...].astype(BF16)
-        row_ref[...] = dot(onehot, table, 0, 0).astype(BF16)
-        x = dot(table, onehot, 0, 0).astype(BF16)
-        x_ref[...] = x
-        normed, inverse = norm_columns(x.astype(F32), as_column(gain_ref[...]))
-        normed_ref[...] = normed
-        inverse_ref[...] = inverse
-        packed = dot(w_qkv_ref[...], normed, 0, 0)
-        packed_ref[:features, :] = (packed[:features] * (math.log2(math.e) * depth**-0.5)).astype(
-            BF16
-        )
-        packed_ref[features:, :] = packed[features:].astype(BF16)
-
-    at = pl.multiple_of(head * depth, depth)
-    query = packed_ref[pl.ds(at, depth), :]
-    keys = packed_ref[pl.ds(features + at, depth), :].T
-    values = packed_ref[pl.ds(2 * features + at, depth), :]
-    values = jnp.concatenate([values, jnp.ones((16, tokens), BF16)])
-    block = SPACE_BLOCK
-    starts = list(range(0, tokens, block))
-    scores = dot(keys, query[:, :block], 1, 0)
-    for start in starts:
-        cols = slice(start, start + block)
-        if start + block < tokens:
-            later = dot(keys, query[:, start + block : start + 2 * block], 1, 0)
-        exps = jnp.exp2(scores - jnp.max(scores, axis=0, keepdims=True)).astype(BF16)
-        exps_ref[0, :, cols] = exps
-        product = dot(values, exps, 1, 0)
-        inverse_total = 1.0 / product[depth : depth + 1]
-        total_ref[0, :, cols] = inverse_total
-        attended_ref[pl.ds(at, depth), cols] = (product[:depth] * inverse_total).astype(BF16)
-        scores = later
-
-    @pl.when(head == HEADS - 1)
-    def _():
-        branch = dot(attended_ref[...], w_out_ref[...], 0, 0)
-        middle = (row_ref[...].astype(F32) + branch).astype(BF16)
-        middle_ref[...] = middle.reshape(middle_ref.shape)
+        for head in range(HEADS):
+            query, keys, values = operands(head)
+            for cols in blocks:
+                scores = dot(keys, query[:, cols], 1, 0)
+                peak = jnp.max(scores, axis=0, keepdims=True)
+                exps_ref[head, :, cols] = jnp.exp2(scores - peak).astype(BF16)
+                attend(head, values, cols)
+
+    branch = dot(attended_ref[...], w_out_ref[...], 0, 0)
+    middle = (row_ref[...].astype(F32) + branch).astype(BF16)
+    middle_ref[...] = middle.reshape(middle_ref.shape)
 
 
 SPACE_BLOCK = 256
+KEY_TILE = 128
+VMEM = pl.BlockSpec(memory_space=pltpu.VMEM)
+ANY = pl.BlockSpec(memory_space=pl.ANY)
 
 
 def run_space_forward(index, tables, gain, w_qkv, w_out, chunks):
@@ -158,16 +184,16 @@
     features = w_out.shape[0]
     shapes = [
         ((chunks, tokens // chunks, features), BF16),
-        ((features, tokens), BF16),
-        ((features, tokens), BF16),
         ((1, tokens), F32),
-        ((3 * features, tokens), BF16),
-        ((features, tokens), BF16),
-        ((HEADS, tokens, tokens), BF16),
+        pltpu.VMEM((features, tokens), BF16),
         ((HEADS, 1, tokens), F32),
+        pltpu.VMEM((features, tokens), BF16),
+        pltpu.VMEM((features, tokens), BF16),
+        pltpu.VMEM((3 * features, tokens), BF16),
+        pltpu.VMEM((HEADS, tokens, tokens), BF16),
     ]
     arguments = (index,) + tables + (gain, w_qkv, w_out)
-    return call(
+    middle, inverse, attended, totals, x, normed, packed, exps = call(
         space_forward,
         shapes,
         arguments,
@@ -177,11 +203,10 @@
             ((tokens, features), BF16),
             ((LEVELS, tokens), BF16),
         ],
-        grid=(HEADS,),
-        in_specs=[whole(a.shape) for a in arguments],
-        out_specs=[whole(shape) for shape, _ in shapes[:6]]
-        + [per_head(shape) for shape, _ in shapes[6:]],
-    )
+        in_specs=[VMEM] * len(arguments),
+        out_specs=[VMEM] * 8,
+    )
+    return middle, x, normed, inverse, packed, attended, exps, totals
 
 
 def time_grad(grad_ref, w_out_ref, grad_row_ref, grad_attended_ref, grads_ref):
@@ -360,74 +385,73 @@
 
 
 def space_backward(
-    grad_ref, normed_ref, packed_ref, attended_ref, exps_ref, total_ref, w_out_ref, time_ref,
+    grad_ref, packed_ref, attended_ref, total_ref, w_out_ref, normed_ref, exps_ref, time_ref,
     grad_packed_ref, pieces_ref,
     grad_attended_ref, grad_scores_ref,
 ):
-    head = pl.program_id(0)
     features, tokens = attended_ref.shape
     depth = features // HEADS
-
-    @pl.when(head == 0)
-    def _():
-        grad = grad_ref[...].reshape(tokens, features)
-        grad_attended_ref[...] = dot(w_out_ref[...], grad, 1, 1).astype(BF16)
-
-    at = pl.multiple_of(head * depth, depth)
-    query = packed_ref[pl.ds(at, depth), :]
-    keys = packed_ref[pl.ds(features + at, depth), :]
-    values = packed_ref[pl.ds(2 * features + at, depth), :].T
-    grad = grad_attended_ref[pl.ds(at, depth), :].astype(F32) * total_ref[0]
-    inner = jnp.sum(
-        grad * attended_ref[pl.ds(at, depth), :].astype(F32), axis=0, keepdims=True
-    )
-    grad = grad.astype(BF16)
-    block = SPACE_BLOCK
-    grad_weights = dot(values, grad[:, :block], 1, 0)
-    for start in range(0, tokens, block):
-        cols = slice(start, start + block)
-        if start + block < tokens:
-            later = dot(values, grad[:, start + block : start + 2 * block], 1, 0)
-        exps = exps_ref[0, :, cols].astype(F32)
-        grad_scores = (exps * (grad_weights - inner[:, cols])).astype(BF16)
-        grad_scores_ref[:, cols] = grad_scores
-        grad_query = dot(keys, grad_scores, 1, 0) * depth**-0.5
-        grad_packed_ref[pl.ds(at, depth), cols] = grad_query.astype(BF16)
-        grad_weights = later
-    grad_packed_ref[pl.ds(2 * features + at, depth), :] = dot(grad, exps_ref[0], 1, 1).astype(BF16)
-    grad_packed_ref[pl.ds(features + at, depth), :] = (
-        dot(query, grad_scores_ref[...], 1, 1) * math.log(2.0)
-    ).astype(BF16)
-
-    @pl.when(head == HEADS - 1)
-    def _():
-        grad = grad_ref[...].reshape(tokens, features)
-        pieces_ref[:, 0:1] = time_ref[...]
-        store_blocks(
-            pieces_ref,
-            1,
-            dot(normed_ref[...], grad_packed_ref[...], 1, 1),
-            dot(attended_ref[...], grad, 1, 0),
+    new = grad_ref[...].reshape(tokens, features)
+    grad_attended_ref[...] = dot(w_out_ref[...], new, 1, 1).astype(BF16)
+    blocks = [slice(start, start + SPACE_BLOCK) for start in range(0, tokens, SPACE_BLOCK)]
+
+    def finish(head, grad):
+        at = head * depth
+        keys = packed_ref[features + at : features + at + depth, :]
+        query = packed_ref[at : at + depth, :]
+        scores = grad_scores_ref[head % 2]
+        grad_packed_ref[at : at + depth, :] = (dot(keys, scores, 1, 0) * depth**-0.5).astype(BF16)
+        grad_packed_ref[features + at : features + at + depth, :] = (
+            dot(query, scores, 1, 1) * math.log(2.0)
+        ).astype(BF16)
+        grad_packed_ref[2 * features + at : 2 * features + at + depth, :] = dot(
+            grad, exps_ref[head], 1, 1
+        ).astype(BF16)
+
+    before = None
+    for head in range(HEADS):
+        at = head * depth
+        values = packed_ref[2 * features + at : 2 * features + at + depth, :]
+        grad = grad_attended_ref[at : at + depth, :].astype(F32) * total_ref[head]
+        inner = jnp.sum(
+            grad * attended_ref[at : at + depth, :].astype(F32), axis=0, keepdims=True
         )
+        grad = grad.astype(BF16)
+        wide_grad = jnp.concatenate([grad, split_rows(inner)])
+        wide_values = jnp.concatenate([values.T, jnp.full((tokens, 16), -1.0, BF16)], axis=1)
+        for cols in blocks:
+            for low in range(0, tokens, KEY_TILE):
+                rows = slice(low, low + KEY_TILE)
+                centred = dot(wide_values[rows], wide_grad[:, cols], 1, 0)
+                grad_scores_ref[head % 2, rows, cols] = (
+                    exps_ref[head, rows, cols].astype(F32) * centred
+                ).astype(BF16)
+        if before is not None:
+            finish(*before)
+        before = head, grad
+    finish(*before)
+    pieces_ref[:, 0:1] = time_ref[...]
+    store_blocks(
+        pieces_ref,
+        1,
+        dot(normed_ref[...], grad_packed_ref[...], 1, 1),
+        dot(attended_ref[...], new, 1, 0),
+    )
 
 
 def run_space_backward(grad, normed, packed, attended, exps, totals, w_out, time_pieces):
     features, tokens = attended.shape
-    arguments = (grad, normed, packed, attended, exps, totals, w_out, time_pieces)
-    in_specs = [whole(a.shape) for a in arguments]
-    in_specs[4] = per_head(exps.shape)
-    in_specs[5] = per_head(totals.shape)
     parts, _, rows, _ = time_pieces.shape
-    shapes = [((3 * features, tokens), BF16), ((parts, 2, rows, features), BF16)]
+    normed, packed, attended, exps = in_vmem(normed, packed, attended, exps)
+    shapes = [pltpu.VMEM((3 * features, tokens), BF16), ((parts, 2, rows, features), BF16)]
     return call(
         space_backward,
         shapes,
-        arguments,
+        (grad, packed, attended, totals, w_out, normed, exps, time_pieces),
         14,
-        scratch=[((features, tokens), BF16), ((tokens, tokens), BF16)],
-        grid=(HEADS,),
-        in_specs=in_specs,
-        out_specs=[whole(shape) for shape, _ in shapes],
+        scratch=[((features, tokens), BF16), ((2, tokens, tokens), BF16)],
+        in_specs=[VMEM] * 8,
+        out_specs=[VMEM] * 2,
     )
 
 
@@ -450,6 +474,7 @@
 def run_space_stream(grad, x, inverse, grad_packed, gain, w_qkv, parts):
     features, tokens = x.shape
     rows = grad.shape[1]
+    x, grad_packed = in_vmem(x, grad_packed)
     return call(
         space_stream,
         [((parts, tokens // (parts * rows) + 2, rows, features), BF16)],

time: 177 us -> 192 us (1.085)
  local copies, waits for them, and re-layouts: 6.86 us -> 32.1 us
  Pallas kernels: 56.2 us -> 45.4 us
    unnamed x15 -> x73, local copies, waits for them, and re-layouts: 3.4 us -> 29.4 us
    pallas_call x8, Pallas kernels: 56.2 us -> 45.4 us  [call(): pl.pallas_call(kernel, out_shape=[jax.ShapeDtypeStruct(*item) if isinstan...]
  transfers between devices with their start and end apart: 6 -> 6, of which waited for: 5 -> 5; matrix products, arithmetic and copies ran while one was open for 1% -> 1% of each run, Pallas kernels for 14% -> 11%
where the time goes in v3:
time: 192 us; the launch traced here: 191 us
  waiting for transfers between devices  59.4 us (31%)
  Pallas kernels  45.4 us (24%)
  starting transfers between devices  36.4 us (19%)
  local copies, waits for them, and re-layouts  32.1 us (17%)
  blocking collectives  15.6 us (8%)
    all_to_all x6, waiting for transfers between devices, exchange(): return lax.all_to_all(values, axes, split_axis=0, concat_axis=0, tiled=True)  59.4 us
    pallas_call x8, Pallas kernels, call(): pl.pallas_call(kernel, out_shape=[jax.ShapeDtypeStruct(*item) if isinstan...  45.4 us
    all_to_all x6, starting transfers between devices, exchange(): return lax.all_to_all(values, axes, split_axis=0, concat_axis=0, tiled=True)  36.4 us
    unnamed x73, local copies, waits for them, and re-layouts  29.4 us
    all_to_all x1, blocking collectives, exchange(): return lax.all_to_all(values, axes, split_axis=0, concat_axis=0, tiled=True)  15.6 us
  transfers between devices with their start and end apart: 6, of which 5 were waited for; matrix products, arithmetic and copies ran while one was open for 1% of the time, Pallas kernels for 11%

profile of v3, /device:TPU:1, one launch (start us, length us, event | category | flops | bytes accessed | tf_op | source)
XLA Modules:
  0.0 191.4 jit_solution(2262449152227669555)
XLA Ops:
  3.4 8.5 %all-to-all-start = ((s32[8,5,128]{2,1,0:T(8,128)}), s32[8,5,128]{2,1,0:T(8,128)S(1)}, u32[]{:S(2)}, u32[]{:S(2)}) async-start(s32[8,5,128]{2,1,0:T(8,128)} %index_kernel.1), calls=%async_computation | async-start | bytes 65536 | tf_op jit(solution)/shard_map/all_to_all | solution.py:510
  12.7 5.8 %all-to-all-done.index_ref = s32[8,5,128]{2,1,0:T(8,128)S(1)} async-done(((s32[8,5,128]{2,1,0:T(8,128)}), s32[8,5,128]{2,1,0:T(8,128)S(1)}, u32[]{:S(2)}, u32[]{:S(2)}) %all-to-all-start) | async-done | bytes 20512 | tf_op jit(solution)/shard_map/all_to_all | solution.py:510
  18.5 6.8 %all-to-all-start.1 = ((bf16[16,8,8,256]{3,2,1,0:T(8,128)(2,1)}), bf16[16,8,8,256]{3,2,1,0:T(8,128)(2,1)S(1)}, u32[]{:S(2)}, u32[]{:S(2)}) async-start(bf16[16,8,8,256]{3,2,1,0:T(8,128)(2,1)} %copy_bitcast_fusion), calls=%async_computation.1 | async-start | bytes 1048576 | tf_op jit(solution)/shard_map/all_to_all | solution.py:510
  25.4 17.1 %space_forward.1 = (bf16[128,8,256]{2,1,0:T(8,128)(2,1)}, f32[1,1024]{1,0:T(1,128)S(1)}, bf16[256,1024]{1,0:T(8,128)(2,1)S(1)}, f32[4,1,1024]{2,1,0:T(1,128)S(1)...) custom-call(s32[8,5,128]{2,1,0:T(8,128)S(1)} %all-to-all-done.index_, ...), custom_call_target="tpu_custom_call" | custom-call | flops 5000000000 | bytes 20000000 | tf_op jit(solution)/shard_map/space_forward/pallas_call | solution.py:27
  42.5 3.3 %copy-done.17 = bf16[4,1024,1024]{2,1,0:T(8,128)(2,1)} copy-done((bf16[4,1024,1024]{2,1,0:T(8,128)(2,1)}, bf16[4,1024,1024]{2,1,0:T(8,128)(2,1)S(1)}, u32[]{:S(2)}) %copy-start.17) | copy-done | bytes 8388632
  45.8 1.1 copy-done.29
  48.6 6.0 %all-to-all-start.2 = ((bf16[128,8,256]{2,1,0:T(8,128)(2,1)}), bf16[128,8,256]{2,1,0:T(8,128)(2,1)S(1)}, u32[]{:S(2)}, u32[]{:S(2)}) async-start(bf16[128,8,256]{2,1,0:T(8,128)(2,1)} %get-tuple-element.36), calls=%async_computation.2 | async-start | bytes 1048576 | tf_op jit(solution)/shard_map/all_to_all | solution.py:510
  56.8 11.5 %all-to-all-done.2 = bf16[128,8,256]{2,1,0:T(8,128)(2,1)S(1)} async-done(((bf16[128,8,256]{2,1,0:T(8,128)(2,1)}), bf16[128,8,256]{2,1,0:T(8,128)(2,1)S(1)}, u32[]{:S(2)}, u32[]{:S(2)}) %all-to-all-start.2) | async-done | bytes 524320 | tf_op jit(solution)/shard_map/all_to_all | solution.py:510
  68.3 1.0 copy-done.22
  69.4 11.5 %time_block.1 = (bf16[8,16,8,256]{3,2,1,0:T(8,128)(2,1)}, bf16[256,1024]{1,0:T(8,128)(2,1)S(1)}, bf16[768,1024]{1,0:T(8,128)(2,1)S(1)}, bf16[256,1024]{1,0:T(8,128)(2,1)S(1)}) custom-call(bf16[8,16,8,256]{3,2,1,0:T(8,128)(2,1)S(1)} %bitcast.13, bf16[16,8,8,256]{3,2,1,0:T(8,128)(2,1)S(1)} %all-to-all-done.1.grad_ref, bf16[256,1024]{1,0:T(8,128)(2,1)S(1)} %copy-done.22, ...), custom_call_target="tpu_custom_call" | custom-call | flops 5000000000 | bytes 20000000 | tf_op jit(solution)/shard_map/time_block/pallas_call | solution.py:27
  80.9 1.1 copy-done.15
  83.6 4.5 %all-to-all-start.3 = ((bf16[128,8,256]{2,1,0:T(8,128)(2,1)}), bf16[128,8,256]{2,1,0:T(8,128)(2,1)S(1)}, u32[]{:S(2)}, u32[]{:S(2)}) async-start(bf16[128,8,256]{2,1,0:T(8,128)(2,1)} %bitcast.6), calls=%async_computation.3 | async-start | bytes 1048576 | tf_op jit(solution)/shard_map/all_to_all | solution.py:510
  88.1 1.4 copy-done.16
  90.6 1.0 copy-done.26
  91.6 1.0 copy-done.28
  92.7 2.2 %time_rest.1 = (bf16[16,24,8,256]{3,2,1,0:T(8,128)(2,1)}, bf16[128,1,8,256]{3,2,1,0:T(8,128)(2,1)S(1)}) custom-call(bf16[8,16,8,256]{3,2,1,0:T(8,128)(2,1)S(1)} %bitcast.14, bf16[256,1024]{1,0:T(8,128)(2,1)S(1)} %copy-done.26, bf16[768,1024]{1,0:T(8,128)(2,1)S(1)} %copy-done.16, bf16[256,1024]{1,0:T(8,128)(2,1)S(1)} %copy-done.28, ...), custom_call_target="tpu_custom_call" | custom-call | flops 2500000000 | bytes 10000000 | tf_op jit(solution)/shard_map/time_rest/pallas_call | solution.py:27
  95.6 6.2 %all-to-all-done.3.grad_ref = bf16[128,8,256]{2,1,0:T(8,128)(2,1)S(1)} async-done(((bf16[128,8,256]{2,1,0:T(8,128)(2,1)}), bf16[128,8,256]{2,1,0:T(8,128)(2,1)S(1)}, u32[]{:S(2)}, u32[]{:S(2)}) %all-to-all-start.3) | async-done | bytes 524320 | tf_op jit(solution)/shard_map/all_to_all | solution.py:510
  101.9 3.4 %copy-done.18 = bf16[4,1024,1024]{2,1,0:T(8,128)(2,1)S(1)} copy-done((bf16[4,1024,1024]{2,1,0:T(8,128)(2,1)S(1)}, bf16[4,1024,1024]{2,1,0:T(8,128)(2,1)}, u32[]{:S(2)}) %copy-start.18) | copy-done | bytes 8388632
  105.2 1.0 copy-done.24
  106.3 1.4 copy-done.30
  107.7 1.0 copy-done.32
  109.8 10.8 %space_backward.1 = (bf16[768,1024]{1,0:T(8,128)(2,1)S(1)}, bf16[128,2,8,256]{3,2,1,0:T(8,128)(2,1)}) custom-call(bf16[128,8,256]{2,1,0:T(8,128)(2,1)S(1)} %all-to-all-done.3.grad_ref, bf16[768,1024]{1,0:T(8,128)(2,1)S(1)} %copy-done.30, bf16[256,1024]{1,0:T(8,128)(2,1)S(1)} %copy-done.32, f32[4,1,1024]{2,1,0:T(1,128)S(1)} %get-tuple-element.49.total_ref, ...), custom_call_target="tpu_custom_call" | custom-call | flops 7000000000 | bytes 28000000 | tf_op jit(solution)/shard_map/space_backward/pallas_call | solution.py:27
  120.5 1.2 copy-done.13
  121.7 5.3 %all-to-all-start.4 = ((bf16[128,2,8,256]{3,2,1,0:T(8,128)(2,1)}), bf16[128,2,8,256]{3,2,1,0:T(8,128)(2,1)}, u32[]{:S(2)}, u32[]{:S(2)}) async-start(bf16[128,2,8,256]{3,2,1,0:T(8,128)(2,1)} %get-tuple-element.54), calls=%async_computation.4 | async-start | bytes 2097152 | tf_op jit(solution)/shard_map/all_to_all | solution.py:510
  127.1 1.4 copy-done.14
  129.5 15.2 %all-to-all-done.4 = bf16[128,2,8,256]{3,2,1,0:T(8,128)(2,1)} async-done(((bf16[128,2,8,256]{3,2,1,0:T(8,128)(2,1)}), bf16[128,2,8,256]{3,2,1,0:T(8,128)(2,1)}, u32[]{:S(2)}, u32[]{:S(2)}) %all-to-all-start.4) | async-done | bytes 1048608 | tf_op jit(solution)/shard_map/all_to_all | solution.py:510
  144.7 1.4 convert_reduce_fusion
  146.1 15.6 %all_to_all.35 = bf16[8,18,8,256]{3,2,1,0:T(8,128)(2,1)S(1)} all-to-all(bf16[8,18,8,256]{3,2,1,0:T(8,128)(2,1)S(1)} %broadcast_dynamic-update-slice_fusion.1), channel_id=1, replica_groups=mesh['rounds'=16,'stab'=8] {'stab'}, dimensions={0} | all-to-all | bytes 1179648 | tf_op jit(solution)/shard_map/all_to_all | solution.py:510
  161.8 1.1 broadcast_dynamic-update-slice_fusion
  162.9 5.3 %all-to-all-start.6 = ((bf16[16,24,8,256]{3,2,1,0:T(8,128)(2,1)}), bf16[16,24,8,256]{3,2,1,0:T(8,128)(2,1)S(1)}, u32[]{:S(2)}, u32[]{:S(2)}) async-start(bf16[16,24,8,256]{3,2,1,0:T(8,128)(2,1)} %broadcast_dynamic-update-slice_fusion), calls=%async_computation.6 | async-start | bytes 3145728 | tf_op jit(solution)/shard_map/all_to_all | solution.py:510
  169.0 20.7 %all-to-all-done.6.incoming_ref = bf16[16,24,8,256]{3,2,1,0:T(8,128)(2,1)S(1)} async-done(((bf16[16,24,8,256]{3,2,1,0:T(8,128)(2,1)}), bf16[16,24,8,256]{3,2,1,0:T(8,128)(2,1)S(1)}, u32[]{:S(2)}, u32[]{:S(2)}) %all-to-all-start.6) | async-done | bytes 1572896 | tf_op jit(solution)/shard_map/all_to_all | solution.py:510
  189.7 1.6 unpack.1
  (69 shorter events, 13.8 us)
Async XLA Ops:
  0.6 11.2 %copy-start = (bf16[8,128,256]{2,1,0:T(8,128)(2,1)S(1)}, bf16[8,128,256]{2,1,0:T(8,128)(2,1)}, u32[]{:S(2)}) copy-start(bf16[8,128,256]{2,1,0:T(8,128)(2,1)} %param.27) | copy-start | bytes 1572868
  2.7 22.6 %copy-start.35 = (bf16[2,42,256]{2,0,1:T(2,128)(2,1)S(1)}, bf16[2,42,256]{2,0,1:T(2,128)(2,1)}, u32[]{:S(2)}) copy-start(bf16[2,42,256]{2,0,1:T(2,128)(2,1)} %param.19) | copy-start | bytes 129028
  3.4 22.0 %copy-start.2 = (bf16[256,768]{1,0:T(8,128)(2,1)S(1)}, bf16[256,768]{1,0:T(8,128)(2,1)}, u32[]{:S(2)}) copy-start(bf16[256,768]{1,0:T(8,128)(2,1)} %w_qkv_ref.5) | copy-start | bytes 1179652
  3.4 22.0 %copy-start.4 = (bf16[256,256]{1,0:T(8,128)(2,1)S(1)}, bf16[256,256]{1,0:T(8,128)(2,1)}, u32[]{:S(2)}) copy-start(bf16[256,256]{1,0:T(8,128)(2,1)} %w_out_ref.7) | copy-start | bytes 393220
  3.4 22.0 %copy-start.6 = (bf16[8,256]{1,0:T(8,128)(2,1)S(1)}, bf16[8,256]{1,0:T(8,128)(2,1)}, u32[]{:S(2)}) copy-start(bf16[8,256]{1,0:T(8,128)(2,1)} %round_table_ref.1) | copy-start | bytes 12292
  3.4 22.0 %copy-start.8 = (bf16[2,256]{1,0:T(2,128)(2,1)S(1)}, bf16[2,256]{1,0:T(2,128)(2,1)}, u32[]{:S(2)}) copy-start(bf16[2,256]{1,0:T(2,128)(2,1)} %syndrome_table_ref.1) | copy-start | bytes 3076
  3.4 22.0 %copy-start.9 = (bf16[2,256]{1,0:T(2,128)(2,1)S(1)}, bf16[2,256]{1,0:T(2,128)(2,1)}, u32[]{:S(2)}) copy-start(bf16[2,256]{1,0:T(2,128)(2,1)} %basis_table_ref.1) | copy-start | bytes 3076
  3.4 22.0 %copy-start.11 = (f32[256]{0:T(256)S(1)}, f32[256]{0:T(256)}, u32[]{:S(2)}) copy-start(f32[256]{0:T(256)} %param.21) | copy-start | bytes 3076
  3.4 15.1 %all-to-all-start = ((s32[8,5,128]{2,1,0:T(8,128)}), s32[8,5,128]{2,1,0:T(8,128)S(1)}, u32[]{:S(2)}, u32[]{:S(2)}) async-start(s32[8,5,128]{2,1,0:T(8,128)} %index_kernel.1), calls=%async_computation | async-start | bytes 65536 | tf_op jit(solution)/shard_map/all_to_all | solution.py:510
  18.5 30.1 %all-to-all-start.1 = ((bf16[16,8,8,256]{3,2,1,0:T(8,128)(2,1)}), bf16[16,8,8,256]{3,2,1,0:T(8,128)(2,1)S(1)}, u32[]{:S(2)}, u32[]{:S(2)}) async-start(bf16[16,8,8,256]{3,2,1,0:T(8,128)(2,1)} %copy_bitcast_fusion), calls=%async_computation.1 | async-start | bytes 1048576 | tf_op jit(solution)/shard_map/all_to_all | solution.py:510
  25.4 29.2 %copy-start.3 = (bf16[256,256]{1,0:T(8,128)(2,1)S(1)}, bf16[256,256]{1,0:T(8,128)(2,1)}, u32[]{:S(2)}) copy-start(bf16[256,256]{1,0:T(8,128)(2,1)} %w_out_ref.6) | copy-start | bytes 393220
  42.5 3.3 %copy-start.17 = (bf16[4,1024,1024]{2,1,0:T(8,128)(2,1)}, bf16[4,1024,1024]{2,1,0:T(8,128)(2,1)S(1)}, u32[]{:S(2)}) copy-start(bf16[4,1024,1024]{2,1,0:T(8,128)(2,1)S(1)} %get-tuple-element.51.exps_ref) | copy-start | bytes 25165828
  45.8 1.1 copy-start.29
  48.6 19.7 %all-to-all-start.2 = ((bf16[128,8,256]{2,1,0:T(8,128)(2,1)}), bf16[128,8,256]{2,1,0:T(8,128)(2,1)S(1)}, u32[]{:S(2)}, u32[]{:S(2)}) async-start(bf16[128,8,256]{2,1,0:T(8,128)(2,1)} %get-tuple-element.36), calls=%async_computation.2 | async-start | bytes 1048576 | tf_op jit(solution)/shard_map/all_to_all | solution.py:510
  54.6 13.7 %copy-start.1 = (bf16[256,768]{1,0:T(8,128)(2,1)S(1)}, bf16[256,768]{1,0:T(8,128)(2,1)}, u32[]{:S(2)}) copy-start(bf16[256,768]{1,0:T(8,128)(2,1)} %w_qkv_ref.4) | copy-start | bytes 1179652
  54.6 13.7 %copy-start.10 = (f32[256]{0:T(256)S(1)}, f32[256]{0:T(256)}, u32[]{:S(2)}) copy-start(f32[256]{0:T(256)} %param.24) | copy-start | bytes 3076
  68.3 1.0 copy-start.22
  80.9 1.1 copy-start.15
  83.6 18.2 %all-to-all-start.3 = ((bf16[128,8,256]{2,1,0:T(8,128)(2,1)}), bf16[128,8,256]{2,1,0:T(8,128)(2,1)S(1)}, u32[]{:S(2)}, u32[]{:S(2)}) async-start(bf16[128,8,256]{2,1,0:T(8,128)(2,1)} %bitcast.6), calls=%async_computation.3 | async-start | bytes 1048576 | tf_op jit(solution)/shard_map/all_to_all | solution.py:510
  88.1 1.4 copy-start.16
  89.5 1.0 copy-start.20
  90.6 1.0 copy-start.26
  91.6 1.0 copy-start.28
  101.9 3.4 %copy-start.18 = (bf16[4,1024,1024]{2,1,0:T(8,128)(2,1)S(1)}, bf16[4,1024,1024]{2,1,0:T(8,128)(2,1)}, u32[]{:S(2)}) copy-start(bf16[4,1024,1024]{2,1,0:T(8,128)(2,1)} %copy-done.17) | copy-start | bytes 25165828
  105.2 1.0 copy-start.24
  106.3 1.4 copy-start.30
  107.7 1.0 copy-start.32
  108.7 1.0 copy-start.34
  120.5 1.2 copy-start.13
  121.7 23.0 %all-to-all-start.4 = ((bf16[128,2,8,256]{3,2,1,0:T(8,128)(2,1)}), bf16[128,2,8,256]{3,2,1,0:T(8,128)(2,1)}, u32[]{:S(2)}, u32[]{:S(2)}) async-start(bf16[128,2,8,256]{3,2,1,0:T(8,128)(2,1)} %get-tuple-element.54), calls=%async_computation.4 | async-start | bytes 2097152 | tf_op jit(solution)/shard_map/all_to_all | solution.py:510
  127.1 1.4 copy-start.14
  162.9 26.9 %all-to-all-start.6 = ((bf16[16,24,8,256]{3,2,1,0:T(8,128)(2,1)}), bf16[16,24,8,256]{3,2,1,0:T(8,128)(2,1)S(1)}, u32[]{:S(2)}, u32[]{:S(2)}) async-start(bf16[16,24,8,256]{3,2,1,0:T(8,128)(2,1)} %broadcast_dynamic-update-slice_fusion), calls=%async_computation.6 | async-start | bytes 3145728 | tf_op jit(solution)/shard_map/all_to_all | solution.py:510
  (10 other events, 7.7 us)

commit v4 on v3

--- a/solution.py
+++ b/solution.py
@@ -9,7 +9,6 @@
 
 HEADS = 4
 EPSILON = 1e-06
-VMEM_BYTES = 20 * 2**20
 F32 = jnp.float32
 BF16 = jnp.bfloat16
 
@@ -23,14 +22,14 @@
     )
 
 
-def call(kernel, shapes, arguments, microseconds, scratch=(), **grid):
+def call(kernel, shapes, arguments, microseconds, scratch=(), megabytes=60, **grid):
     return pl.pallas_call(
         kernel,
         out_shape=[
             jax.ShapeDtypeStruct(*item) if isinstance(item, tuple) else item for item in shapes
         ],
         scratch_shapes=[pltpu.VMEM(*item) if isinstance(item, tuple) else item for item in scratch],
-        compiler_params=pltpu.CompilerParams(vmem_limit_bytes=VMEM_BYTES),
+        compiler_params=pltpu.CompilerParams(vmem_limit_bytes=megabytes * 2**20),
         cost_estimate=pl.CostEstimate(
             flops=microseconds * 500_000_000,
             bytes_accessed=microseconds * 2_000_000,
@@ -41,8 +40,8 @@
     )(*arguments)
 
 
-def in_vmem(*arrays):
-    return [pltpu.with_memory_space_constraint(array, pltpu.VMEM) for array in arrays]
+def in_hbm(*arrays):
+    return [pltpu.with_memory_space_constraint(array, pltpu.HBM) for array in arrays]
 
 
 def in_range(inverse_totals):
@@ -97,11 +96,21 @@
 def space_forward(
     index_ref, syndrome_table_ref, basis_table_ref, coord_table_ref, round_table_ref,
     gain_ref, w_qkv_ref, w_out_ref,
-    middle_ref, inverse_ref, attended_ref, total_ref, x_ref, normed_ref, packed_ref, exps_ref,
-    table_ref, row_ref, onehot_ref,
+    middle_ref, inverse_ref, attended_ref, total_ref, x_out, normed_out, packed_out, exps_out,
+    table_ref, row_ref, onehot_ref, x_ref, normed_ref, packed_ref, exps_ref, sems,
 ):
     features, tokens = x_ref.shape
     depth = features // HEADS
+    copies = [
+        pltpu.make_async_copy(x_ref, x_out, sems.at[HEADS]),
+        pltpu.make_async_copy(normed_ref, normed_out, sems.at[HEADS + 1]),
+        pltpu.make_async_copy(packed_ref, packed_out, sems.at[HEADS + 2]),
+    ]
+    head_copies = [
+        pltpu.make_async_copy(exps_ref.at[head], exps_out.at[head], sems.at[head])
+        for head in range(HEADS)
+    ]
+
     coords = coord_table_ref.shape[1]
     table_ref[...] = jnp.zeros(table_ref.shape, F32)
     table_ref[ROW_AT : ROW_AT + coords, :] = coord_table_ref[0].astype(F32)
@@ -120,12 +129,15 @@
     table = table_ref[...].astype(BF16)
     x = dot(table, onehot_ref[...], 0, 0).astype(BF16)
     x_ref[...] = x
+    copies[0].start()
     normed, inverse = norm_columns(x.astype(F32), as_column(gain_ref[...]))
     normed_ref[...] = normed
+    copies[1].start()
     inverse_ref[...] = inverse
     packed = dot(w_qkv_ref[...], normed, 0, 0)
     packed_ref[:features, :] = (packed[:features] * (math.log2(math.e) * depth**-0.5)).astype(BF16)
     packed_ref[features:, :] = packed[features:].astype(BF16)
+    copies[2].start()
     row_ref[...] = dot(onehot_ref[...], table, 0, 0).astype(BF16)
 
     def operands(head):
@@ -156,10 +168,13 @@
             if before is not None:
                 attend(*before)
             before = head, values, cols
+        head_copies[head].start()
     attend(*before)
 
     @pl.when(jnp.logical_not(in_range(total_ref[...])))
     def _():
+        for copy in head_copies:
+            copy.wait()
         for head in range(HEADS):
             query, keys, values = operands(head)
             for cols in blocks:
@@ -167,14 +182,18 @@
                 peak = jnp.max(scores, axis=0, keepdims=True)
                 exps_ref[head, :, cols] = jnp.exp2(scores - peak).astype(BF16)
                 attend(head, values, cols)
+            head_copies[head].start()
 
     branch = dot(attended_ref[...], w_out_ref[...], 0, 0)
     middle = (row_ref[...].astype(F32) + branch).astype(BF16)
     middle_ref[...] = middle.reshape(middle_ref.shape)
+    for copy in head_copies + copies:
+        copy.wait()
 
 
 SPACE_BLOCK = 256
 KEY_TILE = 128
+LOADS = 4
 VMEM = pl.BlockSpec(memory_space=pltpu.VMEM)
 ANY = pl.BlockSpec(memory_space=pl.ANY)
 
@@ -185,12 +204,12 @@
     shapes = [
         ((chunks, tokens // chunks, features), BF16),
         ((1, tokens), F32),
-        pltpu.VMEM((features, tokens), BF16),
+        ((features, tokens), BF16),
         ((HEADS, 1, tokens), F32),
-        pltpu.VMEM((features, tokens), BF16),
-        pltpu.VMEM((features, tokens), BF16),
-        pltpu.VMEM((3 * features, tokens), BF16),
-        pltpu.VMEM((HEADS, tokens, tokens), BF16),
+        pltpu.HBM((features, tokens), BF16),
+        pltpu.HBM((features, tokens), BF16),
+        pltpu.HBM((3 * features, tokens), BF16),
+        pltpu.HBM((HEADS, tokens, tokens), BF16),
     ]
     arguments = (index,) + tables + (gain, w_qkv, w_out)
     middle, inverse, attended, totals, x, normed, packed, exps = call(
@@ -202,9 +221,14 @@
             ((LEVELS, features), F32),
             ((tokens, features), BF16),
             ((LEVELS, tokens), BF16),
+            ((features, tokens), BF16),
+            ((features, tokens), BF16),
+            ((3 * features, tokens), BF16),
+            ((HEADS, tokens, tokens), BF16),
+            pltpu.SemaphoreType.DMA((HEADS + 3,)),
         ],
         in_specs=[VMEM] * len(arguments),
-        out_specs=[VMEM] * 8,
+        out_specs=[VMEM] * 4 + [ANY] * 4,
     )
     return middle, x, normed, inverse, packed, attended, exps, totals
 
@@ -237,9 +261,10 @@
 
 
 def time_block(
-    middle_ref, grad_ref, grad_attended_ref, gain_ref, w_qkv_ref,
-    grad_middle_ref, normed_ref, grad_packed_ref, attended_ref,
-    x_ref, inverse_ref, packed_ref, rows_ref,
+    middle_ref, grad_in, grad_attended_in, gain_ref, w_qkv_ref,
+    grad_middle_ref, normed_out, grad_packed_out, attended_out,
+    grad_ref, grad_attended_ref, normed_ref, grad_packed_ref, attended_ref, x_ref, packed_ref,
+    rows_ref, sems,
 ):
     stab_parts, round_parts, stabs, features = middle_ref.shape
     rounds = stab_parts * round_parts
@@ -247,6 +272,10 @@
     depth = features // HEADS
     scale = depth**-0.5
 
+    load_grad = pltpu.make_async_copy(grad_in, grad_ref, sems.at[3])
+    load_attended = pltpu.make_async_copy(grad_attended_in, grad_attended_ref, sems.at[4])
+    load_grad.start()
+    load_attended.start()
     middle = jnp.swapaxes(middle_ref[...].astype(F32), 0, 1).reshape(tokens, features)
     lanes = rows_ref.shape[2]
     halves = [slice(part * lanes, (part + 1) * lanes) for part in range(features // lanes)]
@@ -261,43 +290,63 @@
     gain = as_column(gain_ref[...])
     normed, inverse = norm_columns(x, gain)
     normed_ref[...] = normed
-    inverse_ref[...] = inverse
+    store_normed = pltpu.make_async_copy(normed_ref, normed_out, sems.at[0])
+    store_normed.start()
     packed = dot(w_qkv_ref[...], normed, 0, 0)
     to_base_two = math.log2(math.e) * scale
     packed_ref[:features, :] = (packed[:features] * to_base_two).astype(BF16)
     packed_ref[features:, :] = packed[features:].astype(BF16)
 
-    def one_stab(stab, carry):
-        cols = pl.ds(pl.multiple_of(stab * rounds, rounds), rounds)
-        for head in range(HEADS):
-            at = head * depth
-            query = packed_ref[at : at + depth, cols]
-            keys = packed_ref[features + at : features + at + depth, cols]
-            values = packed_ref[2 * features + at : 2 * features + at + depth, cols]
-            grad = grad_attended_ref[at : at + depth, cols]
-            scores = dot(keys, query, 0, 0)
-            shifted = jnp.exp2(scores - jnp.max(scores, axis=0, keepdims=True))
-            probabilities = shifted * (1.0 / jnp.sum(shifted, axis=0, keepdims=True))
-            weights = probabilities.astype(BF16)
-            attended_ref[at : at + depth, cols] = dot(values, weights, 1, 0).astype(BF16)
-            grad_weights = dot(values, grad, 0, 0)
-            inner = jnp.sum(probabilities * grad_weights, axis=0, keepdims=True)
-            grad_scores = (probabilities * (grad_weights - inner)).astype(BF16)
-            grad_packed_ref[at : at + depth, cols] = (dot(keys, grad_scores, 1, 0) * scale).astype(
-                BF16
-            )
+    ones = jnp.ones((16, rounds), BF16)
+    load_attended.wait()
+    load_grad.wait()
+
+    def some_stabs(step, carry):
+        items = []
+        for stab in range(TIME_GROUP):
+            start = pl.multiple_of((step * TIME_GROUP + stab) * rounds, rounds)
+            cols = pl.ds(start, rounds)
+            items += [(head * depth, cols) for head in range(HEADS)]
+        query = [packed_ref[at : at + depth, cols] for at, cols in items]
+        keys = [packed_ref[features + at : features + at + depth, cols] for at, cols in items]
+        values = [
+            packed_ref[2 * features + at : 2 * features + at + depth, cols] for at, cols in items
+        ]
+        scores = [dot(k, q, 0, 0) for k, q in zip(keys, query)]
+        exps = [
+            jnp.exp2(each - jnp.max(each, axis=0, keepdims=True)).astype(BF16) for each in scores
+        ]
+        products = [dot(jnp.concatenate([v, ones]), e, 1, 0) for v, e in zip(values, exps)]
+        grads, inners = [], []
+        for (at, cols), product in zip(items, products):
+            inverse_total = 1.0 / product[depth : depth + 1]
+            attended = product[:depth] * inverse_total
+            attended_ref[at : at + depth, cols] = attended.astype(BF16)
+            grad = grad_attended_ref[at : at + depth, cols].astype(F32) * inverse_total
+            inners.append(jnp.sum(grad * attended, axis=0, keepdims=True))
+            grads.append(grad.astype(BF16))
+        centred = [dot(v, g, 0, 0) - inner for v, g, inner in zip(values, grads, inners)]
+        grad_scores = [(e.astype(F32) * c).astype(BF16) for e, c in zip(exps, centred)]
+        for (at, cols), g, e in zip(items, grads, exps):
+            grad_packed_ref[2 * features + at : 2 * features + at + depth, cols] = dot(
+                g, e, 1, 1
+            ).astype(BF16)
+        for (at, cols), k, each in zip(items, keys, grad_scores):
+            grad_packed_ref[at : at + depth, cols] = (dot(k, each, 1, 0) * scale).astype(BF16)
+        for (at, cols), q, each in zip(items, query, grad_scores):
             grad_packed_ref[features + at : features + at + depth, cols] = (
-                dot(query, grad_scores, 1, 1) * math.log(2.0)
-            ).astype(BF16)
-            grad_packed_ref[2 * features + at : 2 * features + at + depth, cols] = dot(
-                grad, weights, 1, 1
+                dot(q, each, 1, 1) * math.log(2.0)
             ).astype(BF16)
         return carry
 
-    lax.fori_loop(0, stabs, one_stab, 0, unroll=TIME_UNROLL)
+    lax.fori_loop(0, stabs // TIME_GROUP, some_stabs, 0, unroll=TIME_UNROLL)
+    store_attended = pltpu.make_async_copy(attended_ref, attended_out, sems.at[1])
+    store_packed = pltpu.make_async_copy(grad_packed_ref, grad_packed_out, sems.at[2])
+    store_attended.start()
+    store_packed.start()
 
     grad_normed = dot(w_qkv_ref[...], grad_packed_ref[...], 1, 0)
-    grad_stream = norm_columns_backward(x_ref[...], gain, inverse_ref[...], grad_normed)
+    grad_stream = norm_columns_backward(x_ref[...], gain, inverse, grad_normed)
     for stab in range(stabs):
         cols = slice(stab * rounds, (stab + 1) * rounds)
         at = pl.ds(stab, rounds, stride=stabs)
@@ -307,19 +356,24 @@
         grad_middle = rows_ref[part].reshape(round_parts, stab_parts, stabs, lanes)
         grad_middle = grad_middle + grad_ref[:, :, :, half].astype(F32)
         grad_middle_ref[:, :, :, half] = jnp.swapaxes(grad_middle, 0, 1).astype(BF16)
-
-
-TIME_UNROLL = 2
+    store_normed.wait()
+    store_attended.wait()
+    store_packed.wait()
+
+
+TIME_UNROLL = True
+TIME_GROUP = 2
 
 
 def run_time_block(middle, grad, grad_attended, gain, w_qkv):
     stab_parts, round_parts, stabs, features = middle.shape
     tokens = stab_parts * round_parts * stabs
+    grad, grad_attended = in_hbm(grad, grad_attended)
     shapes = [
         (middle.shape, BF16),
-        ((features, tokens), BF16),
-        ((3 * features, tokens), BF16),
-        ((features, tokens), BF16),
+        pltpu.HBM((features, tokens), BF16),
+        pltpu.HBM((3 * features, tokens), BF16),
+        pltpu.HBM((features, tokens), BF16),
     ]
     return call(
         time_block,
@@ -327,11 +381,19 @@
         (middle, grad, grad_attended, gain, w_qkv),
         10,
         scratch=[
+            (grad.shape, BF16),
+            (grad_attended.shape, BF16),
+            ((features, tokens), BF16),
+            ((3 * features, tokens), BF16),
+            ((features, tokens), BF16),
             ((features, tokens), F32),
-            ((1, tokens), F32),
             ((3 * features, tokens), BF16),
             ((features // 128, tokens, 128), F32),
+            pltpu.SemaphoreType.DMA((5,)),
         ],
+        megabytes=24,
+        in_specs=[VMEM, ANY, ANY, VMEM, VMEM],
+        out_specs=[VMEM] + [ANY] * 3,
     )
 
 
@@ -385,14 +447,46 @@
 
 
 def space_backward(
-    grad_ref, packed_ref, attended_ref, total_ref, w_out_ref, normed_ref, exps_ref, time_ref,
-    grad_packed_ref, pieces_ref,
-    grad_attended_ref, grad_scores_ref,
+    grad_ref, total_ref, w_out_ref, packed_in, attended_in, normed_in, exps_in, time_in,
+    grad_packed_out, pieces_out,
+    grad_attended_ref, grad_packed_ref, pieces_ref, packed_ref, attended_ref, normed_ref,
+    exps_ref, grad_scores_ref, sems, load_sems,
 ):
     features, tokens = attended_ref.shape
     depth = features // HEADS
+    part = tokens // LOADS
+    loads = [
+        [
+            pltpu.make_async_copy(
+                exps_in.at[head, pl.ds(low * part, part)],
+                exps_ref.at[head, pl.ds(low * part, part)],
+                load_sems.at[head, low],
+            )
+            for low in range(LOADS)
+        ]
+        for head in range(HEADS)
+    ]
+    load_packed = pltpu.make_async_copy(packed_in, packed_ref, sems.at[0])
+    load_attended = pltpu.make_async_copy(attended_in, attended_ref, sems.at[1])
+    load_normed = pltpu.make_async_copy(normed_in, normed_ref, sems.at[HEADS])
+    copy_time = pltpu.make_async_copy(time_in, pieces_ref.at[:, 0:1], sems.at[HEADS + 1])
+    store_packed = pltpu.make_async_copy(grad_packed_ref, grad_packed_out, sems.at[HEADS + 2])
+    store_pieces = pltpu.make_async_copy(pieces_ref, pieces_out, sems.at[HEADS + 3])
+    load_packed.start()
+    load_attended.start()
+    for load in loads[0]:
+        load.start()
+
     new = grad_ref[...].reshape(tokens, features)
     grad_attended_ref[...] = dot(w_out_ref[...], new, 1, 1).astype(BF16)
+    load_packed.wait()
+    load_attended.wait()
+    for load in loads[0]:
+        load.wait()
+    for load in loads[1] + loads[2] + loads[3]:
+        load.start()
+    load_normed.start()
+    copy_time.start()
     blocks = [slice(start, start + SPACE_BLOCK) for start in range(0, tokens, SPACE_BLOCK)]
 
     def finish(head, grad):
@@ -402,11 +496,11 @@
         scores = grad_scores_ref[head % 2]
         grad_packed_ref[at : at + depth, :] = (dot(keys, scores, 1, 0) * depth**-0.5).astype(BF16)
         grad_packed_ref[features + at : features + at + depth, :] = (
-            dot(query, scores, 1, 1) * math.log(2.0)
+            dot(scores, query.T, 1, 0).T * math.log(2.0)
         ).astype(BF16)
         grad_packed_ref[2 * features + at : 2 * features + at + depth, :] = dot(
-            grad, exps_ref[head], 1, 1
-        ).astype(BF16)
+            exps_ref[head], grad.T, 1, 0
+        ).T.astype(BF16)
 
     before = None
     for head in range(HEADS):
@@ -419,6 +513,9 @@
         grad = grad.astype(BF16)
         wide_grad = jnp.concatenate([grad, split_rows(inner)])
         wide_values = jnp.concatenate([values.T, jnp.full((tokens, 16), -1.0, BF16)], axis=1)
+        if head > 0:
+            for load in loads[head]:
+                load.wait()
         for cols in blocks:
             for low in range(0, tokens, KEY_TILE):
                 rows = slice(low, low + KEY_TILE)
@@ -426,32 +523,48 @@
                 grad_scores_ref[head % 2, rows, cols] = (
                     exps_ref[head, rows, cols].astype(F32) * centred
                 ).astype(BF16)
-        if before is not None:
-            finish(*before)
-        before = head, grad
-    finish(*before)
-    pieces_ref[:, 0:1] = time_ref[...]
+        finish(head, grad)
+    store_packed.start()
+    load_normed.wait()
     store_blocks(
         pieces_ref,
         1,
         dot(normed_ref[...], grad_packed_ref[...], 1, 1),
         dot(attended_ref[...], new, 1, 0),
     )
+    copy_time.wait()
+    store_pieces.start()
+    store_packed.wait()
+    store_pieces.wait()
 
 
 def run_space_backward(grad, normed, packed, attended, exps, totals, w_out, time_pieces):
     features, tokens = attended.shape
     parts, _, rows, _ = time_pieces.shape
-    normed, packed, attended, exps = in_vmem(normed, packed, attended, exps)
-    shapes = [pltpu.VMEM((3 * features, tokens), BF16), ((parts, 2, rows, features), BF16)]
+    packed, attended, normed, exps, time_pieces = in_hbm(
+        packed, attended, normed, exps, time_pieces
+    )
+    shapes = [pltpu.HBM((3 * features, tokens), BF16), ((parts, 2, rows, features), BF16)]
     return call(
         space_backward,
         shapes,
-        (grad, packed, attended, totals, w_out, normed, exps, time_pieces),
+        (grad, totals, w_out, packed, attended, normed, exps, time_pieces),
         14,
-        scratch=[((features, tokens), BF16), ((2, tokens, tokens), BF16)],
-        in_specs=[VMEM] * 8,
-        out_specs=[VMEM] * 2,
+        scratch=[
+            ((features, tokens), BF16),
+            ((3 * features, tokens), BF16),
+            ((parts, 2, rows, features), BF16),
+            ((3 * features, tokens), BF16),
+            ((features, tokens), BF16),
+            ((features, tokens), BF16),
+            ((HEADS, tokens, tokens), BF16),
+            ((2, tokens, tokens), BF16),
+            pltpu.SemaphoreType.DMA((HEADS + 4,)),
+            pltpu.SemaphoreType.DMA((HEADS, LOADS)),
+        ],
+        megabytes=32,
+        in_specs=[VMEM] * 3 + [ANY] * 5,
+        out_specs=[ANY] * 2,
     )
 
 
@@ -474,7 +587,6 @@
 def run_space_stream(grad, x, inverse, grad_packed, gain, w_qkv, parts):
     features, tokens = x.shape
     rows = grad.shape[1]
-    x, grad_packed = in_vmem(x, grad_packed)
     return call(
         space_stream,
         [((parts, tokens // (parts * rows) + 2, rows, features), BF16)],
@@ -582,6 +694,7 @@
         + [((features, 3 * features), F32), ((features, features), F32)] * 2,
         (incoming,),
         3,
+        megabytes=20,
     )
     return (hidden_home, grad_embedded) + tuple(weights)
 

time: 192 us -> 173 us (0.901)
  local copies, waits for them, and re-layouts: 32.1 us -> 4.08 us
  Pallas kernels: 45.4 us -> 54.8 us
    unnamed x73 -> x21, local copies, waits for them, and re-layouts: 29.4 us -> 0.68 us
    pallas_call x8, Pallas kernels: 45.4 us -> 54.8 us  [call(): pl.pallas_call(kernel, out_shape=[jax.ShapeDtypeStruct(*item) if isinstan...]
  transfers between devices with their start and end apart: 6 -> 6, of which waited for: 5 -> 5; matrix products, arithmetic and copies ran while one was open for 1% -> 1% of each run, Pallas kernels for 11% -> 18%
where the time goes in v4:
time: 173 us; the launch traced here: 172 us
  waiting for transfers between devices  61.1 us (35%)
  Pallas kernels  54.8 us (32%)
  starting transfers between devices  35.5 us (21%)
  blocking collectives  15.8 us (9%)
  local copies, waits for them, and re-layouts  4.08 us (2%)
    all_to_all x6, waiting for transfers between devices, exchange(): return lax.all_to_all(values, axes, split_axis=0, concat_axis=0, tiled=True)  61.1 us
    pallas_call x8, Pallas kernels, call(): pl.pallas_call(kernel, out_shape=[jax.ShapeDtypeStruct(*item) if isinstan...  54.8 us
    all_to_all x6, starting transfers between devices, exchange(): return lax.all_to_all(values, axes, split_axis=0, concat_axis=0, tiled=True)  35.5 us
    all_to_all x1, blocking collectives, exchange(): return lax.all_to_all(values, axes, split_axis=0, concat_axis=0, tiled=True)  15.8 us
  transfers between devices with their start and end apart: 6, of which 5 were waited for; matrix products, arithmetic and copies ran while one was open for 1% of the time, Pallas kernels for 18%

profile of v4, /device:TPU:1, one launch (start us, length us, event | category | flops | bytes accessed | tf_op | source)
XLA Modules:
  0.0 172.3 jit_solution(4818198136780740597)
XLA Ops:
  0.6 0.0 copy-start
  0.7 1.4 index_kernel.1
  2.1 8.3 %all-to-all-start = ((s32[8,5,128]{2,1,0:T(8,128)}), s32[8,5,128]{2,1,0:T(8,128)S(1)}, u32[]{:S(2)}, u32[]{:S(2)}) async-start(s32[8,5,128]{2,1,0:T(8,128)} %index_kernel.1), calls=%async_computation | async-start | bytes 65536 | tf_op jit(solution)/shard_map/all_to_all | solution.py:622
  10.4 0.9 copy_bitcast_fusion
  11.3 5.7 %all-to-all-done.index_ref = s32[8,5,128]{2,1,0:T(8,128)S(1)} async-done(((s32[8,5,128]{2,1,0:T(8,128)}), s32[8,5,128]{2,1,0:T(8,128)S(1)}, u32[]{:S(2)}, u32[]{:S(2)}) %all-to-all-start) | async-done | bytes 20512 | tf_op jit(solution)/shard_map/all_to_all | solution.py:622
  17.0 6.8 %all-to-all-start.1 = ((bf16[16,8,8,256]{3,2,1,0:T(8,128)(2,1)}), bf16[16,8,8,256]{3,2,1,0:T(8,128)(2,1)S(1)}, u32[]{:S(2)}, u32[]{:S(2)}) async-start(bf16[16,8,8,256]{3,2,1,0:T(8,128)(2,1)} %copy_bitcast_fusion), calls=%async_computation.1 | async-start | bytes 1048576 | tf_op jit(solution)/shard_map/all_to_all | solution.py:622
  23.8 0.6 copy.22.coord_table_ref
  24.5 20.1 %space_forward.1 = (bf16[128,8,256]{2,1,0:T(8,128)(2,1)}, f32[1,1024]{1,0:T(1,128)}, bf16[256,1024]{1,0:T(8,128)(2,1)}, f32[4,1,1024]{2,1,0:T(1,128)}, bf16[256,...) custom-call(s32[8,5,128]{2,1,0:T(8,128)} %copy-done.9, ...), custom_call_target="tpu_custom_call" | custom-call | flops 5000000000 | bytes 20000000 | tf_op jit(solution)/shard_map/space_forward/pallas_call | solution.py:26
  44.6 0.0 all-to-all-done.1.grad_ref.grad_in
  44.6 6.0 %all-to-all-start.2 = ((bf16[128,8,256]{2,1,0:T(8,128)(2,1)}), bf16[128,8,256]{2,1,0:T(8,128)(2,1)S(1)}, u32[]{:S(2)}, u32[]{:S(2)}) async-start(bf16[128,8,256]{2,1,0:T(8,128)(2,1)} %get-tuple-element.36), calls=%async_computation.2 | async-start | bytes 1048576 | tf_op jit(solution)/shard_map/all_to_all | solution.py:622
  50.6 0.0 copy-start.3
  50.6 0.0 copy-start.5
  50.6 2.5 %time_grad.1 = (bf16[1024,256]{1,0:T(8,128)(2,1)}, bf16[256,1024]{1,0:T(8,128)(2,1)}) custom-call(bf16[16,8,8,256]{3,2,1,0:T(8,128)(2,1)} %copy-done.7, bf16[256,256]{1,0:T(8,128)(2,1)} %w_out_ref.6), custom_call_target="tpu_custom_call" | custom-call | flops 1500000000 | bytes 6000000 | tf_op jit(solution)/shard_map/time_grad/pallas_call | solution.py:26
  53.1 11.2 %all-to-all-done.2 = bf16[128,8,256]{2,1,0:T(8,128)(2,1)S(1)} async-done(((bf16[128,8,256]{2,1,0:T(8,128)(2,1)}), bf16[128,8,256]{2,1,0:T(8,128)(2,1)S(1)}, u32[]{:S(2)}, u32[]{:S(2)}) %all-to-all-start.2) | async-done | bytes 524320 | tf_op jit(solution)/shard_map/all_to_all | solution.py:622
  64.3 0.0 copy-done.5
  64.3 7.7 %time_block.1 = (bf16[8,16,8,256]{3,2,1,0:T(8,128)(2,1)}, bf16[256,1024]{1,0:T(8,128)(2,1)}, bf16[768,1024]{1,0:T(8,128)(2,1)}, bf16[256,1024]{1,0:T(8,128)(2,1)}) custom-call(bf16[8,16,8,256]{3,2,1,0:T(8,128)(2,1)S(1)} %bitcast.13, bf16[16,8,8,256]{3,2,1,0:T(8,128)(2,1)} %copy-done.7, bf16[256,1024]{1,0:T(8,128)(2,1)} %get-tuple-element.38.grad_attended_in, ...), custom_call_target="tpu_custom_call" | custom-call | flops 5000000000 | bytes 20000000 | tf_op jit(solution)/shard_map/time_block/pallas_call | solution.py:26
  72.1 4.5 %all-to-all-start.3 = ((bf16[128,8,256]{2,1,0:T(8,128)(2,1)}), bf16[128,8,256]{2,1,0:T(8,128)(2,1)S(1)}, u32[]{:S(2)}, u32[]{:S(2)}) async-start(bf16[128,8,256]{2,1,0:T(8,128)(2,1)} %bitcast.6), calls=%async_computation.3 | async-start | bytes 1048576 | tf_op jit(solution)/shard_map/all_to_all | solution.py:622
  76.6 0.0 copy-start.4
  76.6 4.5 %time_rest.1 = (bf16[16,24,8,256]{3,2,1,0:T(8,128)(2,1)}, bf16[128,1,8,256]{3,2,1,0:T(8,128)(2,1)}) custom-call(bf16[8,16,8,256]{3,2,1,0:T(8,128)(2,1)} %bitcast.14, bf16[256,1024]{1,0:T(8,128)(2,1)} %get-tuple-element.39.normed_ref, bf16[768,1024]{1,0:T(8,128)(2,1)} %get-tuple-element.40.grad_packed_ref, bf16[256,1024]{1,0:T(8,128)(2,1)} %get-tuple-element.41.attended_ref, ...), custom_call_target="tpu_custom_call" | custom-call | flops 2500000000 | bytes 10000000 | tf_op jit(solution)/shard_map/time_rest/pallas_call | solution.py:26
  81.1 9.2 %all-to-all-done.3.grad_ref = bf16[128,8,256]{2,1,0:T(8,128)(2,1)S(1)} async-done(((bf16[128,8,256]{2,1,0:T(8,128)(2,1)}), bf16[128,8,256]{2,1,0:T(8,128)(2,1)S(1)}, u32[]{:S(2)}, u32[]{:S(2)}) %all-to-all-start.3) | async-done | bytes 524320 | tf_op jit(solution)/shard_map/all_to_all | solution.py:622
  90.3 13.4 %space_backward.1 = (bf16[768,1024]{1,0:T(8,128)(2,1)}, bf16[128,2,8,256]{3,2,1,0:T(8,128)(2,1)}) custom-call(bf16[128,8,256]{2,1,0:T(8,128)(2,1)S(1)} %all-to-all-done.3.grad_ref, f32[4,1,1024]{2,1,0:T(1,128)S(1)} %copy-done.6, bf16[256,256]{1,0:T(8,128)(2,1)S(1)} %copy-done.4, bf16[768,1024]{1,0:T(8,128)(2,1)} %get-tuple-element.48.packed_in, ...), custom_call_target="tpu_custom_call" | custom-call | flops 7000000000 | bytes 28000000 | tf_op jit(solution)/shard_map/space_backward/pallas_call | solution.py:26
  103.7 4.5 %all-to-all-start.4 = ((bf16[128,2,8,256]{3,2,1,0:T(8,128)(2,1)}), bf16[128,2,8,256]{3,2,1,0:T(8,128)(2,1)S(1)}, u32[]{:S(2)}, u32[]{:S(2)}) async-start(bf16[128,2,8,256]{3,2,1,0:T(8,128)(2,1)} %get-tuple-element.54), calls=%async_computation.4 | async-start | bytes 2097152 | tf_op jit(solution)/shard_map/all_to_all | solution.py:622
  108.2 3.6 %space_stream.1 = bf16[8,18,8,256]{3,2,1,0:T(8,128)(2,1)} custom-call(bf16[128,8,256]{2,1,0:T(8,128)(2,1)} %copy-done.1, bf16[256,1024]{1,0:T(8,128)(2,1)} %get-tuple-element.45.x_ref, f32[1,1024]{1,0:T(1,128)} %get-tuple-element.46.inverse_ref, bf16[768,1024]{1,0:T(8,128)(2,1)} %get-tuple-element.53.grad_packed_ref, f32[1,256]{1,0:T(1,128)} %bitcast.18, ...), custom_call_target="tpu_custom_call" | custom-call | flops 2000000000 | bytes 8000000 | tf_op jit(solution)/shard_map/space_stream/pallas_call | solution.py:26
  111.9 14.2 %all-to-all-done.4 = bf16[128,2,8,256]{3,2,1,0:T(8,128)(2,1)S(1)} async-done(((bf16[128,2,8,256]{3,2,1,0:T(8,128)(2,1)}), bf16[128,2,8,256]{3,2,1,0:T(8,128)(2,1)S(1)}, u32[]{:S(2)}, u32[]{:S(2)}) %all-to-all-start.4) | async-done | bytes 1048608 | tf_op jit(solution)/shard_map/all_to_all | solution.py:622
  126.1 0.2 convert_reduce_fusion
  126.3 0.6 broadcast_dynamic-update-slice_fusion.1
  126.9 15.8 %all_to_all.35 = bf16[8,18,8,256]{3,2,1,0:T(8,128)(2,1)S(1)} all-to-all(bf16[8,18,8,256]{3,2,1,0:T(8,128)(2,1)} %broadcast_dynamic-update-slice_fusion.1), channel_id=1, replica_groups=mesh['rounds'=16,'stab'=8] {'stab'}, dimensions={0} | all-to-all | bytes 1179648 | tf_op jit(solution)/shard_map/all_to_all | solution.py:622
  142.8 1.1 broadcast_dynamic-update-slice_fusion
  143.8 5.3 %all-to-all-start.6 = ((bf16[16,24,8,256]{3,2,1,0:T(8,128)(2,1)}), bf16[16,24,8,256]{3,2,1,0:T(8,128)(2,1)S(1)}, u32[]{:S(2)}, u32[]{:S(2)}) async-start(bf16[16,24,8,256]{3,2,1,0:T(8,128)(2,1)} %broadcast_dynamic-update-slice_fusion), calls=%async_computation.6 | async-start | bytes 3145728 | tf_op jit(solution)/shard_map/all_to_all | solution.py:622
  149.1 0.8 slice_bitcast_fusion
  150.0 20.7 %all-to-all-done.6.incoming_ref = bf16[16,24,8,256]{3,2,1,0:T(8,128)(2,1)S(1)} async-done(((bf16[16,24,8,256]{3,2,1,0:T(8,128)(2,1)}), bf16[16,24,8,256]{3,2,1,0:T(8,128)(2,1)S(1)}, u32[]{:S(2)}, u32[]{:S(2)}) %all-to-all-start.6) | async-done | bytes 1572896 | tf_op jit(solution)/shard_map/all_to_all | solution.py:622
  170.7 1.6 unpack.1
  (17 shorter events, 0.0 us)
Async XLA Ops:
  0.6 9.8 %copy-start = (bf16[8,128,256]{2,1,0:T(8,128)(2,1)S(1)}, bf16[8,128,256]{2,1,0:T(8,128)(2,1)}, u32[]{:S(2)}) copy-start(bf16[8,128,256]{2,1,0:T(8,128)(2,1)} %param.27) | copy-start | bytes 1572868
  0.6 23.2 %copy-start.8 = (bf16[2,42,256]{2,0,1:T(2,128)(2,1)S(1)}, bf16[2,42,256]{2,0,1:T(2,128)(2,1)}, u32[]{:S(2)}) copy-start(bf16[2,42,256]{2,0,1:T(2,128)(2,1)} %param.19) | copy-start | bytes 129028
  2.1 14.9 %all-to-all-start = ((s32[8,5,128]{2,1,0:T(8,128)}), s32[8,5,128]{2,1,0:T(8,128)S(1)}, u32[]{:S(2)}, u32[]{:S(2)}) async-start(s32[8,5,128]{2,1,0:T(8,128)} %index_kernel.1), calls=%async_computation | async-start | bytes 65536 | tf_op jit(solution)/shard_map/all_to_all | solution.py:622
  17.0 7.5 %copy-start.9 = (s32[8,5,128]{2,1,0:T(8,128)}, s32[8,5,128]{2,1,0:T(8,128)S(1)}, u32[]{:S(2)}) copy-start(s32[8,5,128]{2,1,0:T(8,128)S(1)} %all-to-all-done.index_ref) | copy-start | bytes 61444
  17.0 27.6 %all-to-all-start.1 = ((bf16[16,8,8,256]{3,2,1,0:T(8,128)(2,1)}), bf16[16,8,8,256]{3,2,1,0:T(8,128)(2,1)S(1)}, u32[]{:S(2)}, u32[]{:S(2)}) async-start(bf16[16,8,8,256]{3,2,1,0:T(8,128)(2,1)} %copy_bitcast_fusion), calls=%async_computation.1 | async-start | bytes 1048576 | tf_op jit(solution)/shard_map/all_to_all | solution.py:622
  44.6 6.0 %copy-start.7 = (bf16[16,8,8,256]{3,2,1,0:T(8,128)(2,1)}, bf16[16,8,8,256]{3,2,1,0:T(8,128)(2,1)S(1)}, u32[]{:S(2)}) copy-start(bf16[16,8,8,256]{3,2,1,0:T(8,128)(2,1)S(1)} %all-to-all-done.1.grad_ref.grad_in) | copy-start | bytes 1572868
  44.6 19.7 %all-to-all-start.2 = ((bf16[128,8,256]{2,1,0:T(8,128)(2,1)}), bf16[128,8,256]{2,1,0:T(8,128)(2,1)S(1)}, u32[]{:S(2)}, u32[]{:S(2)}) async-start(bf16[128,8,256]{2,1,0:T(8,128)(2,1)} %get-tuple-element.36), calls=%async_computation.2 | async-start | bytes 1048576 | tf_op jit(solution)/shard_map/all_to_all | solution.py:622
  50.6 13.7 %copy-start.3 = (bf16[256,768]{1,0:T(8,128)(2,1)S(1)}, bf16[256,768]{1,0:T(8,128)(2,1)}, u32[]{:S(2)}) copy-start(bf16[256,768]{1,0:T(8,128)(2,1)} %w_qkv_ref.4) | copy-start | bytes 1179652
  50.6 13.7 %copy-start.5 = (f32[256]{0:T(256)S(1)}, f32[256]{0:T(256)}, u32[]{:S(2)}) copy-start(f32[256]{0:T(256)} %param.24) | copy-start | bytes 3076
  64.3 7.8 %copy-start.2 = (bf16[128,8,256]{2,1,0:T(8,128)(2,1)}, bf16[128,8,256]{2,1,0:T(8,128)(2,1)S(1)}, u32[]{:S(2)}) copy-start(bf16[128,8,256]{2,1,0:T(8,128)(2,1)S(1)} %all-to-all-done.2) | copy-start | bytes 1572868
  72.1 18.3 %all-to-all-start.3 = ((bf16[128,8,256]{2,1,0:T(8,128)(2,1)}), bf16[128,8,256]{2,1,0:T(8,128)(2,1)S(1)}, u32[]{:S(2)}, u32[]{:S(2)}) async-start(bf16[128,8,256]{2,1,0:T(8,128)(2,1)} %bitcast.6), calls=%async_computation.3 | async-start | bytes 1048576 | tf_op jit(solution)/shard_map/all_to_all | solution.py:622
  76.6 13.7 %copy-start.4 = (bf16[256,256]{1,0:T(8,128)(2,1)S(1)}, bf16[256,256]{1,0:T(8,128)(2,1)}, u32[]{:S(2)}) copy-start(bf16[256,256]{1,0:T(8,128)(2,1)} %w_out_ref.7) | copy-start | bytes 393220
  76.6 13.7 %copy-start.6 = (f32[4,1,1024]{2,1,0:T(1,128)S(1)}, f32[4,1,1024]{2,1,0:T(1,128)}, u32[]{:S(2)}) copy-start(f32[4,1,1024]{2,1,0:T(1,128)} %get-tuple-element.47.total_ref) | copy-start | bytes 49156
  90.3 13.4 %copy-start.1 = (bf16[128,8,256]{2,1,0:T(8,128)(2,1)}, bf16[128,8,256]{2,1,0:T(8,128)(2,1)S(1)}, u32[]{:S(2)}) copy-start(bf16[128,8,256]{2,1,0:T(8,128)(2,1)S(1)} %all-to-all-done.3.grad_ref) | copy-start | bytes 1572868
  103.7 22.3 %all-to-all-start.4 = ((bf16[128,2,8,256]{3,2,1,0:T(8,128)(2,1)}), bf16[128,2,8,256]{3,2,1,0:T(8,128)(2,1)S(1)}, u32[]{:S(2)}, u32[]{:S(2)}) async-start(bf16[128,2,8,256]{3,2,1,0:T(8,128)(2,1)} %get-tuple-element.54), calls=%async_computation.4 | async-start | bytes 2097152 | tf_op jit(solution)/shard_map/all_to_all | solution.py:622
  143.8 26.9 %all-to-all-start.6 = ((bf16[16,24,8,256]{3,2,1,0:T(8,128)(2,1)}), bf16[16,24,8,256]{3,2,1,0:T(8,128)(2,1)S(1)}, u32[]{:S(2)}, u32[]{:S(2)}) async-start(bf16[16,24,8,256]{3,2,1,0:T(8,128)(2,1)} %broadcast_dynamic-update-slice_fusion), calls=%async_computation.6 | async-start | bytes 3145728 | tf_op jit(solution)/shard_map/all_to_all | solution.py:622

commit v5 on v4

--- a/solution.py
+++ b/solution.py
@@ -419,9 +419,7 @@
             rows_ref[part, at, :] = rows_ref[part, at, :] + branch[cols, half]
     for part, half in enumerate(halves):
         hidden = rows_ref[part].reshape(round_parts, stab_parts, stabs, lanes)
-        hidden_ref[:, :stab_parts, :, half] = hidden.astype(BF16)
-    groups = hidden_ref.shape[1] - stab_parts
-    hidden_ref[:, stab_parts:] = jnp.zeros((round_parts, groups, stabs, features), BF16)
+        hidden_ref[:, :, :, half] = hidden.astype(BF16)
     store_blocks(
         pieces_ref,
         0,
@@ -437,7 +435,7 @@
     return call(
         time_rest,
         [
-            ((round_parts, 3 * stab_parts, stabs, features), BF16),
+            ((round_parts, stab_parts, stabs, features), BF16),
             ((parts, 1, 4 * features // parts, features), BF16),
         ],
         (middle, normed, grad_packed, attended, grad_rows, w_out),
@@ -569,49 +567,54 @@
 
 
 def space_stream(
-    grad_ref, x_ref, inverse_ref, grad_packed_ref, gain_ref, w_qkv_ref, out_ref
+    me_ref, grad_ref, x_ref, inverse_ref, grad_packed_ref, gain_ref, w_qkv_ref, *rest
 ):
+    out_refs, rows_ref = rest[:-1], rest[-1]
     features, tokens = x_ref.shape
     grad_normed = dot(w_qkv_ref[...], grad_packed_ref[...], 1, 0)
     grad_stream = norm_columns_backward(
         x_ref[...].astype(F32), as_column(gain_ref[...]), inverse_ref[...], grad_normed
     )
-    parts, groups, rows, _ = out_ref.shape
     grad_new = grad_ref[...].reshape(tokens, features).astype(F32)
-    result = (grad_new + grad_stream.T).astype(BF16)
-    here = tokens // (parts * rows)
-    out_ref[:, :here] = result.reshape(parts, here, rows, features)
-    out_ref[:, here:] = jnp.zeros((parts, groups - here, rows, features), BF16)
-
-
-def run_space_stream(grad, x, inverse, grad_packed, gain, w_qkv, parts):
+    rows_ref[...] = (grad_new + grad_stream.T).astype(BF16)
+    rows = tokens // len(out_refs)
+    for step, out_ref in enumerate(out_refs):
+        at = pl.multiple_of((me_ref[0] ^ step) * rows, rows)
+        out_ref[...] = rows_ref[pl.ds(at, rows), :]
+
+
+SMEM = pl.BlockSpec(memory_space=pltpu.SMEM)
+
+
+def run_space_stream(me, grad, x, inverse, grad_packed, gain, w_qkv, parts):
     features, tokens = x.shape
-    rows = grad.shape[1]
     return call(
         space_stream,
-        [((parts, tokens // (parts * rows) + 2, rows, features), BF16)],
-        (grad, x, inverse, grad_packed, gain, w_qkv),
+        [((tokens // parts, features), BF16)] * parts,
+        (me, grad, x, inverse, grad_packed, gain, w_qkv),
         4,
-    )[0]
-
-
-def unpack(
-    incoming_ref, hidden_ref, space_qkv_ref, space_out_ref, time_qkv_ref, time_out_ref
-):
-    round_parts, _, stabs, features = incoming_ref.shape
-    here = hidden_ref.shape[0]
-    for block in range(round_parts):
-        cols = slice(block * stabs, (block + 1) * stabs)
-        hidden_ref[:, cols, :] = incoming_ref[block, :here]
-    count = round_parts // 4
+        scratch=[((tokens, features), BF16)],
+        in_specs=[SMEM] + [VMEM] * 6,
+        out_specs=[VMEM] * parts,
+    )
+
+
+def place_blocks(me_ref, *refs):
+    in_refs, out_ref = refs[:-1], refs[-1]
+    for step, in_ref in enumerate(in_refs):
+        out_ref[me_ref[0] ^ step] = in_ref[...]
+
+
+def unpack(pieces_ref, space_qkv_ref, space_out_ref, time_qkv_ref, time_out_ref):
+    features = space_out_ref.shape[0]
+    count = pieces_ref.shape[0] // 4
     for j in range(4):
-        pieces = incoming_ref[j * count : (j + 1) * count, here:].astype(F32)
-        pieces = pieces.reshape(count, here, 2, stabs, features)
+        pieces = pieces_ref[j * count : (j + 1) * count].astype(F32)
         for kind, qkv_ref, out_ref in (
             (0, time_qkv_ref, time_out_ref),
             (1, space_qkv_ref, space_out_ref),
         ):
-            block = pieces[:, :, kind].reshape(features, features)
+            block = pieces[:, kind].reshape(features, features)
             if j < 3:
                 qkv_ref[:, j * features : (j + 1) * features] = block
             else:
@@ -620,6 +623,10 @@
 
 def exchange(values, axes):
     return lax.all_to_all(values, axes, split_axis=0, concat_axis=0, tiled=True)
+
+
+def to_pair(block, step, parts):
+    return lax.ppermute(block, "stab", [(i, i ^ step) for i in range(parts)])
 
 
 def on_device(
@@ -672,28 +679,40 @@
     hidden, time_pieces = run_time_rest(
         middle_time, normed_t, grad_packed_t, attended_t, grad_rows, w_out_time
     )
+    hidden, grad_space = lax.optimization_barrier((hidden, grad_space))
+    hidden_home = exchange(hidden, "rounds")
     grad_packed, pieces = run_space_backward(
         grad_space, normed, packed, attended, exps, totals, w_out_space, time_pieces
     )
+    pieces, grad_packed, hidden_home = lax.optimization_barrier((pieces, grad_packed, hidden_home))
     sources = exchange(pieces, ("rounds", "stab"))
-    outgoing = run_space_stream(
-        grad_space, x, inverse, grad_packed, gain_s, w_qkv_space, stab_parts
-    )
+    me = lax.axis_index("stab").astype(jnp.int32).reshape(1)
+    blocks = list(
+        run_space_stream(
+            me, grad_space, x, inverse, grad_packed, gain_s, w_qkv_space, stab_parts
+        )
+    )
+    blocks[1:] = [to_pair(blocks[step], step, stab_parts) for step in range(1, stab_parts)]
+    sources, *blocks = lax.optimization_barrier((sources, *blocks))
     scaling = 1.0 / math.sqrt(parts * rounds_here * stabs_here)
     summed = (jnp.sum(sources.astype(F32), axis=0) * scaling).astype(BF16)
-    here = outgoing.shape[1] - summed.shape[0]
-    spread = jnp.broadcast_to(summed[None], (stab_parts,) + summed.shape)
-    incoming = exchange(lax.dynamic_update_slice(outgoing, spread, (0, here, 0, 0)), "stab")
-    grad_embedded = incoming[:, :here].reshape(grad_hidden.shape)
-    gathered = incoming[:, here:].reshape(1, 2 * stab_parts, stabs_time, features)
-    spread = jnp.broadcast_to(gathered, (round_parts,) + gathered.shape[1:])
-    incoming = exchange(lax.dynamic_update_slice(hidden, spread, (0, stab_parts, 0, 0)), "rounds")
-    hidden_home, *weights = call(
+    gathered = exchange(
+        jnp.broadcast_to(summed[None], (parts,) + summed.shape), ("rounds", "stab")
+    )
+    grad_embedded = call(
+        place_blocks,
+        [(grad_hidden.shape, BF16)],
+        (me, *blocks),
+        2,
+        in_specs=[SMEM] + [VMEM] * stab_parts,
+        out_specs=[VMEM],
+    )[0]
+    hidden_home = jnp.swapaxes(hidden_home, 0, 1).reshape(grad_hidden.shape)
+    weights = call(
         unpack,
-        [(grad_hidden.shape, BF16)]
-        + [((features, 3 * features), F32), ((features, features), F32)] * 2,
-        (incoming,),
-        3,
+        [((features, 3 * features), F32), ((features, features), F32)] * 2,
+        (gathered,),
+        2,
         megabytes=20,
     )
     return (hidden_home, grad_embedded) + tuple(weights)

time: 173 us -> 169 us (0.977)
  starting transfers between devices: 35.5 us -> 59.2 us
  blocking collectives: 15.8 us -> 0 us
  waiting for transfers between devices: 61.1 us -> 49 us
    all_to_all x6 -> x7, waiting for transfers between devices: 61.1 us -> 41.7 us  [exchange(): return lax.all_to_all(values, axes, split_axis=0, concat_axis=0, tiled=True)]
    all_to_all x1 -> x0, blocking collectives: 15.8 us -> none  [exchange(): return lax.all_to_all(values, axes, split_axis=0, concat_axis=0, tiled=True)]
    ppermute x0 -> x7, starting transfers between devices: none -> 14.2 us  [to_pair(): return lax.ppermute(block, 'stab', [(i, i ^ step) for i in range(parts)])]
    all_to_all x6 -> x7, starting transfers between devices: 35.5 us -> 45 us  [exchange(): return lax.all_to_all(values, axes, split_axis=0, concat_axis=0, tiled=True)]
    ppermute x0 -> x7, waiting for transfers between devices: none -> 7.24 us  [to_pair(): return lax.ppermute(block, 'stab', [(i, i ^ step) for i in range(parts)])]
    pallas_call x8 -> x9, Pallas kernels: 54.8 us -> 55.9 us  [call(): pl.pallas_call(kernel, out_shape=[jax.ShapeDtypeStruct(*item) if isinstan...]
  transfers between devices with their start and end apart: 6 -> 14, of which waited for: 5 -> 8; matrix products, arithmetic and copies ran while one was open for 1% -> 1% of each run, Pallas kernels for 18% -> 27%
where the time goes in v5:
time: 169 us
  starting transfers between devices  59.2 us (35%)
  Pallas kernels  55.9 us (33%)
  waiting for transfers between devices  49 us (29%)
  local copies, waits for them, and re-layouts  3.47 us (2%)
    pallas_call x9, Pallas kernels, call(): pl.pallas_call(kernel, out_shape=[jax.ShapeDtypeStruct(*item) if isinstan...  55.9 us
    all_to_all x7, starting transfers between devices, exchange(): return lax.all_to_all(values, axes, split_axis=0, concat_axis=0, tiled=True)  45 us
    all_to_all x7, waiting for transfers between devices, exchange(): return lax.all_to_all(values, axes, split_axis=0, concat_axis=0, tiled=True)  41.7 us
    ppermute x7, starting transfers between devices, to_pair(): return lax.ppermute(block, 'stab', [(i, i ^ step) for i in range(parts)])  14.2 us
    ppermute x7, waiting for transfers between devices, to_pair(): return lax.ppermute(block, 'stab', [(i, i ^ step) for i in range(parts)])  7.24 us
  transfers between devices with their start and end apart: 14, of which 8 were waited for; matrix products, arithmetic and copies ran while one was open for 1% of the time, Pallas kernels for 27%

profile of v5, /device:TPU:1, one launch (start us, length us, event | category | flops | bytes accessed | tf_op | source)
XLA Modules:
  0.0 168.6 jit_solution(5944335720249489592)
XLA Ops:
  0.7 1.4 index_kernel.1
  2.1 8.3 %all-to-all-start = ((s32[8,5,128]{2,1,0:T(8,128)}), s32[8,5,128]{2,1,0:T(8,128)S(1)}, u32[]{:S(2)}, u32[]{:S(2)}) async-start(s32[8,5,128]{2,1,0:T(8,128)} %index_kernel.1), calls=%async_computation | async-start | bytes 65536 | tf_op jit(solution)/shard_map/all_to_all | solution.py:625
  10.4 0.9 copy_bitcast_fusion.1
  11.3 5.7 %all-to-all-done.index_ref = s32[8,5,128]{2,1,0:T(8,128)S(1)} async-done(((s32[8,5,128]{2,1,0:T(8,128)}), s32[8,5,128]{2,1,0:T(8,128)S(1)}, u32[]{:S(2)}, u32[]{:S(2)}) %all-to-all-start) | async-done | bytes 20512 | tf_op jit(solution)/shard_map/all_to_all | solution.py:625
  17.0 6.8 %all-to-all-start.1 = ((bf16[16,8,8,256]{3,2,1,0:T(8,128)(2,1)}), bf16[16,8,8,256]{3,2,1,0:T(8,128)(2,1)S(1)}, u32[]{:S(2)}, u32[]{:S(2)}) async-start(bf16[16,8,8,256]{3,2,1,0:T(8,128)(2,1)} %copy_bitcast_fusion.1), calls=%async_computation.1 | async-start | bytes 1048576 | tf_op jit(solution)/shard_map/all_to_all | solution.py:625
  24.5 20.1 %space_forward.1 = (bf16[128,8,256]{2,1,0:T(8,128)(2,1)}, f32[1,1024]{1,0:T(1,128)}, bf16[256,1024]{1,0:T(8,128)(2,1)}, f32[4,1,1024]{2,1,0:T(1,128)}, bf16[256,...) custom-call(s32[8,5,128]{2,1,0:T(8,128)} %copy-done.9, ...), custom_call_target="tpu_custom_call" | custom-call | flops 5000000000 | bytes 20000000 | tf_op jit(solution)/shard_map/space_forward/pallas_call | solution.py:26
  44.6 6.0 %all-to-all-start.2 = ((bf16[128,8,256]{2,1,0:T(8,128)(2,1)}), bf16[128,8,256]{2,1,0:T(8,128)(2,1)S(1)}, u32[]{:S(2)}, u32[]{:S(2)}) async-start(bf16[128,8,256]{2,1,0:T(8,128)(2,1)} %get-tuple-element.57), calls=%async_computation.2 | async-start | bytes 1048576 | tf_op jit(solution)/shard_map/all_to_all | solution.py:625
  50.7 2.5 %time_grad.1 = (bf16[1024,256]{1,0:T(8,128)(2,1)}, bf16[256,1024]{1,0:T(8,128)(2,1)}) custom-call(bf16[16,8,8,256]{3,2,1,0:T(8,128)(2,1)} %copy-done.7, bf16[256,256]{1,0:T(8,128)(2,1)} %w_out_ref.6), custom_call_target="tpu_custom_call" | custom-call | flops 1500000000 | bytes 6000000 | tf_op jit(solution)/shard_map/time_grad/pallas_call | solution.py:26
  53.2 11.2 %all-to-all-done.2 = bf16[128,8,256]{2,1,0:T(8,128)(2,1)S(1)} async-done(((bf16[128,8,256]{2,1,0:T(8,128)(2,1)}), bf16[128,8,256]{2,1,0:T(8,128)(2,1)S(1)}, u32[]{:S(2)}, u32[]{:S(2)}) %all-to-all-start.2) | async-done | bytes 524320 | tf_op jit(solution)/shard_map/all_to_all | solution.py:625
  64.4 7.7 %time_block.1 = (bf16[8,16,8,256]{3,2,1,0:T(8,128)(2,1)}, bf16[256,1024]{1,0:T(8,128)(2,1)}, bf16[768,1024]{1,0:T(8,128)(2,1)}, bf16[256,1024]{1,0:T(8,128)(2,1)}) custom-call(bf16[8,16,8,256]{3,2,1,0:T(8,128)(2,1)S(1)} %bitcast.16, bf16[16,8,8,256]{3,2,1,0:T(8,128)(2,1)} %copy-done.7, bf16[256,1024]{1,0:T(8,128)(2,1)} %get-tuple-element.59.grad_attended_in, ...), custom_call_target="tpu_custom_call" | custom-call | flops 5000000000 | bytes 20000000 | tf_op jit(solution)/shard_map/time_block/pallas_call | solution.py:26
  72.0 4.5 %all-to-all-start.3 = ((bf16[128,8,256]{2,1,0:T(8,128)(2,1)}), bf16[128,8,256]{2,1,0:T(8,128)(2,1)S(1)}, u32[]{:S(2)}, u32[]{:S(2)}) async-start(bf16[128,8,256]{2,1,0:T(8,128)(2,1)} %bitcast.6), calls=%async_computation.3 | async-start | bytes 1048576 | tf_op jit(solution)/shard_map/all_to_all | solution.py:625
  76.6 4.0 %time_rest.1 = (bf16[16,8,8,256]{3,2,1,0:T(8,128)(2,1)}, bf16[128,1,8,256]{3,2,1,0:T(8,128)(2,1)}) custom-call(bf16[8,16,8,256]{3,2,1,0:T(8,128)(2,1)} %bitcast.17, bf16[256,1024]{1,0:T(8,128)(2,1)} %get-tuple-element.60.normed_ref, bf16[768,1024]{1,0:T(8,128)(2,1)} %get-tuple-element.61.grad_packed_ref, bf16[256,1024]{1,0:T(8,128)(2,1)} %get-tuple-element.62.attended_ref, ...), custom_call_target="tpu_custom_call" | custom-call | flops 2500000000 | bytes 10000000 | tf_op jit(solution)/shard_map/time_rest/pallas_call | solution.py:26
  80.6 9.7 %all-to-all-done.3.grad_ref = bf16[128,8,256]{2,1,0:T(8,128)(2,1)S(1)} async-done(((bf16[128,8,256]{2,1,0:T(8,128)(2,1)}), bf16[128,8,256]{2,1,0:T(8,128)(2,1)S(1)}, u32[]{:S(2)}, u32[]{:S(2)}) %all-to-all-start.3) | async-done | bytes 524320 | tf_op jit(solution)/shard_map/all_to_all | solution.py:625
  90.3 4.2 %all-to-all-start.4 = ((bf16[16,8,8,256]{3,2,1,0:T(8,128)(2,1)}), bf16[16,8,8,256]{3,2,1,0:T(8,128)(2,1)S(1)}, u32[]{:S(2)}, u32[]{:S(2)}) async-start(bf16[16,8,8,256]{3,2,1,0:T(8,128)(2,1)} %get-tuple-element.75), calls=%async_computation.4 | async-start | bytes 1048576 | tf_op jit(solution)/shard_map/all_to_all | solution.py:625
  94.5 13.3 %space_backward.1 = (bf16[768,1024]{1,0:T(8,128)(2,1)}, bf16[128,2,8,256]{3,2,1,0:T(8,128)(2,1)}) custom-call(bf16[128,8,256]{2,1,0:T(8,128)(2,1)S(1)} %all-to-all-done.3.grad_ref, f32[4,1,1024]{2,1,0:T(1,128)S(1)} %copy-done.6, bf16[256,256]{1,0:T(8,128)(2,1)S(1)} %copy-done.4, bf16[768,1024]{1,0:T(8,128)(2,1)} %get-tuple-element.68.packed_in, ...), custom_call_target="tpu_custom_call" | custom-call | flops 7000000000 | bytes 28000000 | tf_op jit(solution)/shard_map/space_backward/pallas_call | solution.py:26
  107.8 5.6 %all-to-all-start.5 = ((bf16[128,2,8,256]{3,2,1,0:T(8,128)(2,1)}), bf16[128,2,8,256]{3,2,1,0:T(8,128)(2,1)S(1)}, u32[]{:S(2)}, u32[]{:S(2)}) async-start(bf16[128,2,8,256]{3,2,1,0:T(8,128)(2,1)} %get-tuple-element.77), calls=%async_computation.5 | async-start | bytes 2097152 | tf_op jit(solution)/shard_map/all_to_all | solution.py:625
  113.5 3.6 %space_stream.1 = (bf16[128,256]{1,0:T(8,128)(2,1)}, bf16[128,256]{1,0:T(8,128)(2,1)}, bf16[128,256]{1,0:T(8,128)(2,1)}, bf16[128,256]{1,0:T(8,128)(2,1)}, bf16[...) custom-call(s32[1]{0:T(128)} %bitcast.9.me_ref, ...), custom_call_target="tpu_custom_call" | custom-call | flops 2000000000 | bytes 8000000 | tf_op jit(solution)/shard_map/space_stream/pallas_call | solution.py:26
  117.1 3.3 %collective-permute-start = (bf16[128,256]{1,0:T(8,128)(2,1)}, bf16[128,256]{1,0:T(8,128)(2,1)S(1)}, u32[]{:S(2)}, u32[]{:S(2)}) collective-permute-start(bf16[128,256]{1,0:T(8,128)(2,1)} %get-tuple-element.82), channel_id=1, source_target_pairs={{0,1},{1,0},{2,3},{3,2},{4,5},{5,4},{6,7},{7,6},{8,9},{9,8},{10,11... | collective-permute-start | bytes 196616 | tf_op jit(solution)/shard_map/ppermute | solution.py:629
  120.4 1.2 collective-permute-start.1
  121.6 2.8 %collective-permute-start.3 = (bf16[128,256]{1,0:T(8,128)(2,1)}, bf16[128,256]{1,0:T(8,128)(2,1)S(1)}, u32[]{:S(2)}, u32[]{:S(2)}) collective-permute-start(bf16[128,256]{1,0:T(8,128)(2,1)} %get-tuple-element.85), channel_id=1, source_target_pairs={{0,4},{1,5},{2,6},{3,7},{4,0},{5,1},{6,2},{7,3},{8,12},{9,13},{10,... | collective-permute-start | bytes 196616 | tf_op jit(solution)/shard_map/ppermute | solution.py:629
  124.5 2.7 %collective-permute-start.4 = (bf16[128,256]{1,0:T(8,128)(2,1)}, bf16[128,256]{1,0:T(8,128)(2,1)S(1)}, u32[]{:S(2)}, u32[]{:S(2)}) collective-permute-start(bf16[128,256]{1,0:T(8,128)(2,1)} %get-tuple-element.86), channel_id=1, source_target_pairs={{0,5},{1,4},{2,7},{3,6},{4,1},{5,0},{6,3},{7,2},{8,13},{9,12},{10,... | collective-permute-start | bytes 196616 | tf_op jit(solution)/shard_map/ppermute | solution.py:629
  127.2 1.3 collective-permute-done.refs_1_
  128.5 1.8 %collective-permute-start.5 = (bf16[128,256]{1,0:T(8,128)(2,1)}, bf16[128,256]{1,0:T(8,128)(2,1)S(1)}, u32[]{:S(2)}, u32[]{:S(2)}) collective-permute-start(bf16[128,256]{1,0:T(8,128)(2,1)} %get-tuple-element.87), channel_id=1, source_target_pairs={{0,6},{1,7},{2,4},{3,5},{4,2},{5,3},{6,0},{7,1},{8,14},{9,15},{10,... | collective-permute-start | bytes 196616 | tf_op jit(solution)/shard_map/ppermute | solution.py:629
  130.3 2.3 %collective-permute-start.6 = (bf16[128,256]{1,0:T(8,128)(2,1)}, bf16[128,256]{1,0:T(8,128)(2,1)S(1)}, u32[]{:S(2)}, u32[]{:S(2)}) collective-permute-start(bf16[128,256]{1,0:T(8,128)(2,1)} %get-tuple-element.88), channel_id=1, source_target_pairs={{0,7},{1,6},{2,5},{3,4},{4,3},{5,2},{6,1},{7,0},{8,15},{9,14},{10,... | collective-permute-start | bytes 196616 | tf_op jit(solution)/shard_map/ppermute | solution.py:629
  133.1 3.8 %collective-permute-done.4.refs_5_ = bf16[128,256]{1,0:T(8,128)(2,1)S(1)} collective-permute-done((bf16[128,256]{1,0:T(8,128)(2,1)}, bf16[128,256]{1,0:T(8,128)(2,1)S(1)}, u32[]{:S(2)}, u32[]{:S(2)}) %collective-permute-start.4) | collective-permute-done | bytes 65568 | tf_op jit(solution)/shard_map/ppermute | solution.py:629
  136.9 1.7 collective-permute-done.6.refs_7_
  138.7 1.1 broadcast_in_dim.2
  139.8 9.5 %all-to-all-start.6 = ((bf16[128,2,8,256]{3,2,1,0:T(8,128)(2,1)}), bf16[128,2,8,256]{3,2,1,0:T(8,128)(2,1)S(1)}, u32[]{:S(2)}, u32[]{:S(2)}) async-start(bf16[128,2,8,256]{3,2,1,0:T(8,128)(2,1)} %broadcast_in_dim.2), calls=%async_computation.6 | async-start | bytes 2097152 | tf_op jit(solution)/shard_map/all_to_all | solution.py:625
  149.4 0.8 copy_bitcast_fusion
  150.2 1.9 %place_blocks.1 = bf16[8,128,256]{2,1,0:T(8,128)(2,1)} custom-call(s32[1]{0:T(128)} %bitcast.9.me_ref, bf16[128,256]{1,0:T(8,128)(2,1)} %get-tuple-element.89.refs_0_, bf16[128,256]{1,0:T(8,128)(2,1)} %copy-done.10, bf16[128,256]{1,0:T(8,128)(2,1)} %copy-done.11, bf16[128,256]{1,0:T(8,128)(2,1)} %copy-done.12, bf16[128,256]{1,0:T(8,128)(2,1)} %copy-done.13, ...), custom_call_target="tpu_custom_call" | custom-call | flops 1000000000 | bytes 4000000 | tf_op jit(solution)/shard_map/place_blocks/pallas_call | solution.py:26
  152.1 15.1 %all-to-all-done.6.pieces_ref = bf16[128,2,8,256]{3,2,1,0:T(8,128)(2,1)S(1)} async-done(((bf16[128,2,8,256]{3,2,1,0:T(8,128)(2,1)}), bf16[128,2,8,256]{3,2,1,0:T(8,128)(2,1)S(1)}, u32[]{:S(2)}, u32[]{:S(2)}) %all-to-all-start.6) | async-done | bytes 1048608 | tf_op jit(solution)/shard_map/all_to_all | solution.py:625
  167.2 1.4 unpack.1
  (45 shorter events, 1.5 us)
Async XLA Ops:
  0.6 9.8 %copy-start = (bf16[8,128,256]{2,1,0:T(8,128)(2,1)S(1)}, bf16[8,128,256]{2,1,0:T(8,128)(2,1)}, u32[]{:S(2)}) copy-start(bf16[8,128,256]{2,1,0:T(8,128)(2,1)} %param.27) | copy-start | bytes 1572868
  0.6 23.2 %copy-start.8 = (bf16[2,42,256]{2,0,1:T(2,128)(2,1)S(1)}, bf16[2,42,256]{2,0,1:T(2,128)(2,1)}, u32[]{:S(2)}) copy-start(bf16[2,42,256]{2,0,1:T(2,128)(2,1)} %param.19) | copy-start | bytes 129028
  2.1 14.9 %all-to-all-start = ((s32[8,5,128]{2,1,0:T(8,128)}), s32[8,5,128]{2,1,0:T(8,128)S(1)}, u32[]{:S(2)}, u32[]{:S(2)}) async-start(s32[8,5,128]{2,1,0:T(8,128)} %index_kernel.1), calls=%async_computation | async-start | bytes 65536 | tf_op jit(solution)/shard_map/all_to_all | solution.py:625
  17.0 7.5 %copy-start.9 = (s32[8,5,128]{2,1,0:T(8,128)}, s32[8,5,128]{2,1,0:T(8,128)S(1)}, u32[]{:S(2)}) copy-start(s32[8,5,128]{2,1,0:T(8,128)S(1)} %all-to-all-done.index_ref) | copy-start | bytes 61444
  17.0 27.6 %all-to-all-start.1 = ((bf16[16,8,8,256]{3,2,1,0:T(8,128)(2,1)}), bf16[16,8,8,256]{3,2,1,0:T(8,128)(2,1)S(1)}, u32[]{:S(2)}, u32[]{:S(2)}) async-start(bf16[16,8,8,256]{3,2,1,0:T(8,128)(2,1)} %copy_bitcast_fusion.1), calls=%async_computation.1 | async-start | bytes 1048576 | tf_op jit(solution)/shard_map/all_to_all | solution.py:625
  44.6 6.0 %copy-start.7 = (bf16[16,8,8,256]{3,2,1,0:T(8,128)(2,1)}, bf16[16,8,8,256]{3,2,1,0:T(8,128)(2,1)S(1)}, u32[]{:S(2)}) copy-start(bf16[16,8,8,256]{3,2,1,0:T(8,128)(2,1)S(1)} %all-to-all-done.1.grad_ref.grad_in) | copy-start | bytes 1572868
  44.6 19.7 %all-to-all-start.2 = ((bf16[128,8,256]{2,1,0:T(8,128)(2,1)}), bf16[128,8,256]{2,1,0:T(8,128)(2,1)S(1)}, u32[]{:S(2)}, u32[]{:S(2)}) async-start(bf16[128,8,256]{2,1,0:T(8,128)(2,1)} %get-tuple-element.57), calls=%async_computation.2 | async-start | bytes 1048576 | tf_op jit(solution)/shard_map/all_to_all | solution.py:625
  50.7 13.7 %copy-start.3 = (bf16[256,768]{1,0:T(8,128)(2,1)S(1)}, bf16[256,768]{1,0:T(8,128)(2,1)}, u32[]{:S(2)}) copy-start(bf16[256,768]{1,0:T(8,128)(2,1)} %w_qkv_ref.4) | copy-start | bytes 1179652
  50.7 13.7 %copy-start.5 = (f32[256]{0:T(256)S(1)}, f32[256]{0:T(256)}, u32[]{:S(2)}) copy-start(f32[256]{0:T(256)} %param.24) | copy-start | bytes 3076
  64.4 7.7 %copy-start.2 = (bf16[128,8,256]{2,1,0:T(8,128)(2,1)}, bf16[128,8,256]{2,1,0:T(8,128)(2,1)S(1)}, u32[]{:S(2)}) copy-start(bf16[128,8,256]{2,1,0:T(8,128)(2,1)S(1)} %all-to-all-done.2) | copy-start | bytes 1572868
  72.0 18.3 %all-to-all-start.3 = ((bf16[128,8,256]{2,1,0:T(8,128)(2,1)}), bf16[128,8,256]{2,1,0:T(8,128)(2,1)S(1)}, u32[]{:S(2)}, u32[]{:S(2)}) async-start(bf16[128,8,256]{2,1,0:T(8,128)(2,1)} %bitcast.6), calls=%async_computation.3 | async-start | bytes 1048576 | tf_op jit(solution)/shard_map/all_to_all | solution.py:625
  76.6 18.0 %copy-start.4 = (bf16[256,256]{1,0:T(8,128)(2,1)S(1)}, bf16[256,256]{1,0:T(8,128)(2,1)}, u32[]{:S(2)}) copy-start(bf16[256,256]{1,0:T(8,128)(2,1)} %w_out_ref.7) | copy-start | bytes 393220
  76.6 18.0 %copy-start.6 = (f32[4,1,1024]{2,1,0:T(1,128)S(1)}, f32[4,1,1024]{2,1,0:T(1,128)}, u32[]{:S(2)}) copy-start(f32[4,1,1024]{2,1,0:T(1,128)} %get-tuple-element.67.total_ref) | copy-start | bytes 49156
  90.3 17.5 %copy-start.1 = (bf16[128,8,256]{2,1,0:T(8,128)(2,1)}, bf16[128,8,256]{2,1,0:T(8,128)(2,1)S(1)}, u32[]{:S(2)}) copy-start(bf16[128,8,256]{2,1,0:T(8,128)(2,1)S(1)} %all-to-all-done.3.grad_ref) | copy-start | bytes 1572868
  90.3 17.5 %all-to-all-start.4 = ((bf16[16,8,8,256]{3,2,1,0:T(8,128)(2,1)}), bf16[16,8,8,256]{3,2,1,0:T(8,128)(2,1)S(1)}, u32[]{:S(2)}, u32[]{:S(2)}) async-start(bf16[16,8,8,256]{3,2,1,0:T(8,128)(2,1)} %get-tuple-element.75), calls=%async_computation.4 | async-start | bytes 1048576 | tf_op jit(solution)/shard_map/all_to_all | solution.py:625
  107.8 30.7 %all-to-all-start.5 = ((bf16[128,2,8,256]{3,2,1,0:T(8,128)(2,1)}), bf16[128,2,8,256]{3,2,1,0:T(8,128)(2,1)S(1)}, u32[]{:S(2)}, u32[]{:S(2)}) async-start(bf16[128,2,8,256]{3,2,1,0:T(8,128)(2,1)} %get-tuple-element.77), calls=%async_computation.5 | async-start | bytes 2097152 | tf_op jit(solution)/shard_map/all_to_all | solution.py:625
  117.1 11.4 %collective-permute-start = (bf16[128,256]{1,0:T(8,128)(2,1)}, bf16[128,256]{1,0:T(8,128)(2,1)S(1)}, u32[]{:S(2)}, u32[]{:S(2)}) collective-permute-start(bf16[128,256]{1,0:T(8,128)(2,1)} %get-tuple-element.82), channel_id=1, source_target_pairs={{0,1},{1,0},{2,3},{3,2},{4,5},{5,4},{6,7},{7,6},{8,9},{9,8},{10,11... | collective-permute-start | bytes 196616 | tf_op jit(solution)/shard_map/ppermute | solution.py:629
  120.4 9.9 %collective-permute-start.1 = (bf16[128,256]{1,0:T(8,128)(2,1)}, bf16[128,256]{1,0:T(8,128)(2,1)S(1)}, u32[]{:S(2)}, u32[]{:S(2)}) collective-permute-start(bf16[128,256]{1,0:T(8,128)(2,1)} %get-tuple-element.83), channel_id=1, source_target_pairs={{0,2},{1,3},{2,0},{3,1},{4,6},{5,7},{6,4},{7,5},{8,10},{9,11},{10,... | collective-permute-start | bytes 196616 | tf_op jit(solution)/shard_map/ppermute | solution.py:629
  121.6 10.9 %collective-permute-start.2 = (bf16[128,256]{1,0:T(8,128)(2,1)}, bf16[128,256]{1,0:T(8,128)(2,1)S(1)}, u32[]{:S(2)}, u32[]{:S(2)}) collective-permute-start(bf16[128,256]{1,0:T(8,128)(2,1)} %get-tuple-element.84), channel_id=1, source_target_pairs={{0,3},{1,2},{2,1},{3,0},{4,7},{5,6},{6,5},{7,4},{8,11},{9,10},{10,... | collective-permute-start | bytes 196616 | tf_op jit(solution)/shard_map/ppermute | solution.py:629
  121.6 11.4 %collective-permute-start.3 = (bf16[128,256]{1,0:T(8,128)(2,1)}, bf16[128,256]{1,0:T(8,128)(2,1)S(1)}, u32[]{:S(2)}, u32[]{:S(2)}) collective-permute-start(bf16[128,256]{1,0:T(8,128)(2,1)} %get-tuple-element.85), channel_id=1, source_target_pairs={{0,4},{1,5},{2,6},{3,7},{4,0},{5,1},{6,2},{7,3},{8,12},{9,13},{10,... | collective-permute-start | bytes 196616 | tf_op jit(solution)/shard_map/ppermute | solution.py:629
  124.5 12.4 %collective-permute-start.4 = (bf16[128,256]{1,0:T(8,128)(2,1)}, bf16[128,256]{1,0:T(8,128)(2,1)S(1)}, u32[]{:S(2)}, u32[]{:S(2)}) collective-permute-start(bf16[128,256]{1,0:T(8,128)(2,1)} %get-tuple-element.86), channel_id=1, source_target_pairs={{0,5},{1,4},{2,7},{3,6},{4,1},{5,0},{6,3},{7,2},{8,13},{9,12},{10,... | collective-permute-start | bytes 196616 | tf_op jit(solution)/shard_map/ppermute | solution.py:629
  128.5 11.3 %copy-start.10 = (bf16[128,256]{1,0:T(8,128)(2,1)}, bf16[128,256]{1,0:T(8,128)(2,1)S(1)}, u32[]{:S(2)}) copy-start(bf16[128,256]{1,0:T(8,128)(2,1)S(1)} %collective-permute-done.refs_1_) | copy-start | bytes 196612
  128.5 8.4 %collective-permute-start.5 = (bf16[128,256]{1,0:T(8,128)(2,1)}, bf16[128,256]{1,0:T(8,128)(2,1)S(1)}, u32[]{:S(2)}, u32[]{:S(2)}) collective-permute-start(bf16[128,256]{1,0:T(8,128)(2,1)} %get-tuple-element.87), channel_id=1, source_target_pairs={{0,6},{1,7},{2,4},{3,5},{4,2},{5,3},{6,0},{7,1},{8,14},{9,15},{10,... | collective-permute-start | bytes 196616 | tf_op jit(solution)/shard_map/ppermute | solution.py:629
  130.3 9.5 %copy-start.11 = (bf16[128,256]{1,0:T(8,128)(2,1)}, bf16[128,256]{1,0:T(8,128)(2,1)S(1)}, u32[]{:S(2)}) copy-start(bf16[128,256]{1,0:T(8,128)(2,1)S(1)} %collective-permute-done.1.refs_2_) | copy-start | bytes 196612
  130.3 8.2 %collective-permute-start.6 = (bf16[128,256]{1,0:T(8,128)(2,1)}, bf16[128,256]{1,0:T(8,128)(2,1)S(1)}, u32[]{:S(2)}, u32[]{:S(2)}) collective-permute-start(bf16[128,256]{1,0:T(8,128)(2,1)} %get-tuple-element.88), channel_id=1, source_target_pairs={{0,7},{1,6},{2,5},{3,4},{4,3},{5,2},{6,1},{7,0},{8,15},{9,14},{10,... | collective-permute-start | bytes 196616 | tf_op jit(solution)/shard_map/ppermute | solution.py:629
  132.5 7.3 %copy-start.12 = (bf16[128,256]{1,0:T(8,128)(2,1)}, bf16[128,256]{1,0:T(8,128)(2,1)S(1)}, u32[]{:S(2)}) copy-start(bf16[128,256]{1,0:T(8,128)(2,1)S(1)} %collective-permute-done.2.refs_3_) | copy-start | bytes 196612
  133.1 6.7 %copy-start.13 = (bf16[128,256]{1,0:T(8,128)(2,1)}, bf16[128,256]{1,0:T(8,128)(2,1)S(1)}, u32[]{:S(2)}) copy-start(bf16[128,256]{1,0:T(8,128)(2,1)S(1)} %collective-permute-done.3.refs_4_) | copy-start | bytes 196612
  136.9 3.0 %copy-start.14 = (bf16[128,256]{1,0:T(8,128)(2,1)}, bf16[128,256]{1,0:T(8,128)(2,1)S(1)}, u32[]{:S(2)}) copy-start(bf16[128,256]{1,0:T(8,128)(2,1)S(1)} %collective-permute-done.4.refs_5_) | copy-start | bytes 196612
  136.9 3.0 %copy-start.15 = (bf16[128,256]{1,0:T(8,128)(2,1)}, bf16[128,256]{1,0:T(8,128)(2,1)S(1)}, u32[]{:S(2)}) copy-start(bf16[128,256]{1,0:T(8,128)(2,1)S(1)} %collective-permute-done.5.refs_6_) | copy-start | bytes 196612
  138.5 1.3 copy-start.16
  139.8 27.3 %all-to-all-start.6 = ((bf16[128,2,8,256]{3,2,1,0:T(8,128)(2,1)}), bf16[128,2,8,256]{3,2,1,0:T(8,128)(2,1)S(1)}, u32[]{:S(2)}, u32[]{:S(2)}) async-start(bf16[128,2,8,256]{3,2,1,0:T(8,128)(2,1)} %broadcast_in_dim.2), calls=%async_computation.6 | async-start | bytes 2097152 | tf_op jit(solution)/shard_map/all_to_all | solution.py:625

commit v6 on v5

--- a/solution.py
+++ b/solution.py
@@ -692,13 +692,26 @@
             me, grad_space, x, inverse, grad_packed, gain_s, w_qkv_space, stab_parts
         )
     )
-    blocks[1:] = [to_pair(blocks[step], step, stab_parts) for step in range(1, stab_parts)]
+    for step in range(1, stab_parts, 2):
+        blocks[step] = to_pair(blocks[step], step, stab_parts)
     sources, *blocks = lax.optimization_barrier((sources, *blocks))
+    blocks = list(blocks)
+    for step in range(2, stab_parts, 2):
+        blocks[step] = to_pair(blocks[step], step, stab_parts)
     scaling = 1.0 / math.sqrt(parts * rounds_here * stabs_here)
     summed = (jnp.sum(sources.astype(F32), axis=0) * scaling).astype(BF16)
     gathered = exchange(
         jnp.broadcast_to(summed[None], (parts,) + summed.shape), ("rounds", "stab")
     )
+    hidden_home = jnp.swapaxes(hidden_home, 0, 1).reshape(grad_hidden.shape)
+    weights = call(
+        unpack,
+        [((features, 3 * features), F32), ((features, features), F32)] * 2,
+        (gathered,),
+        2,
+        megabytes=20,
+    )
+    *weights, hidden_home, blocks = lax.optimization_barrier((*weights, hidden_home, blocks))
     grad_embedded = call(
         place_blocks,
         [(grad_hidden.shape, BF16)],
@@ -707,14 +720,6 @@
         in_specs=[SMEM] + [VMEM] * stab_parts,
         out_specs=[VMEM],
     )[0]
-    hidden_home = jnp.swapaxes(hidden_home, 0, 1).reshape(grad_hidden.shape)
-    weights = call(
-        unpack,
-        [((features, 3 * features), F32), ((features, features), F32)] * 2,
-        (gathered,),
-        2,
-        megabytes=20,
-    )
     return (hidden_home, grad_embedded) + tuple(weights)
 
 

time: 169 us -> 165 us (0.976)
  starting transfers between devices: 59.2 us -> 55.8 us
    all_to_all x7, starting transfers between devices: 45 us -> 42.4 us  [exchange(): return lax.all_to_all(values, axes, split_axis=0, concat_axis=0, tiled=True)]
    all_to_all x7, waiting for transfers between devices: 41.7 us -> 39.7 us  [exchange(): return lax.all_to_all(values, axes, split_axis=0, concat_axis=0, tiled=True)]
  transfers between devices with their start and end apart: 14 -> 14, of which waited for: 8 -> 7; matrix products, arithmetic and copies ran while one was open for 1% -> 1% of each run, Pallas kernels for 27% -> 27%
where the time goes in v6:
time: 165 us; the launch traced here: 164 us
  Pallas kernels  55.8 us (34%)
  starting transfers between devices  55.8 us (34%)
  waiting for transfers between devices  47.7 us (29%)
  local copies, waits for them, and re-layouts  4.11 us (2%)
    pallas_call x9, Pallas kernels, call(): pl.pallas_call(kernel, out_shape=[jax.ShapeDtypeStruct(*item) if isinstan...  55.8 us
    all_to_all x7, starting transfers between devices, exchange(): return lax.all_to_all(values, axes, split_axis=0, concat_axis=0, tiled=True)  42.4 us
    all_to_all x7, waiting for transfers between devices, exchange(): return lax.all_to_all(values, axes, split_axis=0, concat_axis=0, tiled=True)  39.7 us
    ppermute x7, starting transfers between devices, to_pair(): return lax.ppermute(block, 'stab', [(i, i ^ step) for i in range(parts)])  13.4 us
    ppermute x7, waiting for transfers between devices, to_pair(): return lax.ppermute(block, 'stab', [(i, i ^ step) for i in range(parts)])  7.96 us
  transfers between devices with their start and end apart: 14, of which 7 were waited for; matrix products, arithmetic and copies ran while one was open for 1% of the time, Pallas kernels for 27%

profile of v6, /device:TPU:1, one launch (start us, length us, event | category | flops | bytes accessed | tf_op | source)
XLA Modules:
  0.0 164.5 jit_solution(11054550950837216602)
XLA Ops:
  0.7 1.4 index_kernel.1
  2.1 8.3 %all-to-all-start = ((s32[8,5,128]{2,1,0:T(8,128)}), s32[8,5,128]{2,1,0:T(8,128)S(1)}, u32[]{:S(2)}, u32[]{:S(2)}) async-start(s32[8,5,128]{2,1,0:T(8,128)} %index_kernel.1), calls=%async_computation | async-start | bytes 65536 | tf_op jit(solution)/shard_map/all_to_all | solution.py:625
  10.4 0.9 copy_bitcast_fusion.1
  11.2 5.7 %all-to-all-done.index_ref = s32[8,5,128]{2,1,0:T(8,128)S(1)} async-done(((s32[8,5,128]{2,1,0:T(8,128)}), s32[8,5,128]{2,1,0:T(8,128)S(1)}, u32[]{:S(2)}, u32[]{:S(2)}) %all-to-all-start) | async-done | bytes 20512 | tf_op jit(solution)/shard_map/all_to_all | solution.py:625
  17.0 6.8 %all-to-all-start.1 = ((bf16[16,8,8,256]{3,2,1,0:T(8,128)(2,1)}), bf16[16,8,8,256]{3,2,1,0:T(8,128)(2,1)S(1)}, u32[]{:S(2)}, u32[]{:S(2)}) async-start(bf16[16,8,8,256]{3,2,1,0:T(8,128)(2,1)} %copy_bitcast_fusion.1), calls=%async_computation.1 | async-start | bytes 1048576 | tf_op jit(solution)/shard_map/all_to_all | solution.py:625
  23.8 0.6 copy.22.coord_table_ref
  24.5 20.1 %space_forward.1 = (bf16[128,8,256]{2,1,0:T(8,128)(2,1)}, f32[1,1024]{1,0:T(1,128)}, bf16[256,1024]{1,0:T(8,128)(2,1)}, f32[4,1,1024]{2,1,0:T(1,128)}, bf16[256,...) custom-call(s32[8,5,128]{2,1,0:T(8,128)} %copy-done.9, ...), custom_call_target="tpu_custom_call" | custom-call | flops 5000000000 | bytes 20000000 | tf_op jit(solution)/shard_map/space_forward/pallas_call | solution.py:26
  44.6 6.0 %all-to-all-start.2 = ((bf16[128,8,256]{2,1,0:T(8,128)(2,1)}), bf16[128,8,256]{2,1,0:T(8,128)(2,1)S(1)}, u32[]{:S(2)}, u32[]{:S(2)}) async-start(bf16[128,8,256]{2,1,0:T(8,128)(2,1)} %get-tuple-element.70), calls=%async_computation.2 | async-start | bytes 1048576 | tf_op jit(solution)/shard_map/all_to_all | solution.py:625
  50.7 2.5 %time_grad.1 = (bf16[1024,256]{1,0:T(8,128)(2,1)}, bf16[256,1024]{1,0:T(8,128)(2,1)}) custom-call(bf16[16,8,8,256]{3,2,1,0:T(8,128)(2,1)} %copy-done.7, bf16[256,256]{1,0:T(8,128)(2,1)} %w_out_ref.6), custom_call_target="tpu_custom_call" | custom-call | flops 1500000000 | bytes 6000000 | tf_op jit(solution)/shard_map/time_grad/pallas_call | solution.py:26
  53.1 11.2 %all-to-all-done.2 = bf16[128,8,256]{2,1,0:T(8,128)(2,1)S(1)} async-done(((bf16[128,8,256]{2,1,0:T(8,128)(2,1)}), bf16[128,8,256]{2,1,0:T(8,128)(2,1)S(1)}, u32[]{:S(2)}, u32[]{:S(2)}) %all-to-all-start.2) | async-done | bytes 524320 | tf_op jit(solution)/shard_map/all_to_all | solution.py:625
  64.3 7.7 %time_block.1 = (bf16[8,16,8,256]{3,2,1,0:T(8,128)(2,1)}, bf16[256,1024]{1,0:T(8,128)(2,1)}, bf16[768,1024]{1,0:T(8,128)(2,1)}, bf16[256,1024]{1,0:T(8,128)(2,1)}) custom-call(bf16[8,16,8,256]{3,2,1,0:T(8,128)(2,1)S(1)} %bitcast.16, bf16[16,8,8,256]{3,2,1,0:T(8,128)(2,1)} %copy-done.7, bf16[256,1024]{1,0:T(8,128)(2,1)} %get-tuple-element.72.grad_attended_in, ...), custom_call_target="tpu_custom_call" | custom-call | flops 5000000000 | bytes 20000000 | tf_op jit(solution)/shard_map/time_block/pallas_call | solution.py:26
  72.0 4.5 %all-to-all-start.3 = ((bf16[128,8,256]{2,1,0:T(8,128)(2,1)}), bf16[128,8,256]{2,1,0:T(8,128)(2,1)S(1)}, u32[]{:S(2)}, u32[]{:S(2)}) async-start(bf16[128,8,256]{2,1,0:T(8,128)(2,1)} %bitcast.6), calls=%async_computation.3 | async-start | bytes 1048576 | tf_op jit(solution)/shard_map/all_to_all | solution.py:625
  76.6 4.0 %time_rest.1 = (bf16[16,8,8,256]{3,2,1,0:T(8,128)(2,1)}, bf16[128,1,8,256]{3,2,1,0:T(8,128)(2,1)}) custom-call(bf16[8,16,8,256]{3,2,1,0:T(8,128)(2,1)} %bitcast.17, bf16[256,1024]{1,0:T(8,128)(2,1)} %get-tuple-element.73.normed_ref, bf16[768,1024]{1,0:T(8,128)(2,1)} %get-tuple-element.74.grad_packed_ref, bf16[256,1024]{1,0:T(8,128)(2,1)} %get-tuple-element.75.attended_ref, ...), custom_call_target="tpu_custom_call" | custom-call | flops 2500000000 | bytes 10000000 | tf_op jit(solution)/shard_map/time_rest/pallas_call | solution.py:26
  80.6 9.7 %all-to-all-done.3.grad_ref = bf16[128,8,256]{2,1,0:T(8,128)(2,1)S(1)} async-done(((bf16[128,8,256]{2,1,0:T(8,128)(2,1)}), bf16[128,8,256]{2,1,0:T(8,128)(2,1)S(1)}, u32[]{:S(2)}, u32[]{:S(2)}) %all-to-all-start.3) | async-done | bytes 524320 | tf_op jit(solution)/shard_map/all_to_all | solution.py:625
  90.3 4.2 %all-to-all-start.4 = ((bf16[16,8,8,256]{3,2,1,0:T(8,128)(2,1)}), bf16[16,8,8,256]{3,2,1,0:T(8,128)(2,1)S(1)}, u32[]{:S(2)}, u32[]{:S(2)}) async-start(bf16[16,8,8,256]{3,2,1,0:T(8,128)(2,1)} %get-tuple-element.88), calls=%async_computation.4 | async-start | bytes 1048576 | tf_op jit(solution)/shard_map/all_to_all | solution.py:625
  94.5 13.2 %space_backward.1 = (bf16[768,1024]{1,0:T(8,128)(2,1)}, bf16[128,2,8,256]{3,2,1,0:T(8,128)(2,1)}) custom-call(bf16[128,8,256]{2,1,0:T(8,128)(2,1)S(1)} %all-to-all-done.3.grad_ref, f32[4,1,1024]{2,1,0:T(1,128)S(1)} %copy-done.6, bf16[256,256]{1,0:T(8,128)(2,1)S(1)} %copy-done.4, bf16[768,1024]{1,0:T(8,128)(2,1)} %get-tuple-element.81.packed_in, ...), custom_call_target="tpu_custom_call" | custom-call | flops 7000000000 | bytes 28000000 | tf_op jit(solution)/shard_map/space_backward/pallas_call | solution.py:26
  107.8 5.6 %all-to-all-start.5 = ((bf16[128,2,8,256]{3,2,1,0:T(8,128)(2,1)}), bf16[128,2,8,256]{3,2,1,0:T(8,128)(2,1)S(1)}, u32[]{:S(2)}, u32[]{:S(2)}) async-start(bf16[128,2,8,256]{3,2,1,0:T(8,128)(2,1)} %get-tuple-element.89), calls=%async_computation.5 | async-start | bytes 2097152 | tf_op jit(solution)/shard_map/all_to_all | solution.py:625
  113.5 3.6 %space_stream.1 = (bf16[128,256]{1,0:T(8,128)(2,1)}, bf16[128,256]{1,0:T(8,128)(2,1)}, bf16[128,256]{1,0:T(8,128)(2,1)}, bf16[128,256]{1,0:T(8,128)(2,1)}, bf16[...) custom-call(s32[1]{0:T(128)} %bitcast.7.me_ref, ...), custom_call_target="tpu_custom_call" | custom-call | flops 2000000000 | bytes 8000000 | tf_op jit(solution)/shard_map/space_stream/pallas_call | solution.py:26
  117.0 3.3 %collective-permute-start = (bf16[128,256]{1,0:T(8,128)(2,1)}, bf16[128,256]{1,0:T(8,128)(2,1)S(1)}, u32[]{:S(2)}, u32[]{:S(2)}) collective-permute-start(bf16[128,256]{1,0:T(8,128)(2,1)} %get-tuple-element.94), channel_id=1, source_target_pairs={{0,1},{1,0},{2,3},{3,2},{4,5},{5,4},{6,7},{7,6},{8,9},{9,8},{10,11... | collective-permute-start | bytes 196616 | tf_op jit(solution)/shard_map/ppermute | solution.py:629
  120.3 1.1 collective-permute-start.1
  121.4 5.1 %collective-permute-start.2 = (bf16[128,256]{1,0:T(8,128)(2,1)}, bf16[128,256]{1,0:T(8,128)(2,1)S(1)}, u32[]{:S(2)}, u32[]{:S(2)}) collective-permute-start(bf16[128,256]{1,0:T(8,128)(2,1)} %get-tuple-element.98), channel_id=1, source_target_pairs={{0,5},{1,4},{2,7},{3,6},{4,1},{5,0},{6,3},{7,2},{8,13},{9,12},{10,... | collective-permute-start | bytes 196616 | tf_op jit(solution)/shard_map/ppermute | solution.py:629
  126.5 6.5 %collective-permute-done.refs_1_ = bf16[128,256]{1,0:T(8,128)(2,1)S(1)} collective-permute-done((bf16[128,256]{1,0:T(8,128)(2,1)}, bf16[128,256]{1,0:T(8,128)(2,1)S(1)}, u32[]{:S(2)}, u32[]{:S(2)}) %collective-permute-start) | collective-permute-done | bytes 65568 | tf_op jit(solution)/shard_map/ppermute | solution.py:629
  133.1 1.0 collective-permute-done.2.refs_5_
  134.7 1.1 broadcast_in_dim.2
  135.8 6.9 %all-to-all-start.6 = ((bf16[128,2,8,256]{3,2,1,0:T(8,128)(2,1)}), bf16[128,2,8,256]{3,2,1,0:T(8,128)(2,1)S(1)}, u32[]{:S(2)}, u32[]{:S(2)}) async-start(bf16[128,2,8,256]{3,2,1,0:T(8,128)(2,1)} %broadcast_in_dim.2), calls=%async_computation.6 | async-start | bytes 2097152 | tf_op jit(solution)/shard_map/all_to_all | solution.py:625
  142.7 0.8 copy_bitcast_fusion
  143.5 1.4 collective-permute-start.4
  144.9 2.4 %collective-permute-start.5 = (bf16[128,256]{1,0:T(8,128)(2,1)S(1)}, bf16[128,256]{1,0:T(8,128)(2,1)S(1)}, u32[]{:S(2)}, u32[]{:S(2)}) collective-permute-start(bf16[128,256]{1,0:T(8,128)(2,1)S(1)} %copy-done.12), channel_id=1, source_target_pairs={{0,4},{1,5},{2,6},{3,7},{4,0},{5,1},{6,2},{7,3},{8,12},{9,13},{10,... | collective-permute-start | bytes 196616 | tf_op jit(solution)/shard_map/ppermute | solution.py:629
  147.4 13.1 %all-to-all-done.6.pieces_ref = bf16[128,2,8,256]{3,2,1,0:T(8,128)(2,1)S(1)} async-done(((bf16[128,2,8,256]{3,2,1,0:T(8,128)(2,1)}), bf16[128,2,8,256]{3,2,1,0:T(8,128)(2,1)S(1)}, u32[]{:S(2)}, u32[]{:S(2)}) %all-to-all-start.6) | async-done | bytes 1048608 | tf_op jit(solution)/shard_map/all_to_all | solution.py:625
  160.5 1.4 unpack.1
  162.0 0.6 copy-done.17
  162.6 1.9 %place_blocks.1 = bf16[8,128,256]{2,1,0:T(8,128)(2,1)} custom-call(s32[1]{0:T(128)} %bitcast.7.me_ref, bf16[128,256]{1,0:T(8,128)(2,1)} %get-tuple-element.116.refs_0_, bf16[128,256]{1,0:T(8,128)(2,1)} %copy-done.11, bf16[128,256]{1,0:T(8,128)(2,1)} %copy-done.17, bf16[128,256]{1,0:T(8,128)(2,1)} %copy-done.13, bf16[128,256]{1,0:T(8,128)(2,1)} %copy-done.18, ...), custom_call_target="tpu_custom_call" | custom-call | flops 1000000000 | bytes 4000000 | tf_op jit(solution)/shard_map/place_blocks/pallas_call | solution.py:26
  (51 shorter events, 0.9 us)
Async XLA Ops:
  0.6 9.8 %copy-start = (bf16[8,128,256]{2,1,0:T(8,128)(2,1)S(1)}, bf16[8,128,256]{2,1,0:T(8,128)(2,1)}, u32[]{:S(2)}) copy-start(bf16[8,128,256]{2,1,0:T(8,128)(2,1)} %param.27) | copy-start | bytes 1572868
  0.6 23.2 %copy-start.8 = (bf16[2,42,256]{2,0,1:T(2,128)(2,1)S(1)}, bf16[2,42,256]{2,0,1:T(2,128)(2,1)}, u32[]{:S(2)}) copy-start(bf16[2,42,256]{2,0,1:T(2,128)(2,1)} %param.19) | copy-start | bytes 129028
  2.1 14.9 %all-to-all-start = ((s32[8,5,128]{2,1,0:T(8,128)}), s32[8,5,128]{2,1,0:T(8,128)S(1)}, u32[]{:S(2)}, u32[]{:S(2)}) async-start(s32[8,5,128]{2,1,0:T(8,128)} %index_kernel.1), calls=%async_computation | async-start | bytes 65536 | tf_op jit(solution)/shard_map/all_to_all | solution.py:625
  17.0 7.5 %copy-start.9 = (s32[8,5,128]{2,1,0:T(8,128)}, s32[8,5,128]{2,1,0:T(8,128)S(1)}, u32[]{:S(2)}) copy-start(s32[8,5,128]{2,1,0:T(8,128)S(1)} %all-to-all-done.index_ref) | copy-start | bytes 61444
  17.0 27.6 %all-to-all-start.1 = ((bf16[16,8,8,256]{3,2,1,0:T(8,128)(2,1)}), bf16[16,8,8,256]{3,2,1,0:T(8,128)(2,1)S(1)}, u32[]{:S(2)}, u32[]{:S(2)}) async-start(bf16[16,8,8,256]{3,2,1,0:T(8,128)(2,1)} %copy_bitcast_fusion.1), calls=%async_computation.1 | async-start | bytes 1048576 | tf_op jit(solution)/shard_map/all_to_all | solution.py:625
  44.6 6.0 %copy-start.7 = (bf16[16,8,8,256]{3,2,1,0:T(8,128)(2,1)}, bf16[16,8,8,256]{3,2,1,0:T(8,128)(2,1)S(1)}, u32[]{:S(2)}) copy-start(bf16[16,8,8,256]{3,2,1,0:T(8,128)(2,1)S(1)} %all-to-all-done.1.grad_ref.grad_in) | copy-start | bytes 1572868
  44.6 19.7 %all-to-all-start.2 = ((bf16[128,8,256]{2,1,0:T(8,128)(2,1)}), bf16[128,8,256]{2,1,0:T(8,128)(2,1)S(1)}, u32[]{:S(2)}, u32[]{:S(2)}) async-start(bf16[128,8,256]{2,1,0:T(8,128)(2,1)} %get-tuple-element.70), calls=%async_computation.2 | async-start | bytes 1048576 | tf_op jit(solution)/shard_map/all_to_all | solution.py:625
  50.6 13.7 %copy-start.3 = (bf16[256,768]{1,0:T(8,128)(2,1)S(1)}, bf16[256,768]{1,0:T(8,128)(2,1)}, u32[]{:S(2)}) copy-start(bf16[256,768]{1,0:T(8,128)(2,1)} %w_qkv_ref.4) | copy-start | bytes 1179652
  50.6 13.7 %copy-start.5 = (f32[256]{0:T(256)S(1)}, f32[256]{0:T(256)}, u32[]{:S(2)}) copy-start(f32[256]{0:T(256)} %param.24) | copy-start | bytes 3076
  64.3 7.7 %copy-start.2 = (bf16[128,8,256]{2,1,0:T(8,128)(2,1)}, bf16[128,8,256]{2,1,0:T(8,128)(2,1)S(1)}, u32[]{:S(2)}) copy-start(bf16[128,8,256]{2,1,0:T(8,128)(2,1)S(1)} %all-to-all-done.2) | copy-start | bytes 1572868
  72.0 18.3 %all-to-all-start.3 = ((bf16[128,8,256]{2,1,0:T(8,128)(2,1)}), bf16[128,8,256]{2,1,0:T(8,128)(2,1)S(1)}, u32[]{:S(2)}, u32[]{:S(2)}) async-start(bf16[128,8,256]{2,1,0:T(8,128)(2,1)} %bitcast.6), calls=%async_computation.3 | async-start | bytes 1048576 | tf_op jit(solution)/shard_map/all_to_all | solution.py:625
  76.6 18.0 %copy-start.4 = (bf16[256,256]{1,0:T(8,128)(2,1)S(1)}, bf16[256,256]{1,0:T(8,128)(2,1)}, u32[]{:S(2)}) copy-start(bf16[256,256]{1,0:T(8,128)(2,1)} %w_out_ref.7) | copy-start | bytes 393220
  76.6 18.0 %copy-start.6 = (f32[4,1,1024]{2,1,0:T(1,128)S(1)}, f32[4,1,1024]{2,1,0:T(1,128)}, u32[]{:S(2)}) copy-start(f32[4,1,1024]{2,1,0:T(1,128)} %get-tuple-element.80.total_ref) | copy-start | bytes 49156
  90.3 17.5 %copy-start.1 = (bf16[128,8,256]{2,1,0:T(8,128)(2,1)}, bf16[128,8,256]{2,1,0:T(8,128)(2,1)S(1)}, u32[]{:S(2)}) copy-start(bf16[128,8,256]{2,1,0:T(8,128)(2,1)S(1)} %all-to-all-done.3.grad_ref) | copy-start | bytes 1572868
  90.3 17.5 %all-to-all-start.4 = ((bf16[16,8,8,256]{3,2,1,0:T(8,128)(2,1)}), bf16[16,8,8,256]{3,2,1,0:T(8,128)(2,1)S(1)}, u32[]{:S(2)}, u32[]{:S(2)}) async-start(bf16[16,8,8,256]{3,2,1,0:T(8,128)(2,1)} %get-tuple-element.88), calls=%async_computation.4 | async-start | bytes 1048576 | tf_op jit(solution)/shard_map/all_to_all | solution.py:625
  107.8 26.7 %all-to-all-start.5 = ((bf16[128,2,8,256]{3,2,1,0:T(8,128)(2,1)}), bf16[128,2,8,256]{3,2,1,0:T(8,128)(2,1)S(1)}, u32[]{:S(2)}, u32[]{:S(2)}) async-start(bf16[128,2,8,256]{3,2,1,0:T(8,128)(2,1)} %get-tuple-element.89), calls=%async_computation.5 | async-start | bytes 2097152 | tf_op jit(solution)/shard_map/all_to_all | solution.py:625
  117.0 16.0 %collective-permute-start = (bf16[128,256]{1,0:T(8,128)(2,1)}, bf16[128,256]{1,0:T(8,128)(2,1)S(1)}, u32[]{:S(2)}, u32[]{:S(2)}) collective-permute-start(bf16[128,256]{1,0:T(8,128)(2,1)} %get-tuple-element.94), channel_id=1, source_target_pairs={{0,1},{1,0},{2,3},{3,2},{4,5},{5,4},{6,7},{7,6},{8,9},{9,8},{10,11... | collective-permute-start | bytes 196616 | tf_op jit(solution)/shard_map/ppermute | solution.py:629
  120.3 12.7 %collective-permute-start.1 = (bf16[128,256]{1,0:T(8,128)(2,1)}, bf16[128,256]{1,0:T(8,128)(2,1)S(1)}, u32[]{:S(2)}, u32[]{:S(2)}) collective-permute-start(bf16[128,256]{1,0:T(8,128)(2,1)} %get-tuple-element.96), channel_id=1, source_target_pairs={{0,3},{1,2},{2,1},{3,0},{4,7},{5,6},{6,5},{7,4},{8,11},{9,10},{10,... | collective-permute-start | bytes 196616 | tf_op jit(solution)/shard_map/ppermute | solution.py:629
  121.4 12.6 %collective-permute-start.2 = (bf16[128,256]{1,0:T(8,128)(2,1)}, bf16[128,256]{1,0:T(8,128)(2,1)S(1)}, u32[]{:S(2)}, u32[]{:S(2)}) collective-permute-start(bf16[128,256]{1,0:T(8,128)(2,1)} %get-tuple-element.98), channel_id=1, source_target_pairs={{0,5},{1,4},{2,7},{3,6},{4,1},{5,0},{6,3},{7,2},{8,13},{9,12},{10,... | collective-permute-start | bytes 196616 | tf_op jit(solution)/shard_map/ppermute | solution.py:629
  126.5 8.0 %collective-permute-start.3 = (bf16[128,256]{1,0:T(8,128)(2,1)}, bf16[128,256]{1,0:T(8,128)(2,1)S(1)}, u32[]{:S(2)}, u32[]{:S(2)}) collective-permute-start(bf16[128,256]{1,0:T(8,128)(2,1)} %get-tuple-element.100), channel_id=1, source_target_pairs={{0,7},{1,6},{2,5},{3,4},{4,3},{5,2},{6,1},{7,0},{8,15},{9,14},{10,... | collective-permute-start | bytes 196616 | tf_op jit(solution)/shard_map/ppermute | solution.py:629
  133.1 2.7 %copy-start.11 = (bf16[128,256]{1,0:T(8,128)(2,1)}, bf16[128,256]{1,0:T(8,128)(2,1)S(1)}, u32[]{:S(2)}) copy-start(bf16[128,256]{1,0:T(8,128)(2,1)S(1)} %collective-permute-done.refs_1_) | copy-start | bytes 196612
  133.1 2.7 %copy-start.13 = (bf16[128,256]{1,0:T(8,128)(2,1)}, bf16[128,256]{1,0:T(8,128)(2,1)S(1)}, u32[]{:S(2)}) copy-start(bf16[128,256]{1,0:T(8,128)(2,1)S(1)} %collective-permute-done.1.refs_3_) | copy-start | bytes 196612
  134.0 1.8 %copy-start.15 = (bf16[128,256]{1,0:T(8,128)(2,1)}, bf16[128,256]{1,0:T(8,128)(2,1)S(1)}, u32[]{:S(2)}) copy-start(bf16[128,256]{1,0:T(8,128)(2,1)S(1)} %collective-permute-done.2.refs_5_) | copy-start | bytes 196612
  134.5 1.3 copy-start.16
  135.8 7.8 %copy-start.14 = (bf16[128,256]{1,0:T(8,128)(2,1)S(1)}, bf16[128,256]{1,0:T(8,128)(2,1)}, u32[]{:S(2)}) copy-start(bf16[128,256]{1,0:T(8,128)(2,1)} %get-tuple-element.109) | copy-start | bytes 196612
  135.8 9.1 %copy-start.12 = (bf16[128,256]{1,0:T(8,128)(2,1)S(1)}, bf16[128,256]{1,0:T(8,128)(2,1)}, u32[]{:S(2)}) copy-start(bf16[128,256]{1,0:T(8,128)(2,1)} %get-tuple-element.111) | copy-start | bytes 196612
  135.8 11.6 %copy-start.10 = (bf16[128,256]{1,0:T(8,128)(2,1)S(1)}, bf16[128,256]{1,0:T(8,128)(2,1)}, u32[]{:S(2)}) copy-start(bf16[128,256]{1,0:T(8,128)(2,1)} %get-tuple-element.113) | copy-start | bytes 196612
  135.8 24.7 %all-to-all-start.6 = ((bf16[128,2,8,256]{3,2,1,0:T(8,128)(2,1)}), bf16[128,2,8,256]{3,2,1,0:T(8,128)(2,1)S(1)}, u32[]{:S(2)}, u32[]{:S(2)}) async-start(bf16[128,2,8,256]{3,2,1,0:T(8,128)(2,1)} %broadcast_in_dim.2), calls=%async_computation.6 | async-start | bytes 2097152 | tf_op jit(solution)/shard_map/all_to_all | solution.py:625
  143.5 18.4 %collective-permute-start.4 = (bf16[128,256]{1,0:T(8,128)(2,1)S(1)}, bf16[128,256]{1,0:T(8,128)(2,1)S(1)}, u32[]{:S(2)}, u32[]{:S(2)}) collective-permute-start(bf16[128,256]{1,0:T(8,128)(2,1)S(1)} %copy-done.14), channel_id=1, source_target_pairs={{0,2},{1,3},{2,0},{3,1},{4,6},{5,7},{6,4},{7,5},{8,10},{9,11},{10,... | collective-permute-start | bytes 196616 | tf_op jit(solution)/shard_map/ppermute | solution.py:629
  144.9 17.0 %collective-permute-start.5 = (bf16[128,256]{1,0:T(8,128)(2,1)S(1)}, bf16[128,256]{1,0:T(8,128)(2,1)S(1)}, u32[]{:S(2)}, u32[]{:S(2)}) collective-permute-start(bf16[128,256]{1,0:T(8,128)(2,1)S(1)} %copy-done.12), channel_id=1, source_target_pairs={{0,4},{1,5},{2,6},{3,7},{4,0},{5,1},{6,2},{7,3},{8,12},{9,13},{10,... | collective-permute-start | bytes 196616 | tf_op jit(solution)/shard_map/ppermute | solution.py:629
  147.4 14.6 %collective-permute-start.6 = (bf16[128,256]{1,0:T(8,128)(2,1)S(1)}, bf16[128,256]{1,0:T(8,128)(2,1)S(1)}, u32[]{:S(2)}, u32[]{:S(2)}) collective-permute-start(bf16[128,256]{1,0:T(8,128)(2,1)S(1)} %copy-done.10), channel_id=1, source_target_pairs={{0,6},{1,7},{2,4},{3,5},{4,2},{5,3},{6,0},{7,1},{8,14},{9,15},{10,... | collective-permute-start | bytes 196616 | tf_op jit(solution)/shard_map/ppermute | solution.py:629
  162.0 0.7 copy-start.19
  (2 other events, 1.2 us)

commit v7 on v6

--- a/solution.py
+++ b/solution.py
@@ -692,11 +692,12 @@
             me, grad_space, x, inverse, grad_packed, gain_s, w_qkv_space, stab_parts
         )
     )
-    for step in range(1, stab_parts, 2):
+    near = [step for step in range(1, stab_parts) if step % 4 == 2]
+    for step in sorted(set(range(1, stab_parts)) - set(near)):
         blocks[step] = to_pair(blocks[step], step, stab_parts)
     sources, *blocks = lax.optimization_barrier((sources, *blocks))
     blocks = list(blocks)
-    for step in range(2, stab_parts, 2):
+    for step in near:
         blocks[step] = to_pair(blocks[step], step, stab_parts)
     scaling = 1.0 / math.sqrt(parts * rounds_here * stabs_here)
     summed = (jnp.sum(sources.astype(F32), axis=0) * scaling).astype(BF16)
@@ -711,7 +712,6 @@
         2,
         megabytes=20,
     )
-    *weights, hidden_home, blocks = lax.optimization_barrier((*weights, hidden_home, blocks))
     grad_embedded = call(
         place_blocks,
         [(grad_hidden.shape, BF16)],

time: 165 us -> 164 us (level)
    all_to_all x7, waiting for transfers between devices: 39.7 us -> 29.7 us  [exchange(): return lax.all_to_all(values, axes, split_axis=0, concat_axis=0, tiled=True)]
    ppermute x7, waiting for transfers between devices: 7.96 us -> 16.5 us  [to_pair(): return lax.ppermute(block, 'stab', [(i, i ^ step) for i in range(parts)])]
  transfers between devices with their start and end apart: 14 -> 14, of which waited for: 7 -> 9; matrix products, arithmetic and copies ran while one was open for 1% -> 1% of each run, Pallas kernels for 27% -> 28%
where the time goes in v7:
time: 164 us; the launch traced here: 163 us
  Pallas kernels  55.8 us (34%)
  starting transfers between devices  55.7 us (34%)
  waiting for transfers between devices  46.2 us (28%)
  local copies, waits for them, and re-layouts  4.08 us (2%)
    pallas_call x9, Pallas kernels, call(): pl.pallas_call(kernel, out_shape=[jax.ShapeDtypeStruct(*item) if isinstan...  55.8 us
    all_to_all x7, starting transfers between devices, exchange(): return lax.all_to_all(values, axes, split_axis=0, concat_axis=0, tiled=True)  40.9 us
    all_to_all x7, waiting for transfers between devices, exchange(): return lax.all_to_all(values, axes, split_axis=0, concat_axis=0, tiled=True)  29.7 us
    ppermute x7, waiting for transfers between devices, to_pair(): return lax.ppermute(block, 'stab', [(i, i ^ step) for i in range(parts)])  16.5 us
    ppermute x7, starting transfers between devices, to_pair(): return lax.ppermute(block, 'stab', [(i, i ^ step) for i in range(parts)])  14.8 us
  transfers between devices with their start and end apart: 14, of which 9 were waited for; matrix products, arithmetic and copies ran while one was open for 1% of the time, Pallas kernels for 28%

profile of v7, /device:TPU:1, one launch (start us, length us, event | category | flops | bytes accessed | tf_op | source)
XLA Modules:
  0.0 162.9 jit_solution(12905898155552633976)
XLA Ops:
  0.7 1.4 index_kernel.1
  2.1 8.3 %all-to-all-start = ((s32[8,5,128]{2,1,0:T(8,128)}), s32[8,5,128]{2,1,0:T(8,128)S(1)}, u32[]{:S(2)}, u32[]{:S(2)}) async-start(s32[8,5,128]{2,1,0:T(8,128)} %index_kernel.1), calls=%async_computation | async-start | bytes 65536 | tf_op jit(solution)/shard_map/all_to_all | solution.py:625
  11.3 5.7 %all-to-all-done.index_ref = s32[8,5,128]{2,1,0:T(8,128)S(1)} async-done(((s32[8,5,128]{2,1,0:T(8,128)}), s32[8,5,128]{2,1,0:T(8,128)S(1)}, u32[]{:S(2)}, u32[]{:S(2)}) %all-to-all-start) | async-done | bytes 20512 | tf_op jit(solution)/shard_map/all_to_all | solution.py:625
  17.0 6.8 %all-to-all-start.1 = ((bf16[16,8,8,256]{3,2,1,0:T(8,128)(2,1)}), bf16[16,8,8,256]{3,2,1,0:T(8,128)(2,1)S(1)}, u32[]{:S(2)}, u32[]{:S(2)}) async-start(bf16[16,8,8,256]{3,2,1,0:T(8,128)(2,1)} %copy_bitcast_fusion.1), calls=%async_computation.1 | async-start | bytes 1048576 | tf_op jit(solution)/shard_map/all_to_all | solution.py:625
  24.5 20.1 %space_forward.1 = (bf16[128,8,256]{2,1,0:T(8,128)(2,1)}, f32[1,1024]{1,0:T(1,128)}, bf16[256,1024]{1,0:T(8,128)(2,1)}, f32[4,1,1024]{2,1,0:T(1,128)}, bf16[256,...) custom-call(s32[8,5,128]{2,1,0:T(8,128)} %copy-done.9, ...), custom_call_target="tpu_custom_call" | custom-call | flops 5000000000 | bytes 20000000 | tf_op jit(solution)/shard_map/space_forward/pallas_call | solution.py:26
  44.6 6.0 %all-to-all-start.2 = ((bf16[128,8,256]{2,1,0:T(8,128)(2,1)}), bf16[128,8,256]{2,1,0:T(8,128)(2,1)S(1)}, u32[]{:S(2)}, u32[]{:S(2)}) async-start(bf16[128,8,256]{2,1,0:T(8,128)(2,1)} %get-tuple-element.57), calls=%async_computation.2 | async-start | bytes 1048576 | tf_op jit(solution)/shard_map/all_to_all | solution.py:625
  50.7 2.5 %time_grad.1 = (bf16[1024,256]{1,0:T(8,128)(2,1)}, bf16[256,1024]{1,0:T(8,128)(2,1)}) custom-call(bf16[16,8,8,256]{3,2,1,0:T(8,128)(2,1)} %copy-done.7, bf16[256,256]{1,0:T(8,128)(2,1)} %w_out_ref.6), custom_call_target="tpu_custom_call" | custom-call | flops 1500000000 | bytes 6000000 | tf_op jit(solution)/shard_map/time_grad/pallas_call | solution.py:26
  53.1 11.2 %all-to-all-done.2 = bf16[128,8,256]{2,1,0:T(8,128)(2,1)S(1)} async-done(((bf16[128,8,256]{2,1,0:T(8,128)(2,1)}), bf16[128,8,256]{2,1,0:T(8,128)(2,1)S(1)}, u32[]{:S(2)}, u32[]{:S(2)}) %all-to-all-start.2) | async-done | bytes 524320 | tf_op jit(solution)/shard_map/all_to_all | solution.py:625
  64.4 7.7 %time_block.1 = (bf16[8,16,8,256]{3,2,1,0:T(8,128)(2,1)}, bf16[256,1024]{1,0:T(8,128)(2,1)}, bf16[768,1024]{1,0:T(8,128)(2,1)}, bf16[256,1024]{1,0:T(8,128)(2,1)}) custom-call(bf16[8,16,8,256]{3,2,1,0:T(8,128)(2,1)S(1)} %bitcast.16, bf16[16,8,8,256]{3,2,1,0:T(8,128)(2,1)} %copy-done.7, bf16[256,1024]{1,0:T(8,128)(2,1)} %get-tuple-element.59.grad_attended_in, ...), custom_call_target="tpu_custom_call" | custom-call | flops 5000000000 | bytes 20000000 | tf_op jit(solution)/shard_map/time_block/pallas_call | solution.py:26
  72.0 4.5 %all-to-all-start.3 = ((bf16[128,8,256]{2,1,0:T(8,128)(2,1)}), bf16[128,8,256]{2,1,0:T(8,128)(2,1)S(1)}, u32[]{:S(2)}, u32[]{:S(2)}) async-start(bf16[128,8,256]{2,1,0:T(8,128)(2,1)} %bitcast.6), calls=%async_computation.3 | async-start | bytes 1048576 | tf_op jit(solution)/shard_map/all_to_all | solution.py:625
  76.6 4.0 %time_rest.1 = (bf16[16,8,8,256]{3,2,1,0:T(8,128)(2,1)}, bf16[128,1,8,256]{3,2,1,0:T(8,128)(2,1)}) custom-call(bf16[8,16,8,256]{3,2,1,0:T(8,128)(2,1)} %bitcast.17, bf16[256,1024]{1,0:T(8,128)(2,1)} %get-tuple-element.60.normed_ref, bf16[768,1024]{1,0:T(8,128)(2,1)} %get-tuple-element.61.grad_packed_ref, bf16[256,1024]{1,0:T(8,128)(2,1)} %get-tuple-element.62.attended_ref, ...), custom_call_target="tpu_custom_call" | custom-call | flops 2500000000 | bytes 10000000 | tf_op jit(solution)/shard_map/time_rest/pallas_call | solution.py:26
  80.6 9.7 %all-to-all-done.3.grad_ref = bf16[128,8,256]{2,1,0:T(8,128)(2,1)S(1)} async-done(((bf16[128,8,256]{2,1,0:T(8,128)(2,1)}), bf16[128,8,256]{2,1,0:T(8,128)(2,1)S(1)}, u32[]{:S(2)}, u32[]{:S(2)}) %all-to-all-start.3) | async-done | bytes 524320 | tf_op jit(solution)/shard_map/all_to_all | solution.py:625
  90.3 4.2 %all-to-all-start.4 = ((bf16[16,8,8,256]{3,2,1,0:T(8,128)(2,1)}), bf16[16,8,8,256]{3,2,1,0:T(8,128)(2,1)S(1)}, u32[]{:S(2)}, u32[]{:S(2)}) async-start(bf16[16,8,8,256]{3,2,1,0:T(8,128)(2,1)} %get-tuple-element.75), calls=%async_computation.4 | async-start | bytes 1048576 | tf_op jit(solution)/shard_map/all_to_all | solution.py:625
  94.5 13.3 %space_backward.1 = (bf16[768,1024]{1,0:T(8,128)(2,1)}, bf16[128,2,8,256]{3,2,1,0:T(8,128)(2,1)}) custom-call(bf16[128,8,256]{2,1,0:T(8,128)(2,1)S(1)} %all-to-all-done.3.grad_ref, f32[4,1,1024]{2,1,0:T(1,128)S(1)} %copy-done.6, bf16[256,256]{1,0:T(8,128)(2,1)S(1)} %copy-done.4, bf16[768,1024]{1,0:T(8,128)(2,1)} %get-tuple-element.68.packed_in, ...), custom_call_target="tpu_custom_call" | custom-call | flops 7000000000 | bytes 28000000 | tf_op jit(solution)/shard_map/space_backward/pallas_call | solution.py:26
  107.8 5.6 %all-to-all-start.5 = ((bf16[128,2,8,256]{3,2,1,0:T(8,128)(2,1)}), bf16[128,2,8,256]{3,2,1,0:T(8,128)(2,1)S(1)}, u32[]{:S(2)}, u32[]{:S(2)}) async-start(bf16[128,2,8,256]{3,2,1,0:T(8,128)(2,1)} %get-tuple-element.77), calls=%async_computation.5 | async-start | bytes 2097152 | tf_op jit(solution)/shard_map/all_to_all | solution.py:625
  113.5 3.6 %space_stream.1 = (bf16[128,256]{1,0:T(8,128)(2,1)}, bf16[128,256]{1,0:T(8,128)(2,1)}, bf16[128,256]{1,0:T(8,128)(2,1)}, bf16[128,256]{1,0:T(8,128)(2,1)}, bf16[...) custom-call(s32[1]{0:T(128)} %bitcast.9.me_ref, ...), custom_call_target="tpu_custom_call" | custom-call | flops 2000000000 | bytes 8000000 | tf_op jit(solution)/shard_map/space_stream/pallas_call | solution.py:26
  117.1 3.3 %collective-permute-start = (bf16[128,256]{1,0:T(8,128)(2,1)}, bf16[128,256]{1,0:T(8,128)(2,1)S(1)}, u32[]{:S(2)}, u32[]{:S(2)}) collective-permute-start(bf16[128,256]{1,0:T(8,128)(2,1)} %get-tuple-element.82), channel_id=1, source_target_pairs={{0,1},{1,0},{2,3},{3,2},{4,5},{5,4},{6,7},{7,6},{8,9},{9,8},{10,11... | collective-permute-start | bytes 196616 | tf_op jit(solution)/shard_map/ppermute | solution.py:629
  121.4 2.5 %collective-permute-start.2 = (bf16[128,256]{1,0:T(8,128)(2,1)}, bf16[128,256]{1,0:T(8,128)(2,1)S(1)}, u32[]{:S(2)}, u32[]{:S(2)}) collective-permute-start(bf16[128,256]{1,0:T(8,128)(2,1)} %get-tuple-element.85), channel_id=1, source_target_pairs={{0,4},{1,5},{2,6},{3,7},{4,0},{5,1},{6,2},{7,3},{8,12},{9,13},{10,... | collective-permute-start | bytes 196616 | tf_op jit(solution)/shard_map/ppermute | solution.py:629
  123.9 3.0 %collective-permute-start.3 = (bf16[128,256]{1,0:T(8,128)(2,1)}, bf16[128,256]{1,0:T(8,128)(2,1)S(1)}, u32[]{:S(2)}, u32[]{:S(2)}) collective-permute-start(bf16[128,256]{1,0:T(8,128)(2,1)} %get-tuple-element.86), channel_id=1, source_target_pairs={{0,5},{1,4},{2,7},{3,6},{4,1},{5,0},{6,3},{7,2},{8,13},{9,12},{10,... | collective-permute-start | bytes 196616 | tf_op jit(solution)/shard_map/ppermute | solution.py:629
  127.0 1.7 %collective-permute-start.4 = (bf16[128,256]{1,0:T(8,128)(2,1)}, bf16[128,256]{1,0:T(8,128)(2,1)S(1)}, u32[]{:S(2)}, u32[]{:S(2)}) collective-permute-start(bf16[128,256]{1,0:T(8,128)(2,1)} %get-tuple-element.88), channel_id=1, source_target_pairs={{0,7},{1,6},{2,5},{3,4},{4,3},{5,2},{6,1},{7,0},{8,15},{9,14},{10,... | collective-permute-start | bytes 196616 | tf_op jit(solution)/shard_map/ppermute | solution.py:629
  128.6 4.0 %collective-permute-done.refs_1_ = bf16[128,256]{1,0:T(8,128)(2,1)S(1)} collective-permute-done((bf16[128,256]{1,0:T(8,128)(2,1)}, bf16[128,256]{1,0:T(8,128)(2,1)S(1)}, u32[]{:S(2)}, u32[]{:S(2)}) %collective-permute-start) | collective-permute-done | bytes 65568 | tf_op jit(solution)/shard_map/ppermute | solution.py:629
  132.7 2.8 %collective-permute-done.3.refs_5_ = bf16[128,256]{1,0:T(8,128)(2,1)S(1)} collective-permute-done((bf16[128,256]{1,0:T(8,128)(2,1)}, bf16[128,256]{1,0:T(8,128)(2,1)S(1)}, u32[]{:S(2)}, u32[]{:S(2)}) %collective-permute-start.3) | collective-permute-done | bytes 65568 | tf_op jit(solution)/shard_map/ppermute | solution.py:629
  135.4 1.6 collective-permute-done.4.refs_7_
  137.2 1.1 broadcast_in_dim.2
  138.3 5.3 %all-to-all-start.6 = ((bf16[128,2,8,256]{3,2,1,0:T(8,128)(2,1)}), bf16[128,2,8,256]{3,2,1,0:T(8,128)(2,1)S(1)}, u32[]{:S(2)}, u32[]{:S(2)}) async-start(bf16[128,2,8,256]{3,2,1,0:T(8,128)(2,1)} %broadcast_in_dim.2), calls=%async_computation.6 | async-start | bytes 2097152 | tf_op jit(solution)/shard_map/all_to_all | solution.py:625
  143.7 1.5 collective-permute-start.5
  145.1 1.8 %collective-permute-start.6 = (bf16[128,256]{1,0:T(8,128)(2,1)S(1)}, bf16[128,256]{1,0:T(8,128)(2,1)S(1)}, u32[]{:S(2)}, u32[]{:S(2)}) collective-permute-start(bf16[128,256]{1,0:T(8,128)(2,1)S(1)} %copy-done.10), channel_id=1, source_target_pairs={{0,6},{1,7},{2,4},{3,5},{4,2},{5,3},{6,0},{7,1},{8,14},{9,15},{10,... | collective-permute-start | bytes 196616 | tf_op jit(solution)/shard_map/ppermute | solution.py:629
  147.8 6.4 %collective-permute-done.5.refs_2_ = bf16[128,256]{1,0:T(8,128)(2,1)S(1)} collective-permute-done((bf16[128,256]{1,0:T(8,128)(2,1)S(1)}, bf16[128,256]{1,0:T(8,128)(2,1)S(1)}, u32[]{:S(2)}, u32[]{:S(2)}) %collective-permute-start.5) | collective-permute-done | bytes 65568 | tf_op jit(solution)/shard_map/ppermute | solution.py:629
  154.1 1.8 %collective-permute-done.6.refs_6_ = bf16[128,256]{1,0:T(8,128)(2,1)S(1)} collective-permute-done((bf16[128,256]{1,0:T(8,128)(2,1)S(1)}, bf16[128,256]{1,0:T(8,128)(2,1)S(1)}, u32[]{:S(2)}, u32[]{:S(2)}) %collective-permute-start.6) | collective-permute-done | bytes 65568 | tf_op jit(solution)/shard_map/ppermute | solution.py:629
  156.6 1.9 %place_blocks.1 = bf16[8,128,256]{2,1,0:T(8,128)(2,1)} custom-call(s32[1]{0:T(128)} %bitcast.9.me_ref, bf16[128,256]{1,0:T(8,128)(2,1)} %get-tuple-element.89.refs_0_, bf16[128,256]{1,0:T(8,128)(2,1)} %copy-done.11, bf16[128,256]{1,0:T(8,128)(2,1)} %copy-done.17, bf16[128,256]{1,0:T(8,128)(2,1)} %copy-done.13, bf16[128,256]{1,0:T(8,128)(2,1)} %copy-done.14, ...), custom_call_target="tpu_custom_call" | custom-call | flops 1000000000 | bytes 4000000 | tf_op jit(solution)/shard_map/place_blocks/pallas_call | solution.py:26
  158.4 3.0 %all-to-all-done.6.pieces_ref = bf16[128,2,8,256]{3,2,1,0:T(8,128)(2,1)S(1)} async-done(((bf16[128,2,8,256]{3,2,1,0:T(8,128)(2,1)}), bf16[128,2,8,256]{3,2,1,0:T(8,128)(2,1)S(1)}, u32[]{:S(2)}, u32[]{:S(2)}) %all-to-all-start.6) | async-done | bytes 1048608 | tf_op jit(solution)/shard_map/all_to_all | solution.py:625
  161.5 1.4 unpack.1
  (49 shorter events, 4.3 us)
Async XLA Ops:
  0.6 9.8 %copy-start = (bf16[8,128,256]{2,1,0:T(8,128)(2,1)S(1)}, bf16[8,128,256]{2,1,0:T(8,128)(2,1)}, u32[]{:S(2)}) copy-start(bf16[8,128,256]{2,1,0:T(8,128)(2,1)} %param.27) | copy-start | bytes 1572868
  0.6 23.2 %copy-start.8 = (bf16[2,42,256]{2,0,1:T(2,128)(2,1)S(1)}, bf16[2,42,256]{2,0,1:T(2,128)(2,1)}, u32[]{:S(2)}) copy-start(bf16[2,42,256]{2,0,1:T(2,128)(2,1)} %param.19) | copy-start | bytes 129028
  2.1 14.9 %all-to-all-start = ((s32[8,5,128]{2,1,0:T(8,128)}), s32[8,5,128]{2,1,0:T(8,128)S(1)}, u32[]{:S(2)}, u32[]{:S(2)}) async-start(s32[8,5,128]{2,1,0:T(8,128)} %index_kernel.1), calls=%async_computation | async-start | bytes 65536 | tf_op jit(solution)/shard_map/all_to_all | solution.py:625
  17.0 7.5 %copy-start.9 = (s32[8,5,128]{2,1,0:T(8,128)}, s32[8,5,128]{2,1,0:T(8,128)S(1)}, u32[]{:S(2)}) copy-start(s32[8,5,128]{2,1,0:T(8,128)S(1)} %all-to-all-done.index_ref) | copy-start | bytes 61444
  17.0 27.6 %all-to-all-start.1 = ((bf16[16,8,8,256]{3,2,1,0:T(8,128)(2,1)}), bf16[16,8,8,256]{3,2,1,0:T(8,128)(2,1)S(1)}, u32[]{:S(2)}, u32[]{:S(2)}) async-start(bf16[16,8,8,256]{3,2,1,0:T(8,128)(2,1)} %copy_bitcast_fusion.1), calls=%async_computation.1 | async-start | bytes 1048576 | tf_op jit(solution)/shard_map/all_to_all | solution.py:625
  44.6 6.0 %copy-start.7 = (bf16[16,8,8,256]{3,2,1,0:T(8,128)(2,1)}, bf16[16,8,8,256]{3,2,1,0:T(8,128)(2,1)S(1)}, u32[]{:S(2)}) copy-start(bf16[16,8,8,256]{3,2,1,0:T(8,128)(2,1)S(1)} %all-to-all-done.1.grad_ref.grad_in) | copy-start | bytes 1572868
  44.6 19.7 %all-to-all-start.2 = ((bf16[128,8,256]{2,1,0:T(8,128)(2,1)}), bf16[128,8,256]{2,1,0:T(8,128)(2,1)S(1)}, u32[]{:S(2)}, u32[]{:S(2)}) async-start(bf16[128,8,256]{2,1,0:T(8,128)(2,1)} %get-tuple-element.57), calls=%async_computation.2 | async-start | bytes 1048576 | tf_op jit(solution)/shard_map/all_to_all | solution.py:625
  50.6 13.7 %copy-start.3 = (bf16[256,768]{1,0:T(8,128)(2,1)S(1)}, bf16[256,768]{1,0:T(8,128)(2,1)}, u32[]{:S(2)}) copy-start(bf16[256,768]{1,0:T(8,128)(2,1)} %w_qkv_ref.4) | copy-start | bytes 1179652
  50.7 13.7 %copy-start.5 = (f32[256]{0:T(256)S(1)}, f32[256]{0:T(256)}, u32[]{:S(2)}) copy-start(f32[256]{0:T(256)} %param.24) | copy-start | bytes 3076
  64.4 7.7 %copy-start.2 = (bf16[128,8,256]{2,1,0:T(8,128)(2,1)}, bf16[128,8,256]{2,1,0:T(8,128)(2,1)S(1)}, u32[]{:S(2)}) copy-start(bf16[128,8,256]{2,1,0:T(8,128)(2,1)S(1)} %all-to-all-done.2) | copy-start | bytes 1572868
  72.0 18.3 %all-to-all-start.3 = ((bf16[128,8,256]{2,1,0:T(8,128)(2,1)}), bf16[128,8,256]{2,1,0:T(8,128)(2,1)S(1)}, u32[]{:S(2)}, u32[]{:S(2)}) async-start(bf16[128,8,256]{2,1,0:T(8,128)(2,1)} %bitcast.6), calls=%async_computation.3 | async-start | bytes 1048576 | tf_op jit(solution)/shard_map/all_to_all | solution.py:625
  76.6 18.0 %copy-start.4 = (bf16[256,256]{1,0:T(8,128)(2,1)S(1)}, bf16[256,256]{1,0:T(8,128)(2,1)}, u32[]{:S(2)}) copy-start(bf16[256,256]{1,0:T(8,128)(2,1)} %w_out_ref.7) | copy-start | bytes 393220
  76.6 18.0 %copy-start.6 = (f32[4,1,1024]{2,1,0:T(1,128)S(1)}, f32[4,1,1024]{2,1,0:T(1,128)}, u32[]{:S(2)}) copy-start(f32[4,1,1024]{2,1,0:T(1,128)} %get-tuple-element.67.total_ref) | copy-start | bytes 49156
  90.3 17.5 %copy-start.1 = (bf16[128,8,256]{2,1,0:T(8,128)(2,1)}, bf16[128,8,256]{2,1,0:T(8,128)(2,1)S(1)}, u32[]{:S(2)}) copy-start(bf16[128,8,256]{2,1,0:T(8,128)(2,1)S(1)} %all-to-all-done.3.grad_ref) | copy-start | bytes 1572868
  90.3 17.5 %all-to-all-start.4 = ((bf16[16,8,8,256]{3,2,1,0:T(8,128)(2,1)}), bf16[16,8,8,256]{3,2,1,0:T(8,128)(2,1)S(1)}, u32[]{:S(2)}, u32[]{:S(2)}) async-start(bf16[16,8,8,256]{3,2,1,0:T(8,128)(2,1)} %get-tuple-element.75), calls=%async_computation.4 | async-start | bytes 1048576 | tf_op jit(solution)/shard_map/all_to_all | solution.py:625
  107.8 29.2 %all-to-all-start.5 = ((bf16[128,2,8,256]{3,2,1,0:T(8,128)(2,1)}), bf16[128,2,8,256]{3,2,1,0:T(8,128)(2,1)S(1)}, u32[]{:S(2)}, u32[]{:S(2)}) async-start(bf16[128,2,8,256]{3,2,1,0:T(8,128)(2,1)} %get-tuple-element.77), calls=%async_computation.5 | async-start | bytes 2097152 | tf_op jit(solution)/shard_map/all_to_all | solution.py:625
  117.1 15.6 %collective-permute-start = (bf16[128,256]{1,0:T(8,128)(2,1)}, bf16[128,256]{1,0:T(8,128)(2,1)S(1)}, u32[]{:S(2)}, u32[]{:S(2)}) collective-permute-start(bf16[128,256]{1,0:T(8,128)(2,1)} %get-tuple-element.82), channel_id=1, source_target_pairs={{0,1},{1,0},{2,3},{3,2},{4,5},{5,4},{6,7},{7,6},{8,9},{9,8},{10,11... | collective-permute-start | bytes 196616 | tf_op jit(solution)/shard_map/ppermute | solution.py:629
  120.4 12.3 %collective-permute-start.1 = (bf16[128,256]{1,0:T(8,128)(2,1)}, bf16[128,256]{1,0:T(8,128)(2,1)S(1)}, u32[]{:S(2)}, u32[]{:S(2)}) collective-permute-start(bf16[128,256]{1,0:T(8,128)(2,1)} %get-tuple-element.84), channel_id=1, source_target_pairs={{0,3},{1,2},{2,1},{3,0},{4,7},{5,6},{6,5},{7,4},{8,11},{9,10},{10,... | collective-permute-start | bytes 196616 | tf_op jit(solution)/shard_map/ppermute | solution.py:629
  121.4 11.3 %collective-permute-start.2 = (bf16[128,256]{1,0:T(8,128)(2,1)}, bf16[128,256]{1,0:T(8,128)(2,1)S(1)}, u32[]{:S(2)}, u32[]{:S(2)}) collective-permute-start(bf16[128,256]{1,0:T(8,128)(2,1)} %get-tuple-element.85), channel_id=1, source_target_pairs={{0,4},{1,5},{2,6},{3,7},{4,0},{5,1},{6,2},{7,3},{8,12},{9,13},{10,... | collective-permute-start | bytes 196616 | tf_op jit(solution)/shard_map/ppermute | solution.py:629
  123.9 11.5 %collective-permute-start.3 = (bf16[128,256]{1,0:T(8,128)(2,1)}, bf16[128,256]{1,0:T(8,128)(2,1)S(1)}, u32[]{:S(2)}, u32[]{:S(2)}) collective-permute-start(bf16[128,256]{1,0:T(8,128)(2,1)} %get-tuple-element.86), channel_id=1, source_target_pairs={{0,5},{1,4},{2,7},{3,6},{4,1},{5,0},{6,3},{7,2},{8,13},{9,12},{10,... | collective-permute-start | bytes 196616 | tf_op jit(solution)/shard_map/ppermute | solution.py:629
  127.0 10.0 %collective-permute-start.4 = (bf16[128,256]{1,0:T(8,128)(2,1)}, bf16[128,256]{1,0:T(8,128)(2,1)S(1)}, u32[]{:S(2)}, u32[]{:S(2)}) collective-permute-start(bf16[128,256]{1,0:T(8,128)(2,1)} %get-tuple-element.88), channel_id=1, source_target_pairs={{0,7},{1,6},{2,5},{3,4},{4,3},{5,2},{6,1},{7,0},{8,15},{9,14},{10,... | collective-permute-start | bytes 196616 | tf_op jit(solution)/shard_map/ppermute | solution.py:629
  132.7 5.6 %copy-start.11 = (bf16[128,256]{1,0:T(8,128)(2,1)}, bf16[128,256]{1,0:T(8,128)(2,1)S(1)}, u32[]{:S(2)}) copy-start(bf16[128,256]{1,0:T(8,128)(2,1)S(1)} %collective-permute-done.refs_1_) | copy-start | bytes 196612
  132.7 5.6 %copy-start.13 = (bf16[128,256]{1,0:T(8,128)(2,1)}, bf16[128,256]{1,0:T(8,128)(2,1)S(1)}, u32[]{:S(2)}) copy-start(bf16[128,256]{1,0:T(8,128)(2,1)S(1)} %collective-permute-done.1.refs_3_) | copy-start | bytes 196612
  132.7 5.6 %copy-start.14 = (bf16[128,256]{1,0:T(8,128)(2,1)}, bf16[128,256]{1,0:T(8,128)(2,1)S(1)}, u32[]{:S(2)}) copy-start(bf16[128,256]{1,0:T(8,128)(2,1)S(1)} %collective-permute-done.2.refs_4_) | copy-start | bytes 196612
  135.4 2.9 %copy-start.15 = (bf16[128,256]{1,0:T(8,128)(2,1)}, bf16[128,256]{1,0:T(8,128)(2,1)S(1)}, u32[]{:S(2)}) copy-start(bf16[128,256]{1,0:T(8,128)(2,1)S(1)} %collective-permute-done.3.refs_5_) | copy-start | bytes 196612
  137.0 1.3 copy-start.16
  137.2 6.4 %copy-start.12 = (bf16[128,256]{1,0:T(8,128)(2,1)S(1)}, bf16[128,256]{1,0:T(8,128)(2,1)}, u32[]{:S(2)}) copy-start(bf16[128,256]{1,0:T(8,128)(2,1)} %get-tuple-element.91) | copy-start | bytes 196612
  137.2 7.9 %copy-start.10 = (bf16[128,256]{1,0:T(8,128)(2,1)S(1)}, bf16[128,256]{1,0:T(8,128)(2,1)}, u32[]{:S(2)}) copy-start(bf16[128,256]{1,0:T(8,128)(2,1)} %get-tuple-element.95) | copy-start | bytes 196612
  138.3 23.2 %all-to-all-start.6 = ((bf16[128,2,8,256]{3,2,1,0:T(8,128)(2,1)}), bf16[128,2,8,256]{3,2,1,0:T(8,128)(2,1)S(1)}, u32[]{:S(2)}, u32[]{:S(2)}) async-start(bf16[128,2,8,256]{3,2,1,0:T(8,128)(2,1)} %broadcast_in_dim.2), calls=%async_computation.6 | async-start | bytes 2097152 | tf_op jit(solution)/shard_map/all_to_all | solution.py:625
  143.7 10.5 %collective-permute-start.5 = (bf16[128,256]{1,0:T(8,128)(2,1)S(1)}, bf16[128,256]{1,0:T(8,128)(2,1)S(1)}, u32[]{:S(2)}, u32[]{:S(2)}) collective-permute-start(bf16[128,256]{1,0:T(8,128)(2,1)S(1)} %copy-done.12), channel_id=1, source_target_pairs={{0,2},{1,3},{2,0},{3,1},{4,6},{5,7},{6,4},{7,5},{8,10},{9,11},{10,... | collective-permute-start | bytes 196616 | tf_op jit(solution)/shard_map/ppermute | solution.py:629
  145.1 10.8 %collective-permute-start.6 = (bf16[128,256]{1,0:T(8,128)(2,1)S(1)}, bf16[128,256]{1,0:T(8,128)(2,1)S(1)}, u32[]{:S(2)}, u32[]{:S(2)}) collective-permute-start(bf16[128,256]{1,0:T(8,128)(2,1)S(1)} %copy-done.10), channel_id=1, source_target_pairs={{0,6},{1,7},{2,4},{3,5},{4,2},{5,3},{6,0},{7,1},{8,14},{9,15},{10,... | collective-permute-start | bytes 196616 | tf_op jit(solution)/shard_map/ppermute | solution.py:629
  154.1 1.8 %copy-start.17 = (bf16[128,256]{1,0:T(8,128)(2,1)}, bf16[128,256]{1,0:T(8,128)(2,1)S(1)}, u32[]{:S(2)}) copy-start(bf16[128,256]{1,0:T(8,128)(2,1)S(1)} %collective-permute-done.5.refs_2_) | copy-start | bytes 196612
  (1 other events, 0.6 us)
